TPU v7x, 32 devices: a whole 2x2x4 slice. The times are simulated.
32 devices in a mesh: vocab: 8 (over z, x), seq: 4 (over y, core).
Axes of the slice: x: 2, y: 2, z: 4, core: 2. Of those that a mesh axis runs over, the one named last changes fastest.
Arguments:
- token_ids: int32 [3072, 4], P(None, 'seq'), may hold values from 0 to 12607
- lengths: int32 [8, 3], replicated, may hold values from 1 to 1344, 1536 in all within a row
- loss_place: int32 [512, 4], P(None, 'seq'), may hold values from 0 to 383
- targets: int32 [512, 4], P(None, 'seq'), may hold values from 0 to 12607
- loss_flag: int32 [512, 4], P(None, 'seq'), may hold values from 0 to 1, as said below
- layer_weight: float32 [15360, 1280], P(('vocab', 'seq')), may hold values from -8 to 8
- layer_first: float32 [15360, 1280], P(('vocab', 'seq')), may hold values from -0.00024414062 to 0.00024414062
- layer_second: float32 [15360, 1280], P(('vocab', 'seq')), may hold values from 8.37592e-10 to 1.1167893e-08
- rot_basis: float32 [32, 10, 128, 128], P(('vocab', 'seq')), may hold values from -1 to 1, as said below
- stat_matrix: float32 [32, 10, 128, 128], P(('vocab', 'seq')), may hold values from -1 to 1, as said below
- small_params: float32 [17920], replicated, may hold values from -2 to 2
- small_first: float32 [17920], replicated, may hold values from -0.0007324219 to 0.0007324219
- small_second: float32 [17920], replicated, may hold values from 8.37592e-09 to 1.11678936e-07
- embed_table: float32 [12608, 1280], P('vocab', 'seq'), may hold values from -2 to 2
- table_first: float32 [12608, 1280], P('vocab', 'seq'), may hold values from -0.00024414062 to 0.00024414062
- table_second: float32 [12608, 1280], P('vocab', 'seq'), may hold values from 8.37592e-10 to 1.1167893e-08
Outputs:
- loss_sum: float32 [], replicated
- loss_count: float32 [], replicated
- gradient_norm: float32 [], replicated
- layer_next: float32 [15360, 1280], P(('vocab', 'seq'))
- layer_first_next: float32 [15360, 1280], P(('vocab', 'seq'))
- layer_second_next: float32 [15360, 1280], P(('vocab', 'seq'))
- basis_next: float32 [32, 10, 128, 128], P(('vocab', 'seq'))
- stat_next: float32 [32, 10, 128, 128], P(('vocab', 'seq'))
- small_next: float32 [17920], replicated
- small_first_next: float32 [17920], replicated
- small_second_next: float32 [17920], replicated
- table_next: float32 [12608, 1280], P('vocab', 'seq')
- table_first_next: float32 [12608, 1280], P('vocab', 'seq')
- table_second_next: float32 [12608, 1280], P('vocab', 'seq')
- out_bias_grad: float32 [1280], replicated
Inputs may be any that keep to these rules, and one draw needn't show every extreme that they name: Each group's lengths sum to 1536; its longest sequence has exactly 1344 positions. `loss_flag`: every loss position of group 8 - 1 counts. `rot_basis`: each block is orthogonal. `stat_matrix`: each block is symmetric with a positive diagonal larger than the sum of magnitudes of the rest of its row.
All inputs are finite; a program needn't handle non-finite values.
Results may differ from a plain program's by a relative error of at most 0.018.
Values may be sent and summed in bfloat16 or wider, within the bound.
No kernel may reach another device: no remote copies, remote signals or barrier semaphores. Data moves between devices by JAX's collectives and lax.ppermute only.
A program may use at most 384 MiB of HBM per device.

v0:
```python
from functools import partial

import jax
import jax.numpy as jnp
from jax import lax
from jax.sharding import PartitionSpec as P

HEAD_SIZE = 64
VOCAB_REAL = 50257
STEP = 5


NORM_EPS = 1e-05
BETA_ONE = 0.9
BETA_TWO = 0.95
BETA_STAT = 0.95
ADAM_EPS = 1e-08
WEIGHT_DECAY = 0.1
RATE_LAYER = 0.025
RATE_SMALL = 0.08
RATE_TABLE = 0.04
MASKED = -1e30
HIGHEST = lax.Precision.HIGHEST


def layer_norm(inputs, gain, shift):
    centre = inputs - jnp.mean(inputs, -1, keepdims=True)
    spread = jnp.mean(centre * centre, -1, keepdims=True)
    return centre * lax.rsqrt(spread + NORM_EPS) * (1.0 + gain) + shift


def smooth(inputs):
    return jax.nn.gelu(inputs, approximate=True)


def low_dot(left, right):
    return lax.dot_general(
        left, right, (((1,), (1,)), ((), ())), preferred_element_type=jnp.float32
    )


def plain_dot(left, right):
    return jnp.dot(left, right, preferred_element_type=jnp.float32)


def outer_dot(left, right):
    return lax.dot_general(
        left, right, (((0,), (0,)), ((), ())), preferred_element_type=jnp.float32
    )


def column_sum(values):
    return jnp.sum(values.astype(jnp.float32), 0)


def pieces(small_params, model_dim, hidden_units):
    bounds = [0, model_dim, 2 * model_dim, 3 * model_dim, 3 * model_dim + hidden_units]
    for place_id in range(7):
        bounds.append(bounds[-1] + model_dim)
    return [small_params[bounds[place_id] : bounds[place_id + 1]] for place_id in range(11)]


def fetch_weights(layer_weight):
    return lax.all_gather(layer_weight.astype(jnp.bfloat16), ("vocab", "seq"), axis=0, tiled=True)


def split_weights(gathered, model_dim, hidden_units):
    return (
        gathered[: 3 * model_dim],
        gathered[3 * model_dim : 4 * model_dim],
        gathered[4 * model_dim : 4 * model_dim + hidden_units],
        gathered[4 * model_dim + hidden_units :],
    )


def to_heads(tensor):
    return lax.all_to_all(tensor, "seq", split_axis=2, concat_axis=0, tiled=True)


def to_tokens(tensor):
    return lax.all_to_all(tensor, "seq", split_axis=0, concat_axis=3, tiled=True)


def block_scores(queries, key_rows, segments, block_id, block_len):
    length = key_rows.shape[0]
    offset = block_id * block_len
    query_blk = lax.dynamic_slice_in_dim(queries, offset, block_len, 0)
    query_pos = offset + jnp.arange(block_len, dtype=jnp.int32)
    query_seg = lax.dynamic_slice_in_dim(segments, offset, block_len, 0)
    key_pos = jnp.arange(length, dtype=jnp.int32)
    scores = jnp.einsum(
        "qhe,khe->hqk", query_blk, key_rows, preferred_element_type=jnp.float32
    ) * HEAD_SIZE ** (-0.5)
    allowed = (query_seg[:, None] == segments[None, :]) & (key_pos[None, :] <= query_pos[:, None])
    return (query_blk, jnp.where(allowed[None], scores, MASKED))


def attend(queries, key_rows, values, segments):
    length = queries.shape[0]
    block_len = min(512, length)

    def one_block(block_id):
        unused, scores = block_scores(queries, key_rows, segments, block_id, block_len)
        peak_val = jnp.max(scores, -1, keepdims=True)
        raised = jnp.exp(scores - peak_val)
        summed = jnp.sum(raised, -1, keepdims=True)
        chance = (raised / summed).astype(jnp.bfloat16)
        mixture = jnp.einsum("hqk,khe->qhe", chance, values, preferred_element_type=jnp.float32)
        return (mixture.astype(jnp.bfloat16), peak_val[..., 0] + jnp.log(summed[..., 0]))

    mixture, logsum = lax.map(one_block, jnp.arange(length // block_len, dtype=jnp.int32))
    return (mixture.reshape(values.shape), logsum)


def attend_back(queries, key_rows, values, segments, logsum, grad_out):
    length = queries.shape[0]
    block_len = min(512, length)
    temper = HEAD_SIZE ** (-0.5)

    def one_block(running, block_id):
        grad_keys, grad_values = running
        query_blk, scores = block_scores(queries, key_rows, segments, block_id, block_len)
        chance = jnp.exp(scores - logsum[block_id][..., None])
        grad_blk = lax.dynamic_slice_in_dim(grad_out, block_id * block_len, block_len, 0)
        grad_chance = jnp.einsum(
            "qhe,khe->hqk", grad_blk, values, preferred_element_type=jnp.float32
        )
        grad_scores = chance * (grad_chance - jnp.sum(chance * grad_chance, -1, keepdims=True))
        low_scores = grad_scores.astype(jnp.bfloat16)
        grad_query = (
            jnp.einsum("hqk,khe->qhe", low_scores, key_rows, preferred_element_type=jnp.float32)
            * temper
        )
        grad_keys = (
            grad_keys
            + jnp.einsum("hqk,qhe->khe", low_scores, query_blk, preferred_element_type=jnp.float32)
            * temper
        )
        grad_values = grad_values + jnp.einsum(
            "hqk,qhe->khe",
            chance.astype(jnp.bfloat16),
            grad_blk,
            preferred_element_type=jnp.float32,
        )
        return ((grad_keys, grad_values), grad_query)

    zeros = jnp.zeros(key_rows.shape, jnp.float32)
    (grad_keys, grad_values), grad_query = lax.scan(
        one_block, (zeros, zeros), jnp.arange(length // block_len, dtype=jnp.int32)
    )
    return (grad_query.reshape(key_rows.shape), grad_keys, grad_values)


def adam_update(weight, first_mom, second, gradient, step_rate):
    first_mom = BETA_ONE * first_mom + (1.0 - BETA_ONE) * gradient
    second = BETA_TWO * second + (1.0 - BETA_TWO) * gradient * gradient
    direction = (
        first_mom / (1.0 - BETA_ONE**STEP) / (jnp.sqrt(second / (1.0 - BETA_TWO**STEP)) + ADAM_EPS)
    )
    return (weight - step_rate * (direction + WEIGHT_DECAY * weight), first_mom, second)


def rotated_update(weight, first_mom, second, gradient, stat, basis):
    owners = basis.shape[0]
    blocks = basis.shape[1]
    block_len = basis.shape[2]
    shaped = gradient.reshape(owners, -1, blocks, block_len)
    turned = jnp.einsum("arbi,abij->arbj", shaped, basis, precision=HIGHEST).reshape(gradient.shape)
    first_mom = BETA_ONE * first_mom + (1.0 - BETA_ONE) * turned
    second = BETA_TWO * second + (1.0 - BETA_TWO) * turned * turned
    direction = (
        first_mom / (1.0 - BETA_ONE**STEP) / (jnp.sqrt(second / (1.0 - BETA_TWO**STEP)) + ADAM_EPS)
    )
    back = jnp.einsum(
        "arbj,abij->arbi", direction.reshape(shaped.shape), basis, precision=HIGHEST
    ).reshape(weight.shape)
    weight_next = weight - RATE_LAYER * (back + WEIGHT_DECAY * weight)
    stat_next = BETA_STAT * stat + (1.0 - BETA_STAT) * jnp.einsum(
        "arbi,arbj->abij", shaped, shaped, precision=HIGHEST
    )
    spanned = jnp.einsum("abij,abjk->abik", stat_next, basis, precision=HIGHEST)
    gram_mat = jnp.einsum("abij,abik->abjk", spanned, spanned, precision=HIGHEST)
    lower_tri = jnp.linalg.cholesky(gram_mat).reshape(-1, block_len, block_len)
    solved = jax.vmap(partial(jax.scipy.linalg.solve_triangular, lower=True))(
        lower_tri, jnp.swapaxes(spanned, -1, -2).reshape(-1, block_len, block_len)
    )
    basis_next = jnp.swapaxes(solved, -1, -2).reshape(basis.shape)
    return (weight_next, first_mom, second, basis_next, stat_next)


def body(
    token_ids,
    lengths,
    loss_place,
    targets,
    loss_flag,
    layer_weight,
    layer_first,
    layer_second,
    rot_basis,
    stat_matrix,
    small_params,
    small_first,
    small_second,
    embed_table,
    table_first,
    table_second,
):
    group_id = lax.axis_index("vocab")
    groups = lax.axis_size("vocab")
    part_count = lax.axis_size("seq")
    tok_rows = token_ids.shape[0] // groups
    loss_rows = loss_place.shape[0] // groups
    vocab_rows = embed_table.shape[0]
    vocab_live = min(groups * vocab_rows, VOCAB_REAL)
    model_dim = layer_weight.shape[1]
    hidden_units = small_params.shape[0] - 10 * model_dim
    head_width = model_dim // part_count
    length = part_count * tok_rows
    (
        bias_q,
        bias_v,
        bias_out,
        bias_up,
        bias_down,
        gain_one,
        shift_one,
        gain_two,
        shift_two,
        gain_final,
        shift_final,
    ) = pieces(small_params, model_dim, hidden_units)
    project_in, project_out, expand_weight, reduce_weight = split_weights(
        fetch_weights(layer_weight), model_dim, hidden_units
    )
    table_full = lax.all_gather(embed_table.astype(jnp.bfloat16), "seq", axis=1, tiled=True)
    local_ids = token_ids[:, 0] - group_id * vocab_rows
    inside = (local_ids >= 0) & (local_ids < vocab_rows)
    safe_ids = jnp.clip(local_ids, 0, vocab_rows - 1)
    picked = jnp.where(
        inside[:, None], jnp.take(table_full, safe_ids, axis=0).astype(jnp.float32), 0.0
    )
    embedded = lax.psum_scatter(
        picked.astype(jnp.bfloat16), "vocab", scatter_dimension=0, tiled=True
    ).astype(jnp.float32)
    group_lengths = jnp.take(lengths, group_id, axis=0)
    bounds = jnp.cumsum(group_lengths)[:-1]
    positions = jnp.arange(length, dtype=jnp.int32)
    segments = jnp.sum((positions[:, None] >= bounds[None, :]).astype(jnp.int32), 1)
    normed_low = layer_norm(embedded, gain_one, shift_one).astype(jnp.bfloat16)
    joined = low_dot(normed_low, project_in) + jnp.concatenate(
        [bias_q, jnp.zeros_like(bias_q), bias_v]
    )
    joined_heads = to_heads(
        joined.astype(jnp.bfloat16).reshape(tok_rows, 3, part_count, head_width)
    )
    queries = joined_heads[:, 0, 0].reshape(length, -1, HEAD_SIZE)
    key_rows = joined_heads[:, 1, 0].reshape(length, -1, HEAD_SIZE)
    values = joined_heads[:, 2, 0].reshape(length, -1, HEAD_SIZE)
    mixture, logsum = attend(queries, key_rows, values, segments)
    mixed_low = to_tokens(mixture.reshape(part_count, tok_rows, 1, 1, head_width)).reshape(
        tok_rows, model_dim
    )
    middle = embedded + low_dot(mixed_low, project_out) + bias_out
    normed_two_low = layer_norm(middle, gain_two, shift_two).astype(jnp.bfloat16)
    hidden = low_dot(normed_two_low, expand_weight) + bias_up
    active_low = smooth(hidden).astype(jnp.bfloat16)
    residual_out = middle + plain_dot(active_low, reduce_weight) + bias_down
    final_out = layer_norm(residual_out, gain_final, shift_final)
    own_pos = lax.dynamic_slice_in_dim(loss_place[:, 0], group_id * loss_rows, loss_rows, 0)
    chosen = jnp.take(final_out, own_pos, axis=0).astype(jnp.bfloat16)
    head_rows = lax.all_gather(chosen, "vocab", axis=0, tiled=True)
    row_ids = group_id * vocab_rows + jnp.arange(vocab_rows, dtype=jnp.int32)
    logits = jnp.where((row_ids < vocab_live)[None, :], low_dot(head_rows, table_full), MASKED)
    target_local = targets[:, 0] - group_id * vocab_rows
    hit = (target_local >= 0) & (target_local < vocab_rows)
    target_hot = (jnp.arange(vocab_rows, dtype=jnp.int32)[None, :] == target_local[:, None]) & hit[
        :, None
    ]
    target_part = jnp.sum(jnp.where(target_hot, logits, 0.0), 1)
    local_peak = jnp.max(logits, 1)
    peak_all = lax.pmax(local_peak, "vocab")
    sum_all, target_logit = lax.psum(
        (jnp.sum(jnp.exp(logits - peak_all[:, None]), 1), target_part), "vocab"
    )
    logsum_all = peak_all + jnp.log(sum_all)
    weight_rows = loss_flag[:, 0].astype(jnp.float32)
    chance = jnp.exp(logits - logsum_all[:, None])
    grad_logits = weight_rows[:, None] * (chance - target_hot.astype(jnp.float32))
    grad_low = grad_logits.astype(jnp.bfloat16)
    grad_table = outer_dot(grad_low, head_rows)
    grad_chosen = lax.psum_scatter(
        plain_dot(grad_low, table_full), "vocab", scatter_dimension=0, tiled=True
    )
    grad_final = jnp.zeros((tok_rows, model_dim), jnp.float32).at[own_pos].add(grad_chosen)
    is_first = group_id == 0
    loss_part = jnp.where(is_first, jnp.sum(weight_rows * (logsum_all - target_logit)), 0.0)
    count_part = jnp.where(is_first, jnp.sum(weight_rows), 0.0)
    unused, final_back = jax.vjp(layer_norm, residual_out, gain_final, shift_final)
    grad_resid, grad_gain_final, grad_shift_final = final_back(grad_final)
    resid_low = grad_resid.astype(jnp.bfloat16)
    grad_bias_down = column_sum(resid_low)
    grad_reduce = outer_dot(active_low, resid_low)
    grad_active = low_dot(resid_low, reduce_weight)
    unused, gelu_back = jax.vjp(smooth, hidden)
    hidden_low = gelu_back(grad_active)[0].astype(jnp.bfloat16)
    grad_bias_up = column_sum(hidden_low)
    grad_expand = outer_dot(hidden_low, normed_two_low)
    unused, two_back = jax.vjp(layer_norm, middle, gain_two, shift_two)
    grad_middle_part, grad_gain_two, grad_shift_two = two_back(plain_dot(hidden_low, expand_weight))
    grad_middle = grad_resid + grad_middle_part
    middle_low = grad_middle.astype(jnp.bfloat16)
    grad_bias_out = column_sum(middle_low)
    grad_project_out = outer_dot(middle_low, mixed_low)
    grad_mixed = plain_dot(middle_low, project_out)
    grad_heads = to_heads(
        grad_mixed.astype(jnp.bfloat16).reshape(tok_rows, 1, part_count, head_width)
    )
    grad_query, grad_keys, grad_values = attend_back(
        queries, key_rows, values, segments, logsum, grad_heads[:, 0, 0].reshape(values.shape)
    )
    stacked = (
        jnp.stack([grad_query, grad_keys, grad_values], 1)
        .astype(jnp.bfloat16)
        .reshape(part_count, tok_rows, 3, 1, head_width)
    )
    grad_joined = to_tokens(stacked).reshape(tok_rows, 3 * model_dim)
    grad_bias_q = column_sum(grad_joined[:, :model_dim])
    grad_bias_v = column_sum(grad_joined[:, 2 * model_dim :])
    grad_project_in = outer_dot(grad_joined, normed_low)
    unused, one_back = jax.vjp(layer_norm, embedded, gain_one, shift_one)
    grad_embed_part, grad_gain_one, grad_shift_one = one_back(plain_dot(grad_joined, project_in))
    grad_embedded = grad_middle + grad_embed_part
    rows_back = lax.all_gather(grad_embedded.astype(jnp.bfloat16), "vocab", axis=0, tiled=True)
    grad_table = grad_table + jnp.zeros((vocab_rows, model_dim), jnp.float32).at[safe_ids].add(
        jnp.where(inside[:, None], rows_back.astype(jnp.float32), 0.0)
    )
    table_shard_grad = lax.psum_scatter(
        grad_table.astype(jnp.bfloat16), "seq", scatter_dimension=1, tiled=True
    ).astype(jnp.float32)
    layer_grad = jnp.concatenate([grad_project_in, grad_project_out, grad_expand, grad_reduce], 0)
    layer_shard_grad = lax.psum_scatter(
        layer_grad, ("vocab", "seq"), scatter_dimension=0, tiled=True
    )
    small_part = jnp.concatenate(
        [
            grad_bias_q,
            grad_bias_v,
            grad_bias_out,
            grad_bias_up,
            grad_bias_down,
            grad_gain_one,
            grad_shift_one,
            grad_gain_two,
            grad_shift_two,
            grad_gain_final,
            grad_shift_final,
        ]
    )
    small_grad, layer_squares, table_squares, loss_sum, loss_count = lax.psum(
        (
            small_part,
            jnp.sum(layer_shard_grad * layer_shard_grad),
            jnp.sum(table_shard_grad * table_shard_grad),
            loss_part,
            count_part,
        ),
        ("vocab", "seq"),
    )
    gradient_norm = jnp.sqrt(layer_squares + table_squares + jnp.sum(small_grad * small_grad))
    factor = 1.0 / jnp.maximum(gradient_norm, 1.0)
    out_bias_grad = factor * small_grad[2 * model_dim : 3 * model_dim]
    layer_next, layer_first_next, layer_second_next, basis_next, stat_next = rotated_update(
        layer_weight, layer_first, layer_second, factor * layer_shard_grad, stat_matrix, rot_basis
    )
    small_next, small_first_next, small_second_next = adam_update(
        small_params, small_first, small_second, factor * small_grad, RATE_SMALL
    )
    table_next, table_first_next, table_second_next = adam_update(
        embed_table, table_first, table_second, factor * table_shard_grad, RATE_TABLE
    )
    return (
        loss_sum,
        loss_count,
        gradient_norm,
        layer_next,
        layer_first_next,
        layer_second_next,
        basis_next,
        stat_next,
        small_next,
        small_first_next,
        small_second_next,
        table_next,
        table_first_next,
        table_second_next,
        out_bias_grad,
    )


def solution(mesh):
    in_specs = (
        P(None, "seq"),
        P(),
        P(None, "seq"),
        P(None, "seq"),
        P(None, "seq"),
        P(("vocab", "seq"), None),
        P(("vocab", "seq"), None),
        P(("vocab", "seq"), None),
        P(("vocab", "seq"), None, None, None),
        P(("vocab", "seq"), None, None, None),
        P(),
        P(),
        P(),
        P("vocab", "seq"),
        P("vocab", "seq"),
        P("vocab", "seq"),
    )
    out_specs = (
        P(),
        P(),
        P(),
        P(("vocab", "seq"), None),
        P(("vocab", "seq"), None),
        P(("vocab", "seq"), None),
        P(("vocab", "seq"), None, None, None),
        P(("vocab", "seq"), None, None, None),
        P(),
        P(),
        P(),
        P("vocab", "seq"),
        P("vocab", "seq"),
        P("vocab", "seq"),
        P(),
    )
    return jax.shard_map(body, mesh=mesh, in_specs=in_specs, out_specs=out_specs, check_vma=False)
```

profile of v0, /device:TPU:0, one launch (start us, length us, event | category | flops | bytes accessed | tf_op | source)
XLA Modules:
  0.0 2295.9 jit_solution(11650155763334693741)
XLA Ops:
  11.6 37.0 %all-gather.5.cloned.1.call-done = bf16[1576,1280]{0,1:T(8,128)(2,1)} async-done(((bf16[1576,320]{0,1:T(8,128)(2,1)}), bf16[1576,1280]{0,1:T(8,128)(2,1)}) %all-gather.5.cloned.1.call-update) | async-done | bytes 4034576 | tf_op jit(solution)/shard_map/all_gather | solution.py:236
  55.6 20.2 gather_fusion
  87.3 296.3 %reduce-scatter.7.cloned.1.call-done = bf16[384,1280]{1,0:T(8,128)(2,1)} async-done(((bf16[3072,1280]{1,0:T(8,128)(2,1)}), bf16[384,1280]{1,0:T(8,128)(2,1)}) %reduce-scatter.7.cloned.1.call-update) | async-done | bytes 983056 | tf_op jit(solution)/shard_map/reduce_scatter | solution.py:243
  410.3 34.4 %all-to-all-done = bf16[384,3,4,320]{0,3,1,2:T(8,128)(2,1)} async-done(((bf16[384,3,4,320]{0,3,1,2:T(8,128)(2,1)}), bf16[384,3,4,320]{0,3,1,2:T(8,128)(2,1)}, u32[]{:S(2)}, u32[]{:S(2)}) %all-to-all-start) | async-done | bytes 2949152 | tf_op jit(solution)/shard_map/all_to_all | solution.py:77
  447.9 45.7 %while.28 = (s32[]{:T(128)}, bf16[3,512,5,64]{1,3,2,0:T(8,128)(2,1)}, f32[3,5,512]{2,1,0:T(8,128)S(1)}, s32[3]{0:T(128)S(1)}, s32[1536]{0:T(1024)S(1)}, /*index=...) while((s32[]{:T(128)}, ...), condition=%wide.region_8.9_spmd, body=%wide.region_5.8_spmd.sunk | while | flops 1056339968 | bytes 57002716 | solution.py:111
  536.2 13.7 fusion.145
  556.1 39.7 %all-gather.9.cloned.1.call-done = bf16[512,1280]{1,0:T(8,128)(2,1)} async-done(((bf16[64,1280]{1,0:T(8,128)(2,1)}), bf16[512,1280]{1,0:T(8,128)(2,1)}) %all-gather.9.cloned.1.call-update) | async-done | bytes 1310736 | tf_op jit(solution)/shard_map/all_gather | solution.py:272
  602.6 19.1 pmax.7
  624.7 17.2 all-reduce.1
  650.5 69.4 %reduce-scatter.9.cloned.1.call-done = f32[64,1280]{1,0:T(8,128)} async-done(((f32[512,1280]{1,0:T(8,128)}), f32[64,1280]{1,0:T(8,128)}) %reduce-scatter.9.cloned.1.call-update) | async-done | bytes 327696 | tf_op jit(solution)/shard_map/reduce_scatter | solution.py:292
  728.1 14.4 convert_reduce_fusion
  767.9 13.7 all-to-all-done.2
  787.2 178.6 %while.29 = (s32[]{:T(128)}, f32[1536,5,64]{0,2,1:T(8,128)}, f32[1536,5,64]{0,2,1:T(8,128)}, bf16[3,512,5,64]{1,3,2,0:T(8,128)(2,1)}, s32[3]{0:T(128)S(1)}, /*in...) while((s32[]{:T(128)}, f32[1536,5,64]{0,2,1:T(8,128)}, ...), condition=%wide.region_31.32_spmd.clone, body=%wide.region_29.31_spmd.clone.sunk | while | flops 2580543488 | bytes 220486096 | solution.py:148
  799.4 14.2 multiply_reduce_fusion.11
  858.1 14.2 multiply_reduce_fusion.11
  917.8 14.2 multiply_reduce_fusion.11
  985.3 37.3 %all_to_all.63 = bf16[4,384,3,1,320]{1,4,3,2,0:T(8,128)(2,1)S(1)} all-to-all(bf16[4,384,3,1,320]{1,4,3,2,0:T(8,128)(2,1)S(1)} %copy.162), channel_id=1, replica_groups=mesh['vocab'=8,'seq'=4] {'seq'}, dimensions={0} | all-to-all | bytes 5898240 | tf_op jit(solution)/shard_map/all_to_all | solution.py:81
  1068.9 82.5 %all-gather.11.cloned.1.call-done = bf16[3072,1280]{1,0:T(8,128)(2,1)} async-done(((bf16[384,1280]{1,0:T(8,128)(2,1)}), bf16[3072,1280]{1,0:T(8,128)(2,1)}) %all-gather.11.cloned.1.call-update) | async-done | bytes 7864336 | tf_op jit(solution)/shard_map/all_gather | solution.py:334
  1151.4 37.5 %scatter_custom_fusion.1 = f32[1576,1280]{1,0:T(8,128)} fusion(f32[1576,1280]{1,0:T(8,128)} %fusion.127, s32[3072]{0:T(1024)} %bitcast.208, bf16[3072,1280]{1,0:T(8,128)(2,1)} %all-gather.11.cloned.1.call-done, f32[]{:T(128)} %constant.221.clone.1, pred[3072]{0:T(1024)(128)(4,1)S(1)} %copy-done.58), kind=kCustom, calls=%fused_computation.53 | custom fusion | flops 11796480 | bytes 15937024 | tf_op jit(solution)/shard_map/scatter-add | solution.py:335
  1214.4 64.3 %pad_maximum_fusion = f32[15360,1280]{1,0:T(8,128)} fusion(f32[5120,1280]{1,0:T(8,128)} %fusion.134, f32[5120,1280]{1,0:T(8,128)} %fusion.133, f32[1280,1280]{1,0:T(8,128)} %fusion.124, f32[3840,1280]{1,0:T(8,128)S(1)} %fusion.129), kind=kLoop, calls=%fused_computation.52 | loop fusion | flops 58982400 | bytes 157286400 | tf_op jit(solution)/shard_map/concatenate | solution.py:341
  1306.2 651.0 %reduce-scatter.11.cloned.1.call-done = f32[480,1280]{1,0:T(8,128)} async-done(((f32[15360,1280]{1,0:T(8,128)}), f32[480,1280]{1,0:T(8,128)}) %reduce-scatter.11.cloned.1.call-update) | async-done | bytes 2457616 | tf_op jit(solution)/shard_map/reduce_scatter | solution.py:342
  1962.9 39.3 %all-reduce = (f32[]{:T(128)}, f32[]{:T(128)}, f32[]{:T(128)}) all-reduce(f32[]{:T(128)S(6)} %select_n.102, f32[]{:T(128)S(6)} %select_n.103, f32[]{:T(128)S(6)} %add.348), channel_id=1, replica_groups=mesh['vocab'=8,'seq'=4] {'vocab','seq'}, use_global_device_ids=true, to_apply=%region_20.21 | all-reduce | flops 3 | bytes 24 | tf_op jit(solution)/shard_map/psum | solution.py:360
  2035.3 117.5 %custom-call.8 = f32[1,10,128,128]{3,2,1,0:T(8,128)S(1)} custom-call(f32[1,10,128,128]{3,2,1,0:T(8,128)S(1)} %fusion.111), custom_call_target="Cholesky" | custom-call | tf_op jit(solution)/shard_map/jit(cholesky)/cholesky | solution.py:183
  2153.1 98.2 %custom-call.9 = f32[10,1,128,128]{2,3,1,0:T(8,128)S(1)} custom-call(f32[10,1,128,128]{3,2,1,0:T(8,128)S(1)} %select_bitcast_fusion), custom_call_target="InvertDiagBlocksLowerTriangular" | custom-call | tf_op jit(solution)/shard_map/vmap(jit(_solve_triangular))/triangular_solve | solution.py:184
  (432 shorter events, 518.0 us)
Async XLA Ops:
  8.0 2019.2 %copy-start = (f32[1,10,128,128]{3,2,1,0:T(8,128)S(1)}, f32[1,10,128,128]{3,2,1,0:T(8,128)}, u32[]{:S(2)}) copy-start(f32[1,10,128,128]{3,2,1,0:T(8,128)} %param.28) | copy-start | bytes 1966084
  8.0 40.6 %all-gather.5.cloned.1.call-start = ((), (), s32[]{:S(2)}) async-start(), calls=%async_computation.8 | async-start | bytes 5324800 | tf_op jit(solution)/shard_map/all_gather | solution.py:236
  10.8 372.7 %reduce-scatter.7.cloned.1.call-start = ((), (), s32[]{:S(2)}) async-start(), calls=%async_computation.9 | async-start | bytes 8847360 | tf_op jit(solution)/shard_map/reduce_scatter | solution.py:243
  11.0 64.7 %copy-start.57 = (pred[3072]{0:T(1024)(128)(4,1)}, pred[3072]{0:T(1024)(128)(4,1)S(1)}, u32[]{:S(2)}) copy-start(pred[3072]{0:T(1024)(128)(4,1)S(1)} %get-tuple-element.343) | copy-start | bytes 9220
  83.8 302.8 %all-gather.7.cloned.1.call-start = ((), (), s32[]{:S(2)}) async-start(), calls=%async_computation.10 | async-start | bytes 40550400 | tf_op jit(solution)/shard_map/all_gather | solution.py:64
  87.3 309.2 %copy-start.35 = (f32[1280]{0:T(1024)}, f32[1280]{0:T(1024)S(1)}, u32[]{:S(2)}) copy-start(f32[1280]{0:T(1024)S(1)} %get-tuple-element.341) | copy-start | bytes 15364
  87.3 309.2 %copy-start.55 = (f32[1280]{0:T(1024)}, f32[1280]{0:T(1024)S(1)}, u32[]{:S(2)}) copy-start(f32[1280]{0:T(1024)S(1)} %get-tuple-element.340) | copy-start | bytes 15364
  404.8 39.8 %all-to-all-start = ((bf16[384,3,4,320]{0,3,1,2:T(8,128)(2,1)}), bf16[384,3,4,320]{0,3,1,2:T(8,128)(2,1)}, u32[]{:S(2)}, u32[]{:S(2)}) async-start(bf16[384,3,4,320]{0,3,1,2:T(8,128)(2,1)} %copy.154), calls=%async_computation.1 | async-start | bytes 5898240 | tf_op jit(solution)/shard_map/all_to_all | solution.py:77
  496.7 24.2 %copy-start.66 = (f32[1280]{0:T(1024)S(1)}, f32[1280]{0:T(1024)}, u32[]{:S(2)}) copy-start(f32[1280]{0:T(1024)} %get-tuple-element.337) | copy-start | bytes 15364
  502.8 18.1 all-to-all-start.1
  507.1 88.8 %all-gather.9.cloned.1.call-start = ((), (), s32[]{:S(2)}) async-start(), calls=%async_computation.11 | async-start | bytes 1474560 | tf_op jit(solution)/shard_map/all_gather | solution.py:272
  525.0 229.1 %copy-start.53 = (f32[384]{0:T(512)}, f32[384]{0:T(512)S(1)}, u32[]{:S(2)}) copy-start(f32[384]{0:T(512)S(1)} %broadcast_multiply_fusion.2) | copy-start | bytes 4612
  525.4 228.8 %copy-start.60 = (f32[384]{0:T(512)}, f32[384]{0:T(512)S(1)}, u32[]{:S(2)}) copy-start(f32[384]{0:T(512)S(1)} %fusion.122) | copy-start | bytes 4612
  555.5 164.5 %reduce-scatter.9.cloned.1.call-start = ((), (), s32[]{:S(2)}) async-start(), calls=%async_computation.12 | async-start | bytes 2949120 | tf_op jit(solution)/shard_map/reduce_scatter | solution.py:292
  556.0 86.5 %copy-start.71 = (f32[512,1]{0,1:T(1,128)}, f32[512,1]{0,1:T(1,128)S(1)}, u32[]{:S(2)}) copy-start(f32[512,1]{0,1:T(1,128)S(1)} %convert_element_type.108) | copy-start | bytes 6148
  556.0 86.4 %copy-start.73 = (s32[512,1]{0,1:T(1,128)}, s32[512,1]{0,1:T(1,128)S(1)}, u32[]{:S(2)}) copy-start(s32[512,1]{0,1:T(1,128)S(1)} %get-tuple-element.321) | copy-start | bytes 6148
  556.1 86.4 %copy-start.79 = (pred[512]{0:T(512)(128)(4,1)}, pred[512]{0:T(512)(128)(4,1)S(1)}, u32[]{:S(2)}) copy-start(pred[512]{0:T(512)(128)(4,1)S(1)} %get-tuple-element.320) | copy-start | bytes 1540
  763.6 18.1 all-to-all-start.2
  767.8 383.6 %all-gather.11.cloned.1.call-start = ((), (), s32[]{:S(2)}) async-start(), calls=%async_computation.14 | async-start | bytes 8847360 | tf_op jit(solution)/shard_map/all_gather | solution.py:334
  1035.0 267.4 %reduce-scatter.13.cloned.1.call-start = ((), (), s32[]{:S(2)}) async-start(), calls=%async_computation.16 | async-start | bytes 5324800
  1035.1 21.2 slice-start.4
  1056.3 95.1 %copy-start.58 = (pred[3072]{0:T(1024)(128)(4,1)S(1)}, pred[3072]{0:T(1024)(128)(4,1)}, u32[]{:S(2)}) copy-start(pred[3072]{0:T(1024)(128)(4,1)} %copy-done.57) | copy-start | bytes 9220
  1201.3 755.8 %reduce-scatter.11.cloned.1.call-start = ((), (), s32[]{:S(2)}) async-start(), calls=%async_computation.13 | async-start | bytes 81100800 | tf_op jit(solution)/shard_map/reduce_scatter | solution.py:342
  1278.8 682.6 %all-reduce.4.cloned.1.call-start = ((), (), s32[]{:S(2)}) async-start(), calls=%async_computation.15 | async-start | bytes 147456 | tf_op jit(solution)/shard_map/psum | solution.py:360
  (92 other events, 646.3 us)
Sparse Core Ops, SparseCore 0:
  11.0 37.5 all-gather.4
  84.0 299.5 reduce-scatter.6
  555.6 40.1 all-gather.8
  650.7 69.2 reduce-scatter.8
  1035.1 116.3 all-gather.10
  1201.4 43.1 reduce-scatter.12
  1278.9 678.1 reduce-scatter.10
Sparse Core Ops, SparseCore 1:
  87.8 288.5 all-gather.6
  1302.4 144.6 all-reduce.3
where the time goes:
time: 2300 us
  waiting for transfers between devices  1240 us (54%)
  other arithmetic  445 us (19%)
  matrix products  310 us (13%)
  local copies, waits for them, and re-layouts  144 us (6%)
  blocking collectives  113 us (5%)
    reduce_scatter x1, waiting for transfers between devices, body(): lax.psum_scatter(layer_grad, ('vocab', 'seq'), scatter_dimension=0, tiled...  651 us
    reduce_scatter x1, waiting for transfers between devices, body(): lax.psum_scatter(picked.astype(jnp.bfloat16), 'vocab', scatter_dimension=...  296 us
    another operation x4, other arithmetic, rotated_update(): lower_tri = jnp.linalg.cholesky(gram_mat).reshape(-1, block_len, block_len)  118 us
    another operation x3, other arithmetic, rotated_update(): jax.vmap(partial(jax.scipy.linalg.solve_triangular, lower=True))  98.4 us
    all_gather x1, waiting for transfers between devices, body(): lax.all_gather(grad_embedded.astype(jnp.bfloat16), 'vocab', axis=0, tiled...  82.5 us
    reduce_scatter x1, waiting for transfers between devices, body(): lax.psum_scatter(plain_dot(grad_low, table_full), 'vocab', scatter_dimens...  69.4 us
    concatenate x1, other arithmetic, body(): jnp.concatenate([grad_project_in, grad_project_out, grad_expand, grad_red...  64.3 us
    unnamed x184, local copies, waits for them, and re-layouts  51.4 us
  transfers between devices with their start and end apart: 12, of which 9 were waited for; matrix products, arithmetic and copies ran while one was open for 6% of the time, Pallas kernels for 0%

commit v1 on v0

v1 whole, which is shorter than its diff:
```python
from functools import partial

import jax
import jax.numpy as jnp
from jax import lax
from jax.experimental import pallas as pl
from jax.experimental.pallas import tpu as pltpu
from jax.sharding import Mesh, PartitionSpec as P

HEAD_SIZE = 64
VOCAB_REAL = 50257
STEP = 5


NORM_EPS = 1e-05
BETA_ONE = 0.9
BETA_TWO = 0.95
BETA_STAT = 0.95
ADAM_EPS = 1e-08
WEIGHT_DECAY = 0.1
RATE_LAYER = 0.025
RATE_SMALL = 0.08
RATE_TABLE = 0.04
MASKED = -1e30
HIGHEST = lax.Precision.HIGHEST
LANES_BOTH = (((1,), (1,)), ((), ()))
VOCAB = ("z", "w", "x")
SEQ = ("y", "core")
ALL = VOCAB + SEQ
PLANES = 4


def layer_norm(inputs, gain, shift):
    centre = inputs - jnp.mean(inputs, -1, keepdims=True)
    spread = jnp.mean(centre * centre, -1, keepdims=True)
    return centre * lax.rsqrt(spread + NORM_EPS) * (1.0 + gain) + shift


def smooth(inputs):
    return jax.nn.gelu(inputs, approximate=True)


def low_dot(left, right):
    return lax.dot_general(left, right, LANES_BOTH, preferred_element_type=jnp.float32)


def plain_dot(left, right):
    return jnp.dot(left, right, preferred_element_type=jnp.float32)


def outer_dot(left, right, kind=jnp.float32):
    return lax.dot_general(left, right, (((0,), (0,)), ((), ())), preferred_element_type=kind)


def column_sum(values):
    return jnp.sum(values.astype(jnp.float32), 0)


def pieces(small_params, model_dim, hidden_units):
    bounds = [0, model_dim, 2 * model_dim, 3 * model_dim, 3 * model_dim + hidden_units]
    for place_id in range(7):
        bounds.append(bounds[-1] + model_dim)
    return [small_params[bounds[place_id] : bounds[place_id + 1]] for place_id in range(11)]


def swap(tensor, axis):
    return lax.ppermute(tensor, axis, [(0, 1), (1, 0)])


def shift(tensor, step):
    return lax.ppermute(tensor, "z", [(i, (i + step) % PLANES) for i in range(PLANES)])


def pick(tensor, place, axis=0):
    return lax.dynamic_index_in_dim(tensor, place, axis, keepdims=False)


def added(*tensors):
    total = tensors[0].astype(jnp.float32)
    for tensor in tensors[1:]:
        total = total + tensor.astype(jnp.float32)
    return total


def lowered(*tensors):
    return added(*tensors).astype(jnp.bfloat16)


def in_order(place, own, other, axis):
    return jnp.where(
        place == 0, jnp.concatenate([own, other], axis), jnp.concatenate([other, own], axis)
    )


def split_rows(rows):
    return rows * 2 // 3


def exchange_planes(stacked):
    here = lax.axis_index("z")
    got = [pick(stacked, here)]
    for step in (3, 2, 1):
        got.append(shift(pick(stacked, (here + step) % PLANES), step))
    doubled = jnp.concatenate([part[None] for part in got + got[:3]], 0)
    return lax.dynamic_slice_in_dim(doubled, (PLANES - here) % PLANES, PLANES, 0)


def gather_pieces(piece):
    here = lax.axis_index("z")
    got = [piece] + [shift(piece, step) for step in (3, 2, 1)]
    doubled = jnp.concatenate([part[None] for part in got + got[:3]], 0)
    return lax.dynamic_slice_in_dim(doubled, (PLANES - here) % PLANES, PLANES, 0)


def gather_weights(layer_weight):
    rows, model_dim = layer_weight.shape
    quarter = rows // PLANES
    low = layer_weight.astype(jnp.bfloat16).reshape(PLANES, quarter, model_dim)
    held = exchange_planes(low)
    ways = lax.axis_size("w")
    at_x, at_y, at_c = (lax.axis_index(name) for name in ("x", "y", "core"))
    cut = split_rows(rows)
    planes = []
    for place in range(PLANES):
        mine = gather_pieces(held[place]).reshape(1, rows, model_dim)
        if ways > 1:
            mine = lax.all_gather(mine, "w", axis=0, tiled=True)
        whole = jnp.zeros((ways, 8, rows, model_dim), jnp.bfloat16)
        for offset, length, first, second in ((0, cut, "x", "y"), (cut, rows - cut, "y", "x")):
            part = mine[:, None, offset : offset + length]
            near = jnp.concatenate([part, swap(part, first)], 1)
            far = swap(near, second)
            for other, pair in ((0, near), (1, far)):
                for turned, both in ((0, pair), (1, swap(pair, "core"))):
                    for spot in (0, 1):
                        by_x, by_y = (spot, other) if first == "x" else (other, spot)
                        owner = (at_x ^ by_x) * 4 + (at_y ^ by_y) * 2 + (at_c ^ turned)
                        whole = lax.dynamic_update_slice(
                            whole, both[:, spot : spot + 1], (0, owner, offset, 0)
                        )
        planes.append(whole.reshape(-1, model_dim))
    return planes


def scatter_plane(grads):
    model_dim = grads.shape[1]
    ways = lax.axis_size("w")
    at_x, at_y, at_c, here = (lax.axis_index(name) for name in ("x", "y", "core", "z"))
    shaped = grads.reshape(ways, 2, 2, 2, -1, model_dim)
    rows = shaped.shape[4]
    cut = split_rows(rows)
    shaped = lowered(pick(shaped, at_c, 3), swap(pick(shaped, 1 - at_c, 3), "core"))
    parts = []
    for offset, length, first, second in ((0, cut, "y", "x"), (cut, rows - cut, "x", "y")):
        part = shaped[:, :, :, offset : offset + length]
        spot = {"x": at_x, "y": at_y}
        axis = 2 if first == "y" else 1
        part = lowered(
            pick(part, spot[first], axis), swap(pick(part, 1 - spot[first], axis), first)
        )
        part = lowered(pick(part, spot[second], 1), swap(pick(part, 1 - spot[second], 1), second))
        parts.append(part)
    own = jnp.concatenate(parts, 1)
    if ways > 1:
        own = lax.psum_scatter(own, "w", scatter_dimension=0, tiled=True)
    quarters = own.reshape(PLANES, rows // PLANES, model_dim)
    got = [shift(pick(quarters, (here + step) % PLANES), step) for step in (1, 2, 3)]
    return lowered(pick(quarters, here), *got)


def to_groups(theirs, mine):
    here = lax.axis_index("z")
    both = lowered(mine, swap(theirs, "x"))
    if lax.axis_size("w") > 1:
        both = lax.psum_scatter(both, "w", scatter_dimension=1, tiled=False)
    else:
        both = both[:, 0]
    got = [shift(pick(both, (here + step) % PLANES), step) for step in (1, 2, 3)]
    return added(pick(both, here), *got)


def from_groups(tensor):
    here, at_x = lax.axis_index("z"), lax.axis_index("x")
    if lax.axis_size("w") > 1:
        tensor = lax.all_gather(tensor, "w", axis=0, tiled=False)
    else:
        tensor = tensor[None]
    found = [(tensor, here, at_x)]
    for step in (1, 3, 2):
        found.append((shift(tensor, step), (here - step) % PLANES, at_x))
    return found + [(swap(got, "x"), from_z, 1 - at_x) for got, from_z, _ in found]


def total_of(values):
    for axis in ("core", "y", "x"):
        values = values + swap(values, axis)
    for step in (1, 2):
        values = values + lax.ppermute(values, "z", [(i, i ^ step) for i in range(PLANES)])
    if lax.axis_size("w") > 1:
        values = lax.psum(values, "w")
    return values


def _groups(width):
    return [(at,min(128,width-at)) for at in range(0,width,128)]

def _head_part(rows, at, wide):
    lane=lax.broadcasted_iota(jnp.int32,rows.shape,1)
    return jnp.where((lane>=at)&(lane<at+wide),rows,jnp.zeros_like(rows))

def attend_kernel(block, start_ref, q_ref, k_ref, v_ref, low_ref, out_ref, lse_ref, vt_ref):
    step=pl.program_id(0)
    width=q_ref.shape[1]
    for at,wide in _groups(width):
        @pl.when(step==0)
        def _():
            vt_ref[at:at+wide,:]=v_ref[:,at:at+wide].astype(jnp.float32).T.astype(jnp.bfloat16)
    start=start_ref[...]
    sub=lax.broadcasted_iota(jnp.int32,(block,block),0)
    lane=lax.broadcasted_iota(jnp.int32,(block,block),1)
    groups=_groups(width)
    heads=[(at,h) for at,wide in groups for h in range(wide//HEAD_SIZE)]
    parts=[]
    for at,wide in groups:
        queries=q_ref[:,at:at+wide]*jnp.bfloat16(HEAD_SIZE**-0.5)
        parts+=[_head_part(queries,h*HEAD_SIZE,HEAD_SIZE) for h in range(wide//HEAD_SIZE)]
    def chunk(place, carry, diag):
        offset=pl.multiple_of(place*block,block)
        allowed=sub>=start-offset
        if diag:
            allowed=allowed&(sub<=lane)
        fresh=[]
        scored=[]
        for i,(at,h) in enumerate(heads):
            keys=k_ref[pl.ds(offset,block),at:min(at+128,width)]
            scores=lax.dot_general(keys,parts[i],LANES_BOTH,preferred_element_type=jnp.float32)
            scored.append(jnp.where(allowed,scores,MASKED))
        for i,(at,h) in enumerate(heads):
            peak,total,acc=carry[i]
            scores=scored[i]
            higher=jnp.maximum(peak,jnp.max(scores,0,keepdims=True))
            raised=jnp.exp(scores-higher)
            shrink=jnp.exp(peak-higher)
            vt=vt_ref[i*HEAD_SIZE:(i+1)*HEAD_SIZE,pl.ds(offset,block)]
            acc=acc*shrink+jnp.dot(vt,raised.astype(jnp.bfloat16),preferred_element_type=jnp.float32)
            fresh.append((higher,total*shrink+jnp.sum(raised,0,keepdims=True),acc))
        return tuple(fresh)
    carry=tuple((jnp.full((1,block),MASKED,jnp.float32),jnp.zeros((1,block),jnp.float32),jnp.zeros((HEAD_SIZE,block),jnp.float32)) for h in heads)
    carry=lax.fori_loop(0,step,lambda c,x:chunk(c,x,False),carry)
    carry=chunk(step,carry,True)
    for at,wide in groups:
        own=carry[at//HEAD_SIZE:(at+wide)//HEAD_SIZE]
        mixed=jnp.concatenate([acc*(1.0/total) for peak,total,acc in own],0).T
        out_ref[:,at:at+wide]=mixed
        low_ref[:,at:at+wide]=mixed.astype(jnp.bfloat16)
    for i in range(len(heads)):
        peak,total,acc=carry[i]
        lse_ref[i:i+1,:]=peak+jnp.log(total)

def attend(start, queries, keys, values, block=512):
    length,width=queries.shape
    whole=lambda i:(0,0)
    rows=lambda i:(i,0)
    cols=lambda i:(0,i)
    return pl.pallas_call(
        partial(attend_kernel,block),
        grid=(length//block,),
        in_specs=[pl.BlockSpec((1,block),cols),pl.BlockSpec((block,width),rows),pl.BlockSpec((length,width),whole),pl.BlockSpec((length,width),whole)],
        out_specs=[pl.BlockSpec((block,width),rows),pl.BlockSpec((block,width),rows),pl.BlockSpec((8,block),cols)],
        out_shape=[jax.ShapeDtypeStruct((length,width),jnp.bfloat16),jax.ShapeDtypeStruct((length,width),jnp.float32),jax.ShapeDtypeStruct((8,length),jnp.float32)],
        scratch_shapes=[pltpu.VMEM((width,length),jnp.bfloat16)],
        compiler_params=pltpu.CompilerParams(vmem_limit_bytes=40<<20,dimension_semantics=("arbitrary",)),
    )(start,queries,keys,values)

def attend_back_kernel(block, start_ref, q_ref, k_ref, v_ref, do_ref, out_ref, lse_ref, dq_ref, dk_ref, dv_ref, kt_ref, dka_ref, dva_ref):
    step=pl.program_id(0)
    width=q_ref.shape[1]
    @pl.when(step==0)
    def _():
        for at,wide in _groups(width):
            kt_ref[at:at+wide,:]=k_ref[:,at:at+wide].astype(jnp.float32).T.astype(jnp.bfloat16)
        dka_ref[...]=jnp.zeros_like(dka_ref)
        dva_ref[...]=jnp.zeros_like(dva_ref)
    start=start_ref[...]
    sub=lax.broadcasted_iota(jnp.int32,(block,block),0)
    lane=lax.broadcasted_iota(jnp.int32,(block,block),1)
    temper=HEAD_SIZE**-0.5
    for at,wide in _groups(width):
        queries=q_ref[:,at:at+wide]*jnp.bfloat16(temper)
        grads=do_ref[:,at:at+wide]
        heads=range(wide//HEAD_SIZE)
        parts=[_head_part(queries,h*HEAD_SIZE,HEAD_SIZE) for h in heads]
        dparts=[_head_part(grads,h*HEAD_SIZE,HEAD_SIZE) for h in heads]
        crossed=(grads.astype(jnp.float32)*out_ref[:,at:at+wide]).T
        deltas=[jnp.sum(crossed[h*HEAD_SIZE:(h+1)*HEAD_SIZE],0,keepdims=True) for h in heads]
        lses=[lse_ref[at//HEAD_SIZE+h:at//HEAD_SIZE+h+1,:] for h in heads]
        def chunk(place, carry, diag):
            offset=pl.multiple_of(place*block,block)
            keys=k_ref[pl.ds(offset,block),at:at+wide]
            values=v_ref[pl.ds(offset,block),at:at+wide]
            allowed=sub>=start-offset
            if diag:
                allowed=allowed&(sub<=lane)
            fresh=[]
            dkey=None
            for h in heads:
                scores=lax.dot_general(keys,parts[h],LANES_BOTH,preferred_element_type=jnp.float32)
                chance=jnp.exp(jnp.where(allowed,scores,MASKED)-lses[h])
                dchance=lax.dot_general(values,dparts[h],LANES_BOTH,preferred_element_type=jnp.float32)
                dscores=(chance*(dchance-deltas[h])).astype(jnp.bfloat16)
                one=jnp.dot(dscores,parts[h],preferred_element_type=jnp.float32)
                two=jnp.dot(chance.astype(jnp.bfloat16),dparts[h],preferred_element_type=jnp.float32)
                dkey,dval=(one,two) if dkey is None else (dkey+one,dval+two)
                kt=kt_ref[at+h*HEAD_SIZE:at+(h+1)*HEAD_SIZE,pl.ds(offset,block)]
                fresh.append(carry[h]+jnp.dot(kt,dscores,preferred_element_type=jnp.float32))
            dka_ref[pl.ds(offset,block),at:at+wide]+=dkey
            dva_ref[pl.ds(offset,block),at:at+wide]+=dval
            return tuple(fresh)
        carry=tuple(jnp.zeros((HEAD_SIZE,block),jnp.float32) for h in heads)
        carry=lax.fori_loop(0,step,lambda c,x:chunk(c,x,False),carry)
        carry=chunk(step,carry,True)
        dq_ref[:,at:at+wide]=(jnp.concatenate(carry,0).T*temper).astype(jnp.bfloat16)
    @pl.when(step==pl.num_programs(0)-1)
    def _():
        dk_ref[...]=dka_ref[...].astype(jnp.bfloat16)
        dv_ref[...]=dva_ref[...].astype(jnp.bfloat16)

def attend_back(start, queries, keys, values, grad, out, lse, block=512):
    length,width=queries.shape
    whole=lambda i:(0,0)
    rows=lambda i:(i,0)
    cols=lambda i:(0,i)
    return pl.pallas_call(
        partial(attend_back_kernel,block),
        grid=(length//block,),
        in_specs=[pl.BlockSpec((1,block),cols),pl.BlockSpec((block,width),rows),pl.BlockSpec((length,width),whole),pl.BlockSpec((length,width),whole),
                  pl.BlockSpec((block,width),rows),pl.BlockSpec((block,width),rows),pl.BlockSpec((8,block),cols)],
        out_specs=[pl.BlockSpec((block,width),rows),pl.BlockSpec((length,width),whole),pl.BlockSpec((length,width),whole)],
        out_shape=[jax.ShapeDtypeStruct((length,width),jnp.bfloat16)]*3,
        scratch_shapes=[pltpu.VMEM((width,length),jnp.bfloat16),pltpu.VMEM((length,width),jnp.float32),pltpu.VMEM((length,width),jnp.float32)],
        compiler_params=pltpu.CompilerParams(vmem_limit_bytes=40<<20,dimension_semantics=("arbitrary",)),
    )(start,queries,keys,values,grad,out,lse)

def frame_kernel(gram_ref, span_ref, out_ref, work_ref, turn_ref):
    count,size,_=gram_ref.shape
    work_ref[...]=gram_ref[...]
    out_ref[...]=span_ref[...]
    sub=lax.broadcasted_iota(jnp.int32,(count,8,size),1)
    def panel(step, unused):
        top=pl.multiple_of(step*8,8)
        left=work_ref[:,pl.ds(top,8),:]
        right=out_ref[:,pl.ds(top,8),:]
        for k in range(8):
            column=left[:,:,k:k+1]
            pivot=column[:,k:k+1,:]
            inverse=lax.rsqrt(pivot)
            inverse=inverse*(1.5-0.5*pivot*inverse*inverse)
            row_left=left[:,k:k+1,:]*inverse
            row_right=right[:,k:k+1,:]*inverse
            share=column*inverse
            left=jnp.where(sub>k,left-share*row_left,jnp.where(sub==k,row_left,left))
            right=jnp.where(sub>k,right-share*row_right,jnp.where(sub==k,row_right,right))
        out_ref[:,pl.ds(top,8),:]=right
        for b in range(count):
            spread=jnp.concatenate([left[b],jnp.zeros((size-8,size),jnp.float32)],0)
            turn_ref[b]=spread.T
        turned_left=pltpu.roll(left.reshape(count*8,size),size-8,1).reshape(count,8,size)
        def trail(place, unused):
            row=pl.multiple_of(place*8,8)
            shares=turn_ref[:,pl.ds(pl.multiple_of(row-top,8),8),:]
            below_left=pltpu.roll(work_ref[:,pl.ds(row,8),:].reshape(count*8,size),size-8,1).reshape(count,8,size)
            below_right=out_ref[:,pl.ds(row,8),:]
            for k in range(8):
                share=shares[:,:,k:k+1]
                below_left=below_left-share*turned_left[:,k:k+1,:]
                below_right=below_right-share*right[:,k:k+1,:]
            work_ref[:,pl.ds(row,8),:]=below_left
            out_ref[:,pl.ds(row,8),:]=below_right
            return unused
        return lax.fori_loop(step+1,size//8,trail,unused)
    lax.fori_loop(0,size//8,panel,0)

def frame(gram, span):
    return pl.pallas_call(
        frame_kernel,
        out_shape=jax.ShapeDtypeStruct(gram.shape,jnp.float32),
        scratch_shapes=[pltpu.VMEM(gram.shape,jnp.float32),pltpu.VMEM(gram.shape,jnp.float32)],
        compiler_params=pltpu.CompilerParams(vmem_limit_bytes=40<<20),
    )(gram,span)


def adam_update(weight, first_mom, second, gradient, step_rate):
    first_mom = BETA_ONE * first_mom + (1.0 - BETA_ONE) * gradient
    second = BETA_TWO * second + (1.0 - BETA_TWO) * gradient * gradient
    direction = (
        first_mom / (1.0 - BETA_ONE**STEP) / (jnp.sqrt(second / (1.0 - BETA_TWO**STEP)) + ADAM_EPS)
    )
    return (weight - step_rate * (direction + WEIGHT_DECAY * weight), first_mom, second)


def rotated_update(weight, first_mom, second, gradient, factor, stat, basis):
    blocks, block_len = basis.shape[1], basis.shape[2]
    shaped = gradient.reshape(-1, blocks, block_len)
    frames, stats = basis[0], stat[0]
    turned = factor * jnp.einsum("rbi,bij->rbj", shaped, frames, precision=HIGHEST).reshape(
        gradient.shape
    )
    outer = jnp.einsum("rbi,rbj->bij", shaped, shaped, precision=HIGHEST)
    first_mom = BETA_ONE * first_mom + (1.0 - BETA_ONE) * turned
    second = BETA_TWO * second + (1.0 - BETA_TWO) * turned * turned
    direction = (
        first_mom / (1.0 - BETA_ONE**STEP) / (jnp.sqrt(second / (1.0 - BETA_TWO**STEP)) + ADAM_EPS)
    )
    back = jnp.einsum(
        "rbj,bij->rbi", direction.reshape(shaped.shape), frames, precision=HIGHEST
    ).reshape(weight.shape)
    weight_next = weight - RATE_LAYER * (back + WEIGHT_DECAY * weight)
    stat_next = BETA_STAT * stats + (1.0 - BETA_STAT) * (factor * factor) * outer
    spanned = jnp.einsum("bij,bjk->bik", stat_next, frames, precision=HIGHEST)
    gram = jnp.einsum("bij,bik->bjk", spanned, spanned, precision=HIGHEST)
    solved = frame(gram, jnp.swapaxes(spanned, 1, 2))
    return (weight_next, first_mom, second, jnp.swapaxes(solved, 1, 2)[None], stat_next[None])


def body(
    token_ids,
    lengths,
    loss_place,
    targets,
    loss_flag,
    layer_weight,
    layer_first,
    layer_second,
    rot_basis,
    stat_matrix,
    small_params,
    small_first,
    small_second,
    embed_table,
    table_first,
    table_second,
):
    group_id = lax.axis_index(VOCAB)
    groups = lax.axis_size(VOCAB)
    part_count = lax.axis_size(SEQ)
    ways = lax.axis_size("w")
    at_x, at_y, at_c = (lax.axis_index(name) for name in ("x", "y", "core"))
    tok_rows = token_ids.shape[0] // groups
    loss_rows = loss_place.shape[0] // groups
    vocab_rows, slice_width = embed_table.shape
    vocab_live = min(groups * vocab_rows, VOCAB_REAL)
    model_dim = layer_weight.shape[1]
    hidden_units = small_params.shape[0] - 10 * model_dim
    head_width = model_dim // part_count
    length = part_count * tok_rows
    (
        bias_q,
        bias_v,
        bias_out,
        bias_up,
        bias_down,
        gain_one,
        shift_one,
        gain_two,
        shift_two,
        gain_final,
        shift_final,
    ) = pieces(small_params, model_dim, hidden_units)

    table_low = embed_table.astype(jnp.bfloat16)
    table_y = swap(table_low, "y")
    table_near = in_order(at_c, table_low, swap(table_low, "core"), 1)
    planes = gather_weights(layer_weight)
    table_far = in_order(at_c, table_y, swap(table_y, "core"), 1)
    table_full = in_order(at_y, table_near, table_far, 1)

    local_ids = (token_ids[:, 0] - group_id * vocab_rows).reshape(PLANES, ways, 2, tok_rows)
    row_range = jnp.arange(vocab_rows, dtype=jnp.int32)

    def looked_up(ids, rows_of):
        hot = (ids.reshape(-1)[:, None] == row_range[None, :]).astype(jnp.bfloat16)
        got = plain_dot(hot, rows_of).astype(jnp.bfloat16)
        return got.reshape(ids.shape + (rows_of.shape[1],))

    halves = []
    for rows_of in (table_near, table_far):
        chunks = []
        for at in range(0, tok_rows, tok_rows // 2):
            ids = local_ids[..., at : at + tok_rows // 2]
            chunks.append(
                to_groups(
                    looked_up(pick(ids, 1 - at_x, 2), rows_of),
                    looked_up(pick(ids, at_x, 2), rows_of),
                )
            )
        halves.append(jnp.concatenate(chunks, 0))
    embedded = in_order(at_y, halves[0], halves[1], 1)

    group_lengths = jnp.take(lengths, group_id, axis=0)
    bounds = jnp.cumsum(group_lengths)[:-1]
    positions = jnp.arange(length, dtype=jnp.int32)
    starts = jnp.max(
        jnp.where(positions[:, None] >= bounds[None, :], bounds[None, :], 0), 1
    ).astype(jnp.int32)[None]

    normed_low = layer_norm(embedded, gain_one, shift_one).astype(jnp.bfloat16)
    joined = low_dot(normed_low, planes[0]) + jnp.concatenate(
        [bias_q, jnp.zeros_like(bias_q), bias_v]
    )
    joined_heads = lax.all_to_all(
        joined.astype(jnp.bfloat16).reshape(tok_rows, 3, part_count, head_width),
        SEQ,
        split_axis=2,
        concat_axis=0,
        tiled=True,
    )
    queries, key_rows, values = (joined_heads[:, at, 0] for at in range(3))
    mixture, mixture_wide, logsum = attend(starts, queries, key_rows, values)
    mixed_low = lax.all_to_all(
        mixture.reshape(part_count, tok_rows, 1, head_width),
        SEQ,
        split_axis=0,
        concat_axis=2,
        tiled=True,
    ).reshape(tok_rows, model_dim)
    half = planes[1].shape[0] - model_dim
    rest = hidden_units - half
    project_out, expand_one = planes[1][:model_dim], planes[1][model_dim:]
    expand_two, reduce_one = planes[2][:rest], planes[2][rest:]
    reduce_two = planes[3]
    reduce_cut = reduce_one.shape[0]
    middle = embedded + low_dot(mixed_low, project_out) + bias_out
    normed_two_low = layer_norm(middle, gain_two, shift_two).astype(jnp.bfloat16)
    hidden_one = low_dot(normed_two_low, expand_one) + bias_up[:half]
    hidden_two = low_dot(normed_two_low, expand_two) + bias_up[half:]
    hidden = jnp.concatenate([hidden_one, hidden_two], 1)
    active_low = smooth(hidden).astype(jnp.bfloat16)
    residual_out = (
        middle
        + plain_dot(active_low[:, :reduce_cut], reduce_one)
        + plain_dot(active_low[:, reduce_cut:], reduce_two)
        + bias_down
    )
    final_out = layer_norm(residual_out, gain_final, shift_final)
    own_pos = lax.dynamic_slice_in_dim(loss_place[:, 0], group_id * loss_rows, loss_rows, 0)
    pos_hot = own_pos[:, None] == jnp.arange(tok_rows, dtype=jnp.int32)[None, :]
    chosen = plain_dot(pos_hot.astype(jnp.bfloat16), final_out.astype(jnp.bfloat16)).astype(
        jnp.bfloat16
    )

    def whole_groups(tensor, kinds):
        found = from_groups(tensor)
        gathered = jnp.zeros((PLANES, ways, 2) + tensor.shape, kinds)
        for got, from_z, from_x in found:
            gathered = lax.dynamic_update_slice(
                gathered, got[None, :, None], (from_z, 0, from_x) + (0,) * tensor.ndim
            )
        return gathered.reshape((groups,) + tensor.shape)

    head_rows = whole_groups(chosen, jnp.bfloat16).reshape(groups * loss_rows, model_dim)
    logits = low_dot(head_rows, table_full)
    if groups * vocab_rows > vocab_live:
        row_ids = group_id * vocab_rows + row_range
        logits = jnp.where((row_ids < vocab_live)[None, :], logits, MASKED)
    target_local = targets[:, 0] - group_id * vocab_rows
    target_hot = row_range[None, :] == target_local[:, None]
    target_part = jnp.sum(jnp.where(target_hot, logits, 0.0), 1)
    local_peak = jnp.max(logits, 1)
    local_sum = jnp.sum(jnp.exp(logits - local_peak[:, None]), 1)
    everyone = whole_groups(jnp.stack([local_peak, local_sum, target_part]), jnp.float32)
    peak_all = jnp.max(everyone[:, 0], 0)
    sum_all = jnp.sum(everyone[:, 1] * jnp.exp(everyone[:, 0] - peak_all[None]), 0)
    target_logit = jnp.sum(everyone[:, 2], 0)
    logsum_all = peak_all + jnp.log(sum_all)
    weight_rows = loss_flag[:, 0].astype(jnp.float32)
    chance = jnp.exp(logits - logsum_all[:, None])
    grad_logits = weight_rows[:, None] * (chance - target_hot.astype(jnp.float32))
    grad_low = grad_logits.astype(jnp.bfloat16)
    grad_rows = plain_dot(grad_low, table_full).astype(jnp.bfloat16)
    grad_rows = grad_rows.reshape(PLANES, ways, 2, loss_rows, model_dim)
    grad_chosen = to_groups(pick(grad_rows, 1 - at_x, 2), pick(grad_rows, at_x, 2))
    grad_final = lax.dot_general(
        pos_hot.astype(jnp.float32),
        grad_chosen,
        (((0,), (0,)), ((), ())),
        precision=HIGHEST,
        preferred_element_type=jnp.float32,
    )

    head_cols = head_rows.reshape(-1, 2, 2, slice_width)

    def table_part(by_y, by_c):
        cols = pick(pick(head_cols, at_y ^ by_y, 1), at_c ^ by_c, 1)
        return outer_dot(grad_low, cols).astype(jnp.bfloat16)

    far_sum = lowered(table_part(1, 0), swap(table_part(1, 1), "core"))
    near_sum = added(table_part(0, 0), swap(table_part(0, 1), "core"))
    head_table_grad = added(near_sum, swap(far_sum, "y"))

    is_first = group_id == 0
    loss_part = jnp.where(is_first, jnp.sum(weight_rows * (logsum_all - target_logit)), 0.0)
    count_part = jnp.where(is_first, jnp.sum(weight_rows), 0.0)
    unused, final_back = jax.vjp(layer_norm, residual_out, gain_final, shift_final)
    grad_resid, grad_gain_final, grad_shift_final = final_back(grad_final)
    resid_low = grad_resid.astype(jnp.bfloat16)
    grad_bias_down = column_sum(resid_low)
    grad_active = jnp.concatenate(
        [low_dot(resid_low, reduce_one), low_dot(resid_low, reduce_two)], 1
    )
    plane_three = outer_dot(active_low[:, reduce_cut:], resid_low, jnp.bfloat16)
    piece_three = scatter_plane(plane_three)
    unused, gelu_back = jax.vjp(smooth, hidden)
    hidden_low = gelu_back(grad_active)[0].astype(jnp.bfloat16)
    grad_bias_up = column_sum(hidden_low)
    plane_two = jnp.concatenate(
        [
            outer_dot(hidden_low[:, half:], normed_two_low, jnp.bfloat16),
            outer_dot(active_low[:, :reduce_cut], resid_low, jnp.bfloat16),
        ],
        0,
    )
    piece_two = scatter_plane(plane_two)
    unused, two_back = jax.vjp(layer_norm, middle, gain_two, shift_two)
    grad_middle_part, grad_gain_two, grad_shift_two = two_back(
        plain_dot(hidden_low[:, :half], expand_one) + plain_dot(hidden_low[:, half:], expand_two)
    )
    grad_middle = grad_resid + grad_middle_part
    middle_low = grad_middle.astype(jnp.bfloat16)
    grad_bias_out = column_sum(middle_low)
    grad_mixed = plain_dot(middle_low, project_out)
    grad_heads = lax.all_to_all(
        grad_mixed.astype(jnp.bfloat16).reshape(tok_rows, part_count, head_width),
        SEQ,
        split_axis=1,
        concat_axis=0,
        tiled=True,
    )[:, 0]
    plane_one = jnp.concatenate(
        [
            outer_dot(middle_low, mixed_low, jnp.bfloat16),
            outer_dot(hidden_low[:, :half], normed_two_low, jnp.bfloat16),
        ],
        0,
    )
    piece_one = scatter_plane(plane_one)
    grad_query, grad_keys, grad_values = attend_back(
        starts, queries, key_rows, values, grad_heads, mixture_wide, logsum
    )
    grad_joined = lax.all_to_all(
        jnp.stack([grad_query, grad_keys, grad_values], 1).reshape(
            part_count, tok_rows, 3, 1, head_width
        ),
        SEQ,
        split_axis=0,
        concat_axis=3,
        tiled=True,
    ).reshape(tok_rows, 3 * model_dim)
    unused, one_back = jax.vjp(layer_norm, embedded, gain_one, shift_one)
    grad_embed_part, grad_gain_one, grad_shift_one = one_back(plain_dot(grad_joined, planes[0]))
    rows_back = (grad_middle + grad_embed_part).astype(jnp.bfloat16)
    rows_back = lax.all_to_all(rows_back, SEQ, split_axis=1, concat_axis=0, tiled=True)
    all_ids = lax.all_gather(token_ids, SEQ, axis=1, tiled=True) - group_id * vocab_rows
    all_ids = all_ids.reshape(PLANES, ways, 2, tok_rows, part_count).swapaxes(3, 4)
    table_grad = head_table_grad
    for got, from_z, from_x in from_groups(rows_back):
        ids = pick(pick(all_ids, from_z, 0), from_x, 1).reshape(1, -1)
        hot = (row_range[:, None] == ids).astype(jnp.bfloat16)
        table_grad = table_grad + plain_dot(hot, got.reshape(-1, slice_width))
    grad_bias_q = column_sum(grad_joined[:, :model_dim])
    grad_bias_v = column_sum(grad_joined[:, 2 * model_dim :])
    piece_zero = scatter_plane(outer_dot(grad_joined, normed_low, jnp.bfloat16))
    layer_grad = (
        exchange_planes(jnp.stack([piece_zero, piece_one, piece_two, piece_three]))
        .reshape(layer_weight.shape)
        .astype(jnp.float32)
    )
    early = total_of(
        jnp.concatenate(
            [
                grad_bias_out,
                grad_bias_up,
                grad_bias_down,
                grad_gain_two,
                grad_shift_two,
                grad_gain_final,
                grad_shift_final,
                jnp.stack([loss_part, count_part]),
            ]
        )
    )
    late = total_of(jnp.concatenate([grad_bias_q, grad_bias_v, grad_gain_one, grad_shift_one]))
    cut = 2 * model_dim + hidden_units
    small_grad = jnp.concatenate([late[: 2 * model_dim], early[:cut], late[2 * model_dim :], early[cut:-2]])
    loss_sum, loss_count = early[-2], early[-1]
    squares = total_of(jnp.sum(layer_grad * layer_grad) + jnp.sum(table_grad * table_grad))
    gradient_norm = jnp.sqrt(squares + jnp.sum(small_grad * small_grad))
    factor = 1.0 / jnp.maximum(gradient_norm, 1.0)
    out_bias_grad = factor * small_grad[2 * model_dim : 3 * model_dim]
    layer_next, layer_first_next, layer_second_next, basis_next, stat_next = rotated_update(
        layer_weight, layer_first, layer_second, layer_grad, factor, stat_matrix, rot_basis
    )
    small_next, small_first_next, small_second_next = adam_update(
        small_params, small_first, small_second, factor * small_grad, RATE_SMALL
    )
    table_next, table_first_next, table_second_next = adam_update(
        embed_table, table_first, table_second, factor * table_grad, RATE_TABLE
    )
    return (
        loss_sum,
        loss_count,
        gradient_norm,
        layer_next,
        layer_first_next,
        layer_second_next,
        basis_next,
        stat_next,
        small_next,
        small_first_next,
        small_second_next,
        table_next,
        table_first_next,
        table_second_next,
        out_bias_grad,
    )


def solution(mesh):
    vocab, seq = mesh.shape["vocab"], mesh.shape["seq"]
    inner = Mesh(mesh.devices.reshape(PLANES, vocab // 8, 2, seq // 2, 2), ALL)
    in_specs = (
        P(None, SEQ),
        P(),
        P(None, SEQ),
        P(None, SEQ),
        P(None, SEQ),
        P(ALL, None),
        P(ALL, None),
        P(ALL, None),
        P(ALL, None, None, None),
        P(ALL, None, None, None),
        P(),
        P(),
        P(),
        P(VOCAB, SEQ),
        P(VOCAB, SEQ),
        P(VOCAB, SEQ),
    )
    out_specs = (
        P(),
        P(),
        P(),
        P(ALL, None),
        P(ALL, None),
        P(ALL, None),
        P(ALL, None, None, None),
        P(ALL, None, None, None),
        P(),
        P(),
        P(),
        P(VOCAB, SEQ),
        P(VOCAB, SEQ),
        P(VOCAB, SEQ),
        P(),
    )
    return jax.shard_map(body, mesh=inner, in_specs=in_specs, out_specs=out_specs, check_vma=False)
```

time: 2300 us -> 1610 us (0.70)
  waiting for transfers between devices: 1240 us -> 728 us
  other arithmetic: 445 us -> 108 us
  starting transfers between devices: 15.1 us -> 210 us
  matrix products: 310 us -> 205 us
  local copies, waits for them, and re-layouts: 144 us -> 249 us
  blocking collectives: 113 us -> 13.5 us
  Pallas kernels: 0 us -> 79.8 us
    reduce_scatter x3 -> x0, waiting for transfers between devices: 1020 us -> none  [the longest x1 651 us: body(): lax.psum_scatter(layer_grad, ('vocab', 'seq'), scatter_dimension=0, tiled...]
    ppermute x0 -> x144, waiting for transfers between devices: none -> 717 us  [the longest x84 465 us: swap(): return lax.ppermute(tensor, axis, [(0, 1), (1, 0)])]
    another operation x11 -> x8, other arithmetic: 224 us -> 5.57 us  [the longest x1 3.56 us: body(): jnp.stack([grad_query, grad_keys, grad_values], 1)]
    ppermute x0 -> x144, starting transfers between devices: none -> 186 us  [the longest x54 99 us: shift(): lax.ppermute(tensor, 'z', [(i, (i + step) % PLANES) for i in range(PLANES)])]
    all_gather x4 -> x0, waiting for transfers between devices: 159 us -> none  [the longest x1 82.5 us: body(): lax.all_gather(grad_embedded.astype(jnp.bfloat16), 'vocab', axis=0, tiled...]
    dot_general x31 -> x13, matrix products: 216 us -> 62.8 us  [the longest x7 49.1 us: low_dot(): lax.dot_general(left, right, LANES_BOTH, preferred_element_type=jnp.float32)]
    pallas_call x0 -> x3, Pallas kernels: none -> 79.8 us  [the longest x1 37.6 us: frame(): pl.pallas_call(frame_kernel, out_shape=jax.ShapeDtypeStruct(gram.shape, j...]
    dynamic_update_slice x0 -> x79, local copies, waits for them, and re-layouts: none -> 77.8 us  [the longest x64 76.9 us: gather_weights(): lax.dynamic_update_slice(whole, both[:, spot:spot + 1], (0, owner, offset...]
  transfers between devices with their start and end apart: 12 -> 149, of which waited for: 9 -> 61; matrix products, arithmetic and copies ran while one was open for 6% -> 27% of each run, Pallas kernels for 0% -> 3%
where the time goes in v1:
time: 1610 us; the launch traced here: 1600 us
  waiting for transfers between devices  728 us (45%)
  local copies, waits for them, and re-layouts  249 us (15%)
  starting transfers between devices  210 us (13%)
  matrix products  205 us (13%)
  other arithmetic  108 us (7%)
  Pallas kernels  79.8 us (5%)
    ppermute x84, waiting for transfers between devices, swap(): return lax.ppermute(tensor, axis, [(0, 1), (1, 0)])  465 us
    ppermute x54, waiting for transfers between devices, shift(): lax.ppermute(tensor, 'z', [(i, (i + step) % PLANES) for i in range(PLANES)])  243 us
    ppermute x54, starting transfers between devices, shift(): lax.ppermute(tensor, 'z', [(i, (i + step) % PLANES) for i in range(PLANES)])  99 us
    dot_general x24, matrix products, plain_dot(): return jnp.dot(left, right, preferred_element_type=jnp.float32)  91.1 us
    ppermute x84, starting transfers between devices, swap(): return lax.ppermute(tensor, axis, [(0, 1), (1, 0)])  76.9 us
    dynamic_update_slice x64, local copies, waits for them, and re-layouts, gather_weights(): lax.dynamic_update_slice(whole, both[:, spot:spot + 1], (0, owner, offset...  76.9 us
    dot_general x10, matrix products, outer_dot(): lax.dot_general(left, right, (((0,), (0,)), ((), ())), preferred_element_...  50.7 us
    dot_general x7, matrix products, low_dot(): lax.dot_general(left, right, LANES_BOTH, preferred_element_type=jnp.float32)  49.1 us
  transfers between devices with their start and end apart: 149, of which 61 were waited for; matrix products, arithmetic and copies ran while one was open for 27% of the time, Pallas kernels for 3%

profile of v1, /device:TPU:0, one launch (start us, length us, event | category | flops | bytes accessed | tf_op | source)
XLA Modules:
  0.0 1603.2 jit_solution(14268862972716609434)
XLA Ops:
  55.0 28.6 %collective-permute-done.45 = bf16[120,1280]{1,0:T(8,128)(2,1)S(1)} collective-permute-done((bf16[120,1280]{1,0:T(8,128)(2,1)S(1)}, bf16[120,1280]{1,0:T(8,128)(2,1)S(1)}, u32[]{:S(2)}, u32[]{:S(2)}) %collective-permute-start.45) | collective-permute-done | bytes 307232 | tf_op jit(solution)/shard_map/ppermute | solution.py:71
  87.6 22.3 %collective-permute-done.34 = bf16[120,1280]{1,0:T(8,128)(2,1)S(1)} collective-permute-done((bf16[120,1280]{1,0:T(8,128)(2,1)S(1)}, bf16[120,1280]{1,0:T(8,128)(2,1)S(1)}, u32[]{:S(2)}, u32[]{:S(2)}) %collective-permute-start.34) | collective-permute-done | bytes 307232 | tf_op jit(solution)/shard_map/ppermute | solution.py:71
  113.9 22.3 %collective-permute-done.23 = bf16[120,1280]{1,0:T(8,128)(2,1)S(1)} collective-permute-done((bf16[120,1280]{1,0:T(8,128)(2,1)S(1)}, bf16[120,1280]{1,0:T(8,128)(2,1)S(1)}, u32[]{:S(2)}, u32[]{:S(2)}) %collective-permute-start.23) | collective-permute-done | bytes 307232 | tf_op jit(solution)/shard_map/ppermute | solution.py:71
  243.5 19.9 %collective-permute-done.5 = bf16[4,1,192,640]{3,2,1,0:T(8,128)(2,1)S(1)} collective-permute-done((bf16[4,1,192,640]{3,2,1,0:T(8,128)(2,1)S(1)}, bf16[4,1,192,640]{3,2,1,0:T(8,128)(2,1)S(1)}, u32[]{:S(2)}, u32[]{:S(2)}) %collective-permute-start.5) | collective-permute-done | bytes 983072 | tf_op jit(solution)/shard_map/ppermute | solution.py:67
  327.9 20.8 %collective-permute-done.60 = bf16[1,2,320,1280]{3,2,1,0:T(8,128)(2,1)} collective-permute-done((bf16[1,2,320,1280]{3,2,1,0:T(8,128)(2,1)S(1)}, bf16[1,2,320,1280]{3,2,1,0:T(8,128)(2,1)}, u32[]{:S(2)}, u32[]{:S(2)}) %collective-permute-start.60) | collective-permute-done | bytes 1638432 | tf_op jit(solution)/shard_map/ppermute | solution.py:67
  352.9 30.9 %collective-permute-done.38 = bf16[1,2,320,1280]{3,2,1,0:T(8,128)(2,1)} collective-permute-done((bf16[1,2,320,1280]{3,2,1,0:T(8,128)(2,1)S(1)}, bf16[1,2,320,1280]{3,2,1,0:T(8,128)(2,1)}, u32[]{:S(2)}, u32[]{:S(2)}) %collective-permute-start.38) | collective-permute-done | bytes 1638432 | tf_op jit(solution)/shard_map/ppermute | solution.py:67
  394.4 24.4 %collective-permute-done.27 = bf16[1,2,320,1280]{3,2,1,0:T(8,128)(2,1)S(1)} collective-permute-done((bf16[1,2,320,1280]{3,2,1,0:T(8,128)(2,1)S(1)}, bf16[1,2,320,1280]{3,2,1,0:T(8,128)(2,1)S(1)}, u32[]{:S(2)}, u32[]{:S(2)}) %collective-permute-start.27) | collective-permute-done | bytes 1638432 | tf_op jit(solution)/shard_map/ppermute | solution.py:67
  427.6 23.1 %collective-permute-done.49 = bf16[1,2,320,1280]{3,2,1,0:T(8,128)(2,1)S(1)} collective-permute-done((bf16[1,2,320,1280]{3,2,1,0:T(8,128)(2,1)S(1)}, bf16[1,2,320,1280]{3,2,1,0:T(8,128)(2,1)S(1)}, u32[]{:S(2)}, u32[]{:S(2)}) %collective-permute-start.49) | collective-permute-done | bytes 1638432 | tf_op jit(solution)/shard_map/ppermute | solution.py:67
  477.3 24.8 %collective-permute-done.31 = bf16[1,2,160,1280]{3,2,1,0:T(8,128)(2,1)S(1)} collective-permute-done((bf16[1,2,160,1280]{3,2,1,0:T(8,128)(2,1)S(1)}, bf16[1,2,160,1280]{3,2,1,0:T(8,128)(2,1)S(1)}, u32[]{:S(2)}, u32[]{:S(2)}) %collective-permute-start.31) | collective-permute-done | bytes 819232 | tf_op jit(solution)/shard_map/ppermute | solution.py:67
  565.7 16.7 %collective-permute-done.53 = bf16[1,2,160,1280]{3,2,1,0:T(8,128)(2,1)} collective-permute-done((bf16[1,2,160,1280]{3,2,1,0:T(8,128)(2,1)S(1)}, bf16[1,2,160,1280]{3,2,1,0:T(8,128)(2,1)}, u32[]{:S(2)}, u32[]{:S(2)}) %collective-permute-start.53) | collective-permute-done | bytes 819232 | tf_op jit(solution)/shard_map/ppermute | solution.py:67
  875.9 27.3 %shard_map.272 = (bf16[1536,320]{1,0:T(8,128)(2,1)S(1)}, bf16[1536,320]{1,0:T(8,128)(2,1)S(1)}, bf16[1536,320]{1,0:T(8,128)(2,1)S(1)}) custom-call(s32[1,1536]{1,0:T(1,128)S(1)} %broadcast_in_dim.136.start_ref, bf16[1536,320]{1,0:T(8,128)(2,1)S(1)} %copy-done.2, bf16[1536,320]{1,0:T(8,128)(2,1)S(1)} %get-tuple-element.165.k_ref, ...), custom_call_target="tpu_custom_call" | custom-call | tf_op jit(solution)/shard_map/pallas_call | solution.py:333
  936.0 19.8 %collective-permute-done.85 = f32[12802]{0:T(1024)S(1)} collective-permute-done((f32[12802]{0:T(1024)S(1)}, f32[12802]{0:T(1024)S(1)}, u32[]{:S(2)}, u32[]{:S(2)}) %collective-permute-start.85) | collective-permute-done | bytes 51240 | tf_op jit(solution)/shard_map/ppermute | solution.py:67
  1047.0 17.1 %collective-permute-done.127 = bf16[1,1536,320]{1,2,0:T(8,128)(2,1)S(1)} collective-permute-done((bf16[1,1536,320]{1,2,0:T(8,128)(2,1)S(1)}, bf16[1,1536,320]{1,2,0:T(8,128)(2,1)S(1)}, u32[]{:S(2)}, u32[]{:S(2)}) %collective-permute-start.127) | collective-permute-done | bytes 983072 | tf_op jit(solution)/shard_map/ppermute | solution.py:71
  1073.5 28.1 %collective-permute-done.129 = bf16[1,1536,320]{1,2,0:T(8,128)(2,1)} collective-permute-done((bf16[1,1536,320]{1,2,0:T(8,128)(2,1)S(1)}, bf16[1,1536,320]{1,2,0:T(8,128)(2,1)}, u32[]{:S(2)}, u32[]{:S(2)}) %collective-permute-start.129) | collective-permute-done | bytes 983072 | tf_op jit(solution)/shard_map/ppermute | solution.py:71
  1171.5 15.8 collective-permute-done.108
  1188.2 16.3 %collective-permute-done.116 = bf16[1,2,160,1280]{3,2,1,0:T(8,128)(2,1)S(1)} collective-permute-done((bf16[1,2,160,1280]{3,2,1,0:T(8,128)(2,1)S(1)}, bf16[1,2,160,1280]{3,2,1,0:T(8,128)(2,1)S(1)}, u32[]{:S(2)}, u32[]{:S(2)}) %collective-permute-start.116) | collective-permute-done | bytes 819232 | tf_op jit(solution)/shard_map/ppermute | solution.py:67
  1205.4 46.7 %collective-permute-done.101 = bf16[1,160,1280]{2,1,0:T(8,128)(2,1)S(1)} collective-permute-done((bf16[1,160,1280]{2,1,0:T(8,128)(2,1)S(1)}, bf16[1,160,1280]{2,1,0:T(8,128)(2,1)S(1)}, u32[]{:S(2)}, u32[]{:S(2)}) %collective-permute-start.101) | collective-permute-done | bytes 409632 | tf_op jit(solution)/shard_map/ppermute | solution.py:67
  1277.4 16.6 %collective-permute-done.99 = bf16[1,320,1280]{2,1,0:T(8,128)(2,1)S(1)} collective-permute-done((bf16[1,320,1280]{2,1,0:T(8,128)(2,1)S(1)}, bf16[1,320,1280]{2,1,0:T(8,128)(2,1)S(1)}, u32[]{:S(2)}, u32[]{:S(2)}) %collective-permute-start.99) | collective-permute-done | bytes 819232 | tf_op jit(solution)/shard_map/ppermute | solution.py:67
  1347.3 21.6 %collective-permute-done.90 = bf16[1,2,320,1280]{3,2,1,0:T(8,128)(2,1)S(1)} collective-permute-done((bf16[1,2,320,1280]{3,2,1,0:T(8,128)(2,1)S(1)}, bf16[1,2,320,1280]{3,2,1,0:T(8,128)(2,1)S(1)}, u32[]{:S(2)}, u32[]{:S(2)}) %collective-permute-start.90) | collective-permute-done | bytes 1638432 | tf_op jit(solution)/shard_map/ppermute | solution.py:67
  1378.1 17.6 %collective-permute-done.93 = bf16[1,160,1280]{2,1,0:T(8,128)(2,1)S(1)} collective-permute-done((bf16[1,160,1280]{2,1,0:T(8,128)(2,1)S(1)}, bf16[1,160,1280]{2,1,0:T(8,128)(2,1)S(1)}, u32[]{:S(2)}, u32[]{:S(2)}) %collective-permute-start.93) | collective-permute-done | bytes 409632 | tf_op jit(solution)/shard_map/ppermute | solution.py:67
  1400.4 16.3 %collective-permute-done.119 = bf16[120,1280]{1,0:T(8,128)(2,1)S(1)} collective-permute-done((bf16[120,1280]{1,0:T(8,128)(2,1)S(1)}, bf16[120,1280]{1,0:T(8,128)(2,1)S(1)}, u32[]{:S(2)}, u32[]{:S(2)}) %collective-permute-start.119) | collective-permute-done | bytes 307232 | tf_op jit(solution)/shard_map/ppermute | solution.py:71
  1420.2 16.2 %collective-permute-done.95 = bf16[120,1280]{1,0:T(8,128)(2,1)S(1)} collective-permute-done((bf16[120,1280]{1,0:T(8,128)(2,1)S(1)}, bf16[120,1280]{1,0:T(8,128)(2,1)S(1)}, u32[]{:S(2)}, u32[]{:S(2)}) %collective-permute-start.95) | collective-permute-done | bytes 307232 | tf_op jit(solution)/shard_map/ppermute | solution.py:71
  1464.5 18.5 %collective-permute-done.122 = bf16[120,1280]{1,0:T(8,128)(2,1)S(1)} collective-permute-done((bf16[120,1280]{1,0:T(8,128)(2,1)S(1)}, bf16[120,1280]{1,0:T(8,128)(2,1)S(1)}, u32[]{:S(2)}, u32[]{:S(2)}) %collective-permute-start.122) | collective-permute-done | bytes 307232 | tf_op jit(solution)/shard_map/ppermute | solution.py:71
  1522.3 37.6 %shard_map.273 = f32[10,128,128]{2,1,0:T(8,128)S(1)} custom-call(f32[10,128,128]{2,1,0:T(8,128)S(1)} %fusion.237.gram_ref, f32[10,128,128]{2,1,0:T(8,128)S(1)} %bitcast.636), custom_call_target="tpu_custom_call" | custom-call | tf_op jit(solution)/shard_map/pallas_call | solution.py:384
  (965 shorter events, 1042.2 us)
Async XLA Ops:
  3.5 210.1 %collective-permute-start.9 = (bf16[1576,320]{0,1:T(8,128)(2,1)}, bf16[1576,320]{0,1:T(8,128)(2,1)}, u32[]{:S(2)}, u32[]{:S(2)}) collective-permute-start(bf16[1576,320]{0,1:T(8,128)(2,1)} %convert_element_type.792), channel_id=1, source_target_pairs={{0,2},{2,0},{1,3},{3,1},{4,6},{6,4},{5,7},{7,5},{8,10},{10,8},{9,1... | collective-permute-start | bytes 3025928 | tf_op jit(solution)/shard_map/ppermute | solution.py:67
  6.5 170.3 %collective-permute-start = (bf16[1576,320]{0,1:T(8,128)(2,1)}, bf16[1576,320]{0,1:T(8,128)(2,1)}, u32[]{:S(2)}, u32[]{:S(2)}) collective-permute-start(bf16[1576,320]{0,1:T(8,128)(2,1)} %convert_element_type.792), channel_id=1, source_target_pairs={{0,1},{1,0},{2,3},{3,2},{4,5},{5,4},{6,7},{7,6},{8,9},{9,8},{10,11... | collective-permute-start | bytes 3025928 | tf_op jit(solution)/shard_map/ppermute | solution.py:67
  213.6 63.2 %collective-permute-start.1 = (bf16[4,1,192,640]{3,2,1,0:T(8,128)(2,1)S(1)}, bf16[4,1,192,640]{3,2,1,0:T(8,128)(2,1)S(1)}, u32[]{:S(2)}, u32[]{:S(2)}) collective-permute-start(bf16[4,1,192,640]{3,2,1,0:T(8,128)(2,1)S(1)} %bitcast.728), channel_id=1, source_target_pairs={{0,4},{4,0},{1,5},{5,1},{2,6},{6,2},{3,7},{7,3},{8,12},{12,8},{9,1... | collective-permute-start | bytes 2949128 | tf_op jit(solution)/shard_map/ppermute | solution.py:67
  224.8 98.0 %collective-permute-start.59 = (bf16[1,2,320,1280]{3,2,1,0:T(8,128)(2,1)S(1)}, bf16[1,2,320,1280]{3,2,1,0:T(8,128)(2,1)S(1)}, u32[]{:S(2)}, u32[]{:S(2)}) collective-permute-start(bf16[1,2,320,1280]{3,2,1,0:T(8,128)(2,1)S(1)} %pad_maximum_fusion.8), channel_id=1, source_target_pairs={{0,1},{1,0},{2,3},{3,2},{4,5},{5,4},{6,7},{7,6},{8,9},{9,8},{10,11... | collective-permute-start | bytes 4915208 | tf_op jit(solution)/shard_map/ppermute | solution.py:67
  307.1 247.8 %collective-permute-start.63 = (bf16[1,2,160,1280]{3,2,1,0:T(8,128)(2,1)}, bf16[1,2,160,1280]{3,2,1,0:T(8,128)(2,1)}, u32[]{:S(2)}, u32[]{:S(2)}) collective-permute-start(bf16[1,2,160,1280]{3,2,1,0:T(8,128)(2,1)} %pad_maximum_fusion.17), channel_id=1, source_target_pairs={{0,1},{1,0},{2,3},{3,2},{4,5},{5,4},{6,7},{7,6},{8,9},{9,8},{10,11... | collective-permute-start | bytes 2457608 | tf_op jit(solution)/shard_map/ppermute | solution.py:67
  322.8 67.2 %collective-permute-start.26 = (bf16[1,2,320,1280]{3,2,1,0:T(8,128)(2,1)S(1)}, bf16[1,2,320,1280]{3,2,1,0:T(8,128)(2,1)S(1)}, u32[]{:S(2)}, u32[]{:S(2)}) collective-permute-start(bf16[1,2,320,1280]{3,2,1,0:T(8,128)(2,1)S(1)} %pad_maximum_fusion.5), channel_id=1, source_target_pairs={{0,1},{1,0},{2,3},{3,2},{4,5},{5,4},{6,7},{7,6},{8,9},{9,8},{10,11... | collective-permute-start | bytes 4915208 | tf_op jit(solution)/shard_map/ppermute | solution.py:67
  324.9 93.9 %collective-permute-start.27 = (bf16[1,2,320,1280]{3,2,1,0:T(8,128)(2,1)S(1)}, bf16[1,2,320,1280]{3,2,1,0:T(8,128)(2,1)S(1)}, u32[]{:S(2)}, u32[]{:S(2)}) collective-permute-start(bf16[1,2,320,1280]{3,2,1,0:T(8,128)(2,1)S(1)} %pad_maximum_fusion.5), channel_id=1, source_target_pairs={{0,2},{2,0},{1,3},{3,1},{4,6},{6,4},{5,7},{7,5},{8,10},{10,8},{9,1... | collective-permute-start | bytes 4915208 | tf_op jit(solution)/shard_map/ppermute | solution.py:67
  348.7 75.9 %collective-permute-start.48 = (bf16[1,2,320,1280]{3,2,1,0:T(8,128)(2,1)S(1)}, bf16[1,2,320,1280]{3,2,1,0:T(8,128)(2,1)S(1)}, u32[]{:S(2)}, u32[]{:S(2)}) collective-permute-start(bf16[1,2,320,1280]{3,2,1,0:T(8,128)(2,1)S(1)} %pad_maximum_fusion.7), channel_id=1, source_target_pairs={{0,1},{1,0},{2,3},{3,2},{4,5},{5,4},{6,7},{7,6},{8,9},{9,8},{10,11... | collective-permute-start | bytes 4915208 | tf_op jit(solution)/shard_map/ppermute | solution.py:67
  383.8 66.9 %collective-permute-start.49 = (bf16[1,2,320,1280]{3,2,1,0:T(8,128)(2,1)S(1)}, bf16[1,2,320,1280]{3,2,1,0:T(8,128)(2,1)S(1)}, u32[]{:S(2)}, u32[]{:S(2)}) collective-permute-start(bf16[1,2,320,1280]{3,2,1,0:T(8,128)(2,1)S(1)} %pad_maximum_fusion.7), channel_id=1, source_target_pairs={{0,2},{2,0},{1,3},{3,1},{4,6},{6,4},{5,7},{7,5},{8,10},{10,8},{9,1... | collective-permute-start | bytes 4915208 | tf_op jit(solution)/shard_map/ppermute | solution.py:67
  390.0 62.7 %collective-permute-start.16 = (bf16[192,640]{1,0:T(8,128)(2,1)S(1)}, bf16[192,640]{1,0:T(8,128)(2,1)S(1)}, u32[]{:S(2)}, u32[]{:S(2)}) collective-permute-start(bf16[192,640]{1,0:T(8,128)(2,1)S(1)} %get-tuple-element.206), channel_id=1, source_target_pairs={{0,8},{8,16},{16,24},{24,0},{1,9},{9,17},{17,25},{25,1},{2,10},{10... | collective-permute-start | bytes 737288 | tf_op jit(solution)/shard_map/ppermute | solution.py:71
  464.7 90.2 %collective-permute-start.64 = (bf16[1,2,160,1280]{3,2,1,0:T(8,128)(2,1)}, bf16[1,2,160,1280]{3,2,1,0:T(8,128)(2,1)}, u32[]{:S(2)}, u32[]{:S(2)}) collective-permute-start(bf16[1,2,160,1280]{3,2,1,0:T(8,128)(2,1)} %pad_maximum_fusion.17), channel_id=1, source_target_pairs={{0,4},{4,0},{1,5},{5,1},{2,6},{6,2},{3,7},{7,3},{8,12},{12,8},{9,1... | collective-permute-start | bytes 2457608 | tf_op jit(solution)/shard_map/ppermute | solution.py:67
  502.1 89.7 %collective-permute-start.41 = (bf16[1,2,160,1280]{3,2,1,0:T(8,128)(2,1)}, bf16[1,2,160,1280]{3,2,1,0:T(8,128)(2,1)}, u32[]{:S(2)}, u32[]{:S(2)}) collective-permute-start(bf16[1,2,160,1280]{3,2,1,0:T(8,128)(2,1)} %pad_maximum_fusion.15), channel_id=1, source_target_pairs={{0,1},{1,0},{2,3},{3,2},{4,5},{5,4},{6,7},{7,6},{8,9},{9,8},{10,11... | collective-permute-start | bytes 2457608 | tf_op jit(solution)/shard_map/ppermute | solution.py:67
  532.7 71.9 %all-to-all-start = ((bf16[384,3,4,320]{0,3,1,2:T(8,128)(2,1)}), bf16[384,3,4,320]{0,3,1,2:T(8,128)(2,1)}, u32[]{:S(2)}, u32[]{:S(2)}) async-start(bf16[384,3,4,320]{0,3,1,2:T(8,128)(2,1)} %copy.213), calls=%async_computation | async-start | bytes 5898240 | tf_op jit(solution)/shard_map/all_to_all | solution.py:510
  770.7 231.8 %collective-permute-start.125 = (bf16[1576,320]{0,1:T(8,128)(2,1)}, bf16[1576,320]{0,1:T(8,128)(2,1)}, u32[]{:S(2)}, u32[]{:S(2)}) collective-permute-start(bf16[1576,320]{0,1:T(8,128)(2,1)} %convolution_convert_fusion.1), channel_id=1, source_target_pairs={{0,1},{1,0},{2,3},{3,2},{4,5},{5,4},{6,7},{7,6},{8,9},{9,8},{10,11... | collective-permute-start | bytes 3025928 | tf_op jit(solution)/shard_map/ppermute | solution.py:67
  848.1 78.1 %collective-permute-start.84 = (f32[12802]{0:T(1024)S(1)}, f32[12802]{0:T(1024)S(1)}, u32[]{:S(2)}, u32[]{:S(2)}) collective-permute-start(f32[12802]{0:T(1024)S(1)} %concatenate.135), channel_id=1, source_target_pairs={{0,1},{1,0},{2,3},{3,2},{4,5},{5,4},{6,7},{7,6},{8,9},{9,8},{10,11... | collective-permute-start | bytes 153632 | tf_op jit(solution)/shard_map/ppermute | solution.py:67
  858.9 252.4 %collective-permute-start.97 = (bf16[1,2,2,480,1280]{4,3,2,1,0:T(8,128)(2,1)}, bf16[1,2,2,480,1280]{4,3,2,1,0:T(8,128)(2,1)}, u32[]{:S(2)}, u32[]{:S(2)}) collective-permute-start(bf16[1,2,2,480,1280]{4,3,2,1,0:T(8,128)(2,1)} %dynamic-slice_bitcast_fusion.2), channel_id=1, source_target_pairs={{0,1},{1,0},{2,3},{3,2},{4,5},{5,4},{6,7},{7,6},{8,9},{9,8},{10,11... | collective-permute-start | bytes 14745608 | tf_op jit(solution)/shard_map/ppermute | solution.py:67
  958.7 165.1 %collective-permute-start.105 = (bf16[1,2,2,480,1280]{4,3,2,1,0:T(8,128)(2,1)}, bf16[1,2,2,480,1280]{4,3,2,1,0:T(8,128)(2,1)}, u32[]{:S(2)}, u32[]{:S(2)}) collective-permute-start(bf16[1,2,2,480,1280]{4,3,2,1,0:T(8,128)(2,1)} %dynamic-slice_bitcast_fusion.1), channel_id=1, source_target_pairs={{0,1},{1,0},{2,3},{3,2},{4,5},{5,4},{6,7},{7,6},{8,9},{9,8},{10,11... | collective-permute-start | bytes 14745608 | tf_op jit(solution)/shard_map/ppermute | solution.py:67
  992.9 135.2 %collective-permute-start.113 = (bf16[1,2,2,480,1280]{4,3,2,1,0:T(8,128)(2,1)}, bf16[1,2,2,480,1280]{4,3,2,1,0:T(8,128)(2,1)}, u32[]{:S(2)}, u32[]{:S(2)}) collective-permute-start(bf16[1,2,2,480,1280]{4,3,2,1,0:T(8,128)(2,1)} %dynamic-slice_bitcast_fusion), channel_id=1, source_target_pairs={{0,1},{1,0},{2,3},{3,2},{4,5},{5,4},{6,7},{7,6},{8,9},{9,8},{10,11... | collective-permute-start | bytes 14745608 | tf_op jit(solution)/shard_map/ppermute | solution.py:67
  1101.6 224.0 %collective-permute-start.89 = (bf16[1,2,2,480,1280]{4,3,2,1,0:T(8,128)(2,1)}, bf16[1,2,2,480,1280]{4,3,2,1,0:T(8,128)(2,1)}, u32[]{:S(2)}, u32[]{:S(2)}) collective-permute-start(bf16[1,2,2,480,1280]{4,3,2,1,0:T(8,128)(2,1)} %dynamic-slice_bitcast_fusion.3), channel_id=1, source_target_pairs={{0,1},{1,0},{2,3},{3,2},{4,5},{5,4},{6,7},{7,6},{8,9},{9,8},{10,11... | collective-permute-start | bytes 14745608 | tf_op jit(solution)/shard_map/ppermute | solution.py:67
  1135.4 136.8 %collective-permute-start.98 = (bf16[1,2,320,1280]{3,2,1,0:T(8,128)(2,1)S(1)}, bf16[1,2,320,1280]{3,2,1,0:T(8,128)(2,1)S(1)}, u32[]{:S(2)}, u32[]{:S(2)}) collective-permute-start(bf16[1,2,320,1280]{3,2,1,0:T(8,128)(2,1)S(1)} %dynamic-slice_bitcast_fusion.6), channel_id=1, source_target_pairs={{0,2},{2,0},{1,3},{3,1},{4,6},{6,4},{5,7},{7,5},{8,10},{10,8},{9,1... | collective-permute-start | bytes 4915208 | tf_op jit(solution)/shard_map/ppermute | solution.py:67
  1138.1 136.1 %collective-permute-start.106 = (bf16[1,2,320,1280]{3,2,1,0:T(8,128)(2,1)S(1)}, bf16[1,2,320,1280]{3,2,1,0:T(8,128)(2,1)S(1)}, u32[]{:S(2)}, u32[]{:S(2)}) collective-permute-start(bf16[1,2,320,1280]{3,2,1,0:T(8,128)(2,1)S(1)} %dynamic-slice_bitcast_fusion.5), channel_id=1, source_target_pairs={{0,2},{2,0},{1,3},{3,1},{4,6},{6,4},{5,7},{7,5},{8,10},{10,8},{9,1... | collective-permute-start | bytes 4915208 | tf_op jit(solution)/shard_map/ppermute | solution.py:67
  1187.4 88.0 %collective-permute-start.114 = (bf16[1,2,320,1280]{3,2,1,0:T(8,128)(2,1)S(1)}, bf16[1,2,320,1280]{3,2,1,0:T(8,128)(2,1)S(1)}, u32[]{:S(2)}, u32[]{:S(2)}) collective-permute-start(bf16[1,2,320,1280]{3,2,1,0:T(8,128)(2,1)S(1)} %dynamic-slice_bitcast_fusion.4), channel_id=1, source_target_pairs={{0,2},{2,0},{1,3},{3,1},{4,6},{6,4},{5,7},{7,5},{8,10},{10,8},{9,1... | collective-permute-start | bytes 4915208 | tf_op jit(solution)/shard_map/ppermute | solution.py:67
  1332.4 110.7 %collective-permute-start.124 = (bf16[1576,320]{0,1:T(8,128)(2,1)S(1)}, bf16[1576,320]{0,1:T(8,128)(2,1)S(1)}, u32[]{:S(2)}, u32[]{:S(2)}) collective-permute-start(bf16[1576,320]{0,1:T(8,128)(2,1)S(1)} %copy-done.125), channel_id=1, source_target_pairs={{0,1},{1,0},{2,3},{3,2},{4,5},{5,4},{6,7},{7,6},{8,9},{9,8},{10,11... | collective-permute-start | bytes 3025928 | tf_op jit(solution)/shard_map/ppermute | solution.py:67
  1332.5 110.6 %collective-permute-start.126 = (bf16[1576,320]{0,1:T(8,128)(2,1)S(1)}, bf16[1576,320]{0,1:T(8,128)(2,1)S(1)}, u32[]{:S(2)}, u32[]{:S(2)}) collective-permute-start(bf16[1576,320]{0,1:T(8,128)(2,1)S(1)} %copy-done.126), channel_id=1, source_target_pairs={{0,2},{2,0},{1,3},{3,1},{4,6},{6,4},{5,7},{7,5},{8,10},{10,8},{9,1... | collective-permute-start | bytes 3025928 | tf_op jit(solution)/shard_map/ppermute | solution.py:67
  (269 other events, 7531.1 us)

commit v2 on v1

--- a/solution.py
+++ b/solution.py
@@ -24,9 +24,11 @@
 MASKED = -1e30
 HIGHEST = lax.Precision.HIGHEST
 LANES_BOTH = (((1,), (1,)), ((), ()))
-VOCAB = ("z", "w", "x")
+PLANE = ("za", "zb")
+VOCAB = PLANE + ("w", "x")
 SEQ = ("y", "core")
 ALL = VOCAB + SEQ
+OWNERS = ("w", "x", "y", "core")
 PLANES = 4
 
 
@@ -68,7 +70,22 @@
 
 
 def shift(tensor, step):
-    return lax.ppermute(tensor, "z", [(i, (i + step) % PLANES) for i in range(PLANES)])
+    step %= PLANES
+    if step == 0:
+        return tensor
+    return lax.ppermute(tensor, PLANE, [(i, (i + step) % PLANES) for i in range(PLANES)])
+
+
+def planes_from_here():
+    return [(lax.axis_index(PLANE) + step) % PLANES for step in range(PLANES)]
+
+
+def gathered_z(tensor):
+    return [shift(tensor, -step) for step in range(PLANES)]
+
+
+def sent_z(terms):
+    return [shift(terms[step], step) for step in range(PLANES)]
 
 
 def pick(tensor, place, axis=0):
@@ -92,113 +109,92 @@
     )
 
 
-def split_rows(rows):
-    return rows * 2 // 3
-
-
-def exchange_planes(stacked):
-    here = lax.axis_index("z")
-    got = [pick(stacked, here)]
-    for step in (3, 2, 1):
-        got.append(shift(pick(stacked, (here + step) % PLANES), step))
-    doubled = jnp.concatenate([part[None] for part in got + got[:3]], 0)
-    return lax.dynamic_slice_in_dim(doubled, (PLANES - here) % PLANES, PLANES, 0)
-
-
-def gather_pieces(piece):
-    here = lax.axis_index("z")
-    got = [piece] + [shift(piece, step) for step in (3, 2, 1)]
-    doubled = jnp.concatenate([part[None] for part in got + got[:3]], 0)
-    return lax.dynamic_slice_in_dim(doubled, (PLANES - here) % PLANES, PLANES, 0)
-
-
-def gather_weights(layer_weight):
-    rows, model_dim = layer_weight.shape
-    quarter = rows // PLANES
-    low = layer_weight.astype(jnp.bfloat16).reshape(PLANES, quarter, model_dim)
-    held = exchange_planes(low)
-    ways = lax.axis_size("w")
+class Order:
+    def __init__(self):
+        self.marks = []
+
+    def hold(self, tensors, *earlier):
+        marks = [lax.slice(t, (0,) * t.ndim, (1,) * t.ndim).reshape(()) for t in earlier]
+        tensors, *marks = lax.optimization_barrier((tensors, *marks))
+        self.marks += [mark.astype(jnp.float32) for mark in marks]
+        return tensors
+
+    def zero(self):
+        return sum(0.0 * mark for mark in self.marks)
+
+
+def flip(tensor, by_core):
+    pairs = []
+    for place in range(8):
+        pairs.append((place, place ^ (4 if by_core[place % 2] == "x" else 2)))
+    return lax.ppermute(tensor, ("x", "y", "core"), pairs)
+
+
+def reduce_plane(grads):
+    return lax.psum_scatter(grads, OWNERS + PLANE, scatter_dimension=0, tiled=True)
+
+
+def scatter_core(grads):
+    model_dim = grads.shape[1]
+    at_c = lax.axis_index("core")
+    shaped = grads.reshape(lax.axis_size("w"), 2, 2, 2, -1, model_dim)
+    return lowered(pick(shaped, at_c, 3), swap(pick(shaped, 1 - at_c, 3), "core"))
+
+
+def scatter_first(shaped):
     at_x, at_y, at_c = (lax.axis_index(name) for name in ("x", "y", "core"))
-    cut = split_rows(rows)
-    planes = []
-    for place in range(PLANES):
-        mine = gather_pieces(held[place]).reshape(1, rows, model_dim)
-        if ways > 1:
-            mine = lax.all_gather(mine, "w", axis=0, tiled=True)
-        whole = jnp.zeros((ways, 8, rows, model_dim), jnp.bfloat16)
-        for offset, length, first, second in ((0, cut, "x", "y"), (cut, rows - cut, "y", "x")):
-            part = mine[:, None, offset : offset + length]
-            near = jnp.concatenate([part, swap(part, first)], 1)
-            far = swap(near, second)
-            for other, pair in ((0, near), (1, far)):
-                for turned, both in ((0, pair), (1, swap(pair, "core"))):
-                    for spot in (0, 1):
-                        by_x, by_y = (spot, other) if first == "x" else (other, spot)
-                        owner = (at_x ^ by_x) * 4 + (at_y ^ by_y) * 2 + (at_c ^ turned)
-                        whole = lax.dynamic_update_slice(
-                            whole, both[:, spot : spot + 1], (0, owner, offset, 0)
-                        )
-        planes.append(whole.reshape(-1, model_dim))
-    return planes
-
-
-def scatter_plane(grads):
-    model_dim = grads.shape[1]
-    ways = lax.axis_size("w")
-    at_x, at_y, at_c, here = (lax.axis_index(name) for name in ("x", "y", "core", "z"))
-    shaped = grads.reshape(ways, 2, 2, 2, -1, model_dim)
-    rows = shaped.shape[4]
-    cut = split_rows(rows)
-    shaped = lowered(pick(shaped, at_c, 3), swap(pick(shaped, 1 - at_c, 3), "core"))
-    parts = []
-    for offset, length, first, second in ((0, cut, "y", "x"), (cut, rows - cut, "x", "y")):
-        part = shaped[:, :, :, offset : offset + length]
-        spot = {"x": at_x, "y": at_y}
-        axis = 2 if first == "y" else 1
-        part = lowered(
-            pick(part, spot[first], axis), swap(pick(part, 1 - spot[first], axis), first)
-        )
-        part = lowered(pick(part, spot[second], 1), swap(pick(part, 1 - spot[second], 1), second))
-        parts.append(part)
-    own = jnp.concatenate(parts, 1)
-    if ways > 1:
+    ways, unused, unused, rows, model_dim = shaped.shape
+    shaped = shaped.reshape(ways, 4, rows, model_dim)
+
+    def half(x, y):
+        spots = (jnp.where(at_c == 0, y, 2 * x), jnp.where(at_c == 0, 2 + y, 2 * x + 1))
+        return jnp.stack([pick(shaped, spot, 1) for spot in spots], 1)
+
+    return lowered(half(at_x, at_y), flip(half(1 - at_x, 1 - at_y), "yx"))
+
+
+def scatter_second(pair):
+    spot = jnp.where(lax.axis_index("core") == 0, lax.axis_index("x"), lax.axis_index("y"))
+    own = lowered(pick(pair, spot, 1), flip(pick(pair, 1 - spot, 1), "xy"))
+    if lax.axis_size("w") > 1:
         own = lax.psum_scatter(own, "w", scatter_dimension=0, tiled=True)
+    return own[0]
+
+
+def scatter_last(own):
+    rows, model_dim = own.shape
     quarters = own.reshape(PLANES, rows // PLANES, model_dim)
-    got = [shift(pick(quarters, (here + step) % PLANES), step) for step in (1, 2, 3)]
-    return lowered(pick(quarters, here), *got)
-
-
-def to_groups(theirs, mine):
-    here = lax.axis_index("z")
+    return lowered(*sent_z([pick(quarters, plane) for plane in planes_from_here()]))
+
+
+def own_first(tensor, place, axis):
+    return jnp.stack([pick(tensor, place, axis), pick(tensor, 1 - place, axis)])
+
+
+def to_group(theirs, mine):
     both = lowered(mine, swap(theirs, "x"))
     if lax.axis_size("w") > 1:
         both = lax.psum_scatter(both, "w", scatter_dimension=1, tiled=False)
     else:
         both = both[:, 0]
-    got = [shift(pick(both, (here + step) % PLANES), step) for step in (1, 2, 3)]
-    return added(pick(both, here), *got)
-
-
-def from_groups(tensor):
-    here, at_x = lax.axis_index("z"), lax.axis_index("x")
+    return added(both[0], swap(both[1], "za"))
+
+
+def from_groups(tensor, order=None, *earlier):
     if lax.axis_size("w") > 1:
         tensor = lax.all_gather(tensor, "w", axis=0, tiled=False)
     else:
         tensor = tensor[None]
-    found = [(tensor, here, at_x)]
-    for step in (1, 3, 2):
-        found.append((shift(tensor, step), (here - step) % PLANES, at_x))
-    return found + [(swap(got, "x"), from_z, 1 - at_x) for got, from_z, _ in found]
+    both = [tensor, swap(tensor, "za")]
+    if order is not None:
+        both[1] = order.hold(both[1], *earlier)
+    return jnp.stack(both + [swap(part, "x") for part in both]).reshape((2, 2) + tensor.shape)
 
 
 def total_of(values):
-    for axis in ("core", "y", "x"):
-        values = values + swap(values, axis)
-    for step in (1, 2):
-        values = values + lax.ppermute(values, "z", [(i, i ^ step) for i in range(PLANES)])
-    if lax.axis_size("w") > 1:
-        values = lax.psum(values, "w")
-    return values
+    for name in ("core", "y", "x", "zb", "za"):
+        values = values + swap(values, name)
+    return lax.psum(values, "w") if lax.axis_size("w") > 1 else values
 
 
 def _groups(width):
@@ -398,28 +394,74 @@
     return (weight - step_rate * (direction + WEIGHT_DECAY * weight), first_mom, second)
 
 
+def rotated_kernel(
+    place_ref,
+    factor_ref,
+    weight_ref,
+    first_ref,
+    second_ref,
+    grad_ref,
+    stat_ref,
+    basis_ref,
+    weight_out,
+    first_out,
+    second_out,
+    stat_out,
+    gram_ref,
+    span_ref,
+):
+    def product(left, right, dims):
+        return lax.dot_general(
+            left, right, (dims, ((), ())), precision=HIGHEST, preferred_element_type=jnp.float32
+        )
+
+    basis = basis_ref[0, 0]
+    gradient = jnp.concatenate(
+        [grad_ref[(place_ref[0] + PLANES - piece) % PLANES] for piece in range(PLANES)], 0
+    )
+    gradient = gradient.astype(jnp.float32) * factor_ref[0, 0]
+    turned = product(gradient, basis, ((1,), (0,)))
+    first_mom = BETA_ONE * first_ref[...] + (1.0 - BETA_ONE) * turned
+    second = BETA_TWO * second_ref[...] + (1.0 - BETA_TWO) * turned * turned
+    direction = (
+        first_mom / (1.0 - BETA_ONE**STEP) / (jnp.sqrt(second / (1.0 - BETA_TWO**STEP)) + ADAM_EPS)
+    )
+    back = product(direction, basis, ((1,), (1,)))
+    weight = weight_ref[...]
+    weight_out[...] = weight - RATE_LAYER * (back + WEIGHT_DECAY * weight)
+    first_out[...] = first_mom
+    second_out[...] = second
+    stat_next = BETA_STAT * stat_ref[0, 0] + (1.0 - BETA_STAT) * product(
+        gradient, gradient, ((0,), (0,))
+    )
+    stat_out[0, 0] = stat_next
+    spanned = product(stat_next, basis, ((1,), (0,)))
+    turned_span = spanned.T
+    span_ref[0] = turned_span
+    gram_ref[0] = product(turned_span, spanned, ((1,), (0,)))
+
+
 def rotated_update(weight, first_mom, second, gradient, factor, stat, basis):
     blocks, block_len = basis.shape[1], basis.shape[2]
-    shaped = gradient.reshape(-1, blocks, block_len)
-    frames, stats = basis[0], stat[0]
-    turned = factor * jnp.einsum("rbi,bij->rbj", shaped, frames, precision=HIGHEST).reshape(
-        gradient.shape
-    )
-    outer = jnp.einsum("rbi,rbj->bij", shaped, shaped, precision=HIGHEST)
-    first_mom = BETA_ONE * first_mom + (1.0 - BETA_ONE) * turned
-    second = BETA_TWO * second + (1.0 - BETA_TWO) * turned * turned
-    direction = (
-        first_mom / (1.0 - BETA_ONE**STEP) / (jnp.sqrt(second / (1.0 - BETA_TWO**STEP)) + ADAM_EPS)
-    )
-    back = jnp.einsum(
-        "rbj,bij->rbi", direction.reshape(shaped.shape), frames, precision=HIGHEST
-    ).reshape(weight.shape)
-    weight_next = weight - RATE_LAYER * (back + WEIGHT_DECAY * weight)
-    stat_next = BETA_STAT * stats + (1.0 - BETA_STAT) * (factor * factor) * outer
-    spanned = jnp.einsum("bij,bjk->bik", stat_next, frames, precision=HIGHEST)
-    gram = jnp.einsum("bij,bik->bjk", spanned, spanned, precision=HIGHEST)
-    solved = frame(gram, jnp.swapaxes(spanned, 1, 2))
-    return (weight_next, first_mom, second, jnp.swapaxes(solved, 1, 2)[None], stat_next[None])
+    rows = weight.shape[0]
+    column = pl.BlockSpec((rows, block_len), lambda b: (0, b))
+    square = pl.BlockSpec((1, 1, block_len, block_len), lambda b: (0, b, 0, 0))
+    flat = pl.BlockSpec((1, block_len, block_len), lambda b: (b, 0, 0))
+    wide = jax.ShapeDtypeStruct(weight.shape, jnp.float32)
+    small = jax.ShapeDtypeStruct((blocks, block_len, block_len), jnp.float32)
+    weight_next, first_next, second_next, stat_next, gram, span = pl.pallas_call(
+        rotated_kernel,
+        grid=(blocks,),
+        in_specs=[pl.BlockSpec(memory_space=pltpu.SMEM)] * 2
+        + [column] * 3
+        + [pl.BlockSpec((PLANES, rows // PLANES, block_len), lambda b: (0, 0, b))]
+        + [square] * 2,
+        out_specs=[column] * 3 + [square] + [flat] * 2,
+        out_shape=[wide] * 3 + [jax.ShapeDtypeStruct(stat.shape, jnp.float32)] + [small] * 2,
+        compiler_params=pltpu.CompilerParams(vmem_limit_bytes=40 << 20),
+    )(lax.axis_index(PLANE).reshape(1), factor.reshape(1, 1), weight, first_mom, second, gradient, stat, basis)
+    solved = frame(gram, span)
+    return (weight_next, first_next, second_next, jnp.swapaxes(solved, 1, 2)[None], stat_next)
 
 
 def body(
@@ -467,34 +509,50 @@
         shift_final,
     ) = pieces(small_params, model_dim, hidden_units)
 
+    at_a, at_b = lax.axis_index("za"), lax.axis_index("zb")
+    order = Order()
+    weight_low = layer_weight.astype(jnp.bfloat16)
+    gathered = lax.all_gather(weight_low, ALL, axis=0, tiled=True)
     table_low = embed_table.astype(jnp.bfloat16)
-    table_y = swap(table_low, "y")
-    table_near = in_order(at_c, table_low, swap(table_low, "core"), 1)
-    planes = gather_weights(layer_weight)
-    table_far = in_order(at_c, table_y, swap(table_y, "core"), 1)
+    other_low = swap(table_low, "zb")
+    far_low = swap(table_low, "y")
+    pair = in_order(at_b, table_low, other_low, 0)
+    table_near = in_order(at_c, pair, swap(pair, "core"), 1)
+
+    pair_rows = 2 * vocab_rows
+    pair_range = jnp.arange(pair_rows, dtype=jnp.int32)
+    plane_step = 2 * ways * vocab_rows
+    first_start = (group_id - at_b * 2 * ways) * vocab_rows
+
+    def in_pair(ids):
+        one, two = ids - first_start, ids - first_start - plane_step
+        inside = (one >= 0) & (one < vocab_rows)
+        both = (two >= 0) & (two < vocab_rows)
+        return jnp.where(inside, one, jnp.where(both, two + vocab_rows, -1))
+
+    def of_this_b(tensor):
+        shaped = pick(tensor.reshape(2, 2, ways, 2, -1, tensor.shape[-1]), at_b, 1)
+        return own_first(own_first(shaped, at_a, 0), at_x, 2)
+
+    own_ids = of_this_b(token_ids)
+    near_ids = in_order(at_c, own_ids, swap(own_ids, "core"), 4)
+    all_ids = in_order(at_y, near_ids, swap(near_ids, "y"), 4).swapaxes(3, 4)
+
+    def looked_up(ids, rows_of):
+        hot = (in_pair(ids).reshape(-1, 1) == pair_range[None, :]).astype(jnp.bfloat16)
+        got = plain_dot(hot, rows_of).astype(jnp.bfloat16)
+        return got.reshape(2, ways, tok_rows, -1)
+
+    near = [looked_up(own_ids[at], table_near) for at in (1, 0)]
+    far_low = order.hold(far_low, near[0])
+    far_other = order.hold(swap(other_low, "y"), near[1])
+    pair = in_order(at_b, far_low, far_other, 0)
+    table_far = in_order(at_c, pair, swap(pair, "core"), 1)
+    far = [looked_up(own_ids[at], table_far) for at in (1, 0)]
+    half_near = to_group(*near)
+    half_far = to_group(*far)
+    embedded = in_order(at_y, half_near, half_far, 1)
     table_full = in_order(at_y, table_near, table_far, 1)
-
-    local_ids = (token_ids[:, 0] - group_id * vocab_rows).reshape(PLANES, ways, 2, tok_rows)
-    row_range = jnp.arange(vocab_rows, dtype=jnp.int32)
-
-    def looked_up(ids, rows_of):
-        hot = (ids.reshape(-1)[:, None] == row_range[None, :]).astype(jnp.bfloat16)
-        got = plain_dot(hot, rows_of).astype(jnp.bfloat16)
-        return got.reshape(ids.shape + (rows_of.shape[1],))
-
-    halves = []
-    for rows_of in (table_near, table_far):
-        chunks = []
-        for at in range(0, tok_rows, tok_rows // 2):
-            ids = local_ids[..., at : at + tok_rows // 2]
-            chunks.append(
-                to_groups(
-                    looked_up(pick(ids, 1 - at_x, 2), rows_of),
-                    looked_up(pick(ids, at_x, 2), rows_of),
-                )
-            )
-        halves.append(jnp.concatenate(chunks, 0))
-    embedded = in_order(at_y, halves[0], halves[1], 1)
 
     group_lengths = jnp.take(lengths, group_id, axis=0)
     bounds = jnp.cumsum(group_lengths)[:-1]
@@ -504,7 +562,7 @@
     ).astype(jnp.int32)[None]
 
     normed_low = layer_norm(embedded, gain_one, shift_one).astype(jnp.bfloat16)
-    joined = low_dot(normed_low, planes[0]) + jnp.concatenate(
+    joined = low_dot(normed_low, gathered[: 3 * model_dim]) + jnp.concatenate(
         [bias_q, jnp.zeros_like(bias_q), bias_v]
     )
     joined_heads = lax.all_to_all(
@@ -523,24 +581,14 @@
         concat_axis=2,
         tiled=True,
     ).reshape(tok_rows, model_dim)
-    half = planes[1].shape[0] - model_dim
-    rest = hidden_units - half
-    project_out, expand_one = planes[1][:model_dim], planes[1][model_dim:]
-    expand_two, reduce_one = planes[2][:rest], planes[2][rest:]
-    reduce_two = planes[3]
-    reduce_cut = reduce_one.shape[0]
+    project_out = gathered[3 * model_dim : 4 * model_dim]
+    expand_weight = gathered[4 * model_dim : 4 * model_dim + hidden_units]
+    reduce_weight = gathered[4 * model_dim + hidden_units :]
     middle = embedded + low_dot(mixed_low, project_out) + bias_out
     normed_two_low = layer_norm(middle, gain_two, shift_two).astype(jnp.bfloat16)
-    hidden_one = low_dot(normed_two_low, expand_one) + bias_up[:half]
-    hidden_two = low_dot(normed_two_low, expand_two) + bias_up[half:]
-    hidden = jnp.concatenate([hidden_one, hidden_two], 1)
+    hidden = low_dot(normed_two_low, expand_weight) + bias_up
     active_low = smooth(hidden).astype(jnp.bfloat16)
-    residual_out = (
-        middle
-        + plain_dot(active_low[:, :reduce_cut], reduce_one)
-        + plain_dot(active_low[:, reduce_cut:], reduce_two)
-        + bias_down
-    )
+    residual_out = middle + plain_dot(active_low, reduce_weight) + bias_down
     final_out = layer_norm(residual_out, gain_final, shift_final)
     own_pos = lax.dynamic_slice_in_dim(loss_place[:, 0], group_id * loss_rows, loss_rows, 0)
     pos_hot = own_pos[:, None] == jnp.arange(tok_rows, dtype=jnp.int32)[None, :]
@@ -548,37 +596,47 @@
         jnp.bfloat16
     )
 
-    def whole_groups(tensor, kinds):
-        found = from_groups(tensor)
-        gathered = jnp.zeros((PLANES, ways, 2) + tensor.shape, kinds)
-        for got, from_z, from_x in found:
-            gathered = lax.dynamic_update_slice(
-                gathered, got[None, :, None], (from_z, 0, from_x) + (0,) * tensor.ndim
-            )
-        return gathered.reshape((groups,) + tensor.shape)
-
-    head_rows = whole_groups(chosen, jnp.bfloat16).reshape(groups * loss_rows, model_dim)
+    head_rows = from_groups(chosen).reshape(-1, model_dim)
     logits = low_dot(head_rows, table_full)
     if groups * vocab_rows > vocab_live:
-        row_ids = group_id * vocab_rows + row_range
-        logits = jnp.where((row_ids < vocab_live)[None, :], logits, MASKED)
-    target_local = targets[:, 0] - group_id * vocab_rows
-    target_hot = row_range[None, :] == target_local[:, None]
+        live = jnp.minimum(vocab_live - first_start, vocab_rows)
+        live_two = vocab_live - first_start - plane_step
+        kept = jnp.where(pair_range < vocab_rows, pair_range < live, pair_range - vocab_rows < live_two)
+        logits = jnp.where(kept[None, :], logits, MASKED)
+    target_hot = pair_range[None, :] == in_pair(of_this_b(targets)).reshape(-1, 1)
     target_part = jnp.sum(jnp.where(target_hot, logits, 0.0), 1)
     local_peak = jnp.max(logits, 1)
     local_sum = jnp.sum(jnp.exp(logits - local_peak[:, None]), 1)
-    everyone = whole_groups(jnp.stack([local_peak, local_sum, target_part]), jnp.float32)
+    everyone = from_groups(jnp.stack([local_peak, local_sum, target_part]))
+    everyone = everyone.reshape(2, 2, ways, 3, 2, 2, -1)
+    aligned = []
+    for by_x in (0, 1):
+        for by_a in (0, 1):
+            turned = jnp.roll(everyone[by_x, by_a], (by_x, by_a), (2, 3))
+            aligned.append(turned.reshape(ways, 3, -1))
+    everyone = jnp.concatenate(aligned, 0)
     peak_all = jnp.max(everyone[:, 0], 0)
     sum_all = jnp.sum(everyone[:, 1] * jnp.exp(everyone[:, 0] - peak_all[None]), 0)
     target_logit = jnp.sum(everyone[:, 2], 0)
     logsum_all = peak_all + jnp.log(sum_all)
-    weight_rows = loss_flag[:, 0].astype(jnp.float32)
+    weight_rows = of_this_b(loss_flag).reshape(-1).astype(jnp.float32)
     chance = jnp.exp(logits - logsum_all[:, None])
     grad_logits = weight_rows[:, None] * (chance - target_hot.astype(jnp.float32))
     grad_low = grad_logits.astype(jnp.bfloat16)
     grad_rows = plain_dot(grad_low, table_full).astype(jnp.bfloat16)
-    grad_rows = grad_rows.reshape(PLANES, ways, 2, loss_rows, model_dim)
-    grad_chosen = to_groups(pick(grad_rows, 1 - at_x, 2), pick(grad_rows, at_x, 2))
+    grad_rows = grad_rows.reshape(2, 2, ways, loss_rows, model_dim)
+    grad_chosen = to_group(grad_rows[1], grad_rows[0])
+
+    def table_part(by_y, by_c):
+        place = (at_y ^ by_y) * 2 + (at_c ^ by_c)
+        cols = lax.dynamic_slice_in_dim(head_rows, place * slice_width, slice_width, 1)
+        return outer_dot(grad_low, cols).astype(jnp.bfloat16)
+
+    far_sum = lowered(table_part(1, 0), swap(table_part(1, 1), "core"))
+    near_sum = added(table_part(0, 0), swap(table_part(0, 1), "core"))
+    grad_chosen = order.hold(grad_chosen, near_sum, far_sum, all_ids)
+    head_table_grad = added(near_sum, swap(far_sum, "y"))
+
     grad_final = lax.dot_general(
         pos_hot.astype(jnp.float32),
         grad_chosen,
@@ -587,31 +645,23 @@
         preferred_element_type=jnp.float32,
     )
 
-    head_cols = head_rows.reshape(-1, 2, 2, slice_width)
-
-    def table_part(by_y, by_c):
-        cols = pick(pick(head_cols, at_y ^ by_y, 1), at_c ^ by_c, 1)
-        return outer_dot(grad_low, cols).astype(jnp.bfloat16)
-
-    far_sum = lowered(table_part(1, 0), swap(table_part(1, 1), "core"))
-    near_sum = added(table_part(0, 0), swap(table_part(0, 1), "core"))
-    head_table_grad = added(near_sum, swap(far_sum, "y"))
-
-    is_first = group_id == 0
+    is_first = group_id == 2 * ways * at_b
     loss_part = jnp.where(is_first, jnp.sum(weight_rows * (logsum_all - target_logit)), 0.0)
     count_part = jnp.where(is_first, jnp.sum(weight_rows), 0.0)
     unused, final_back = jax.vjp(layer_norm, residual_out, gain_final, shift_final)
     grad_resid, grad_gain_final, grad_shift_final = final_back(grad_final)
     resid_low = grad_resid.astype(jnp.bfloat16)
     grad_bias_down = column_sum(resid_low)
-    grad_active = jnp.concatenate(
-        [low_dot(resid_low, reduce_one), low_dot(resid_low, reduce_two)], 1
-    )
+    plane_rows = layer_weight.shape[0] * groups * part_count // PLANES
+    reduce_cut = hidden_units - plane_rows
     plane_three = outer_dot(active_low[:, reduce_cut:], resid_low, jnp.bfloat16)
-    piece_three = scatter_plane(plane_three)
+    piece_three = reduce_plane(plane_three)
+    resid_low = order.hold(resid_low, plane_three)
+    grad_active = low_dot(resid_low, reduce_weight)
     unused, gelu_back = jax.vjp(smooth, hidden)
     hidden_low = gelu_back(grad_active)[0].astype(jnp.bfloat16)
     grad_bias_up = column_sum(hidden_low)
+    half = plane_rows - model_dim
     plane_two = jnp.concatenate(
         [
             outer_dot(hidden_low[:, half:], normed_two_low, jnp.bfloat16),
@@ -619,11 +669,9 @@
         ],
         0,
     )
-    piece_two = scatter_plane(plane_two)
+    piece_two = reduce_plane(plane_two)
     unused, two_back = jax.vjp(layer_norm, middle, gain_two, shift_two)
-    grad_middle_part, grad_gain_two, grad_shift_two = two_back(
-        plain_dot(hidden_low[:, :half], expand_one) + plain_dot(hidden_low[:, half:], expand_two)
-    )
+    grad_middle_part, grad_gain_two, grad_shift_two = two_back(plain_dot(hidden_low, expand_weight))
     grad_middle = grad_resid + grad_middle_part
     middle_low = grad_middle.astype(jnp.bfloat16)
     grad_bias_out = column_sum(middle_low)
@@ -635,64 +683,82 @@
         concat_axis=0,
         tiled=True,
     )[:, 0]
-    plane_one = jnp.concatenate(
-        [
-            outer_dot(middle_low, mixed_low, jnp.bfloat16),
-            outer_dot(hidden_low[:, :half], normed_two_low, jnp.bfloat16),
-        ],
-        0,
-    )
-    piece_one = scatter_plane(plane_one)
+    core_one = scatter_core(
+        jnp.concatenate(
+            [
+                outer_dot(middle_low, mixed_low, jnp.bfloat16),
+                outer_dot(hidden_low[:, :half], normed_two_low, jnp.bfloat16),
+            ],
+            0,
+        )
+    )
+    grad_heads = order.hold(grad_heads, plane_two)
     grad_query, grad_keys, grad_values = attend_back(
         starts, queries, key_rows, values, grad_heads, mixture_wide, logsum
     )
+    grad_heads = order.hold(jnp.stack([grad_query, grad_keys, grad_values], 1), core_one)
     grad_joined = lax.all_to_all(
-        jnp.stack([grad_query, grad_keys, grad_values], 1).reshape(
-            part_count, tok_rows, 3, 1, head_width
-        ),
+        grad_heads.reshape(part_count, tok_rows, 3, 1, head_width),
         SEQ,
         split_axis=0,
         concat_axis=3,
         tiled=True,
     ).reshape(tok_rows, 3 * model_dim)
+    core_zero = scatter_core(outer_dot(grad_joined, normed_low, jnp.bfloat16))
     unused, one_back = jax.vjp(layer_norm, embedded, gain_one, shift_one)
-    grad_embed_part, grad_gain_one, grad_shift_one = one_back(plain_dot(grad_joined, planes[0]))
+    grad_embed_part, grad_gain_one, grad_shift_one = one_back(plain_dot(grad_joined, gathered[: 3 * model_dim]))
     rows_back = (grad_middle + grad_embed_part).astype(jnp.bfloat16)
+    first_one = scatter_first(order.hold(core_one, grad_joined))
+    rows_back = order.hold(rows_back, core_zero)
     rows_back = lax.all_to_all(rows_back, SEQ, split_axis=1, concat_axis=0, tiled=True)
-    all_ids = lax.all_gather(token_ids, SEQ, axis=1, tiled=True) - group_id * vocab_rows
-    all_ids = all_ids.reshape(PLANES, ways, 2, tok_rows, part_count).swapaxes(3, 4)
-    table_grad = head_table_grad
-    for got, from_z, from_x in from_groups(rows_back):
-        ids = pick(pick(all_ids, from_z, 0), from_x, 1).reshape(1, -1)
-        hot = (row_range[:, None] == ids).astype(jnp.bfloat16)
-        table_grad = table_grad + plain_dot(hot, got.reshape(-1, slice_width))
     grad_bias_q = column_sum(grad_joined[:, :model_dim])
     grad_bias_v = column_sum(grad_joined[:, 2 * model_dim :])
-    piece_zero = scatter_plane(outer_dot(grad_joined, normed_low, jnp.bfloat16))
-    layer_grad = (
-        exchange_planes(jnp.stack([piece_zero, piece_one, piece_two, piece_three]))
-        .reshape(layer_weight.shape)
-        .astype(jnp.float32)
-    )
-    early = total_of(
+    first_zero = scatter_first(core_zero)
+    second_one = scatter_second(first_one)
+    second_zero = scatter_second(first_zero)
+    row_range = jnp.arange(vocab_rows, dtype=jnp.int32)[:, None]
+    sides = {"mine": at_b, "theirs": 1 - at_b}
+    spread = {
+        name: lax.dynamic_slice_in_dim(head_table_grad, side * vocab_rows, vocab_rows, 0)
+        for name, side in sides.items()
+    }
+    rows_back = rows_back.reshape(2, length // 2, slice_width)
+    id_halves = all_ids.reshape(2, 2, ways, 2, length // 2)
+    for at in range(2):
+        got = from_groups(rows_back[at], order, (first_one, first_zero)[at])
+        got = order.hold(got, (second_one, second_zero)[at]).reshape(-1, slice_width)
+        ids = id_halves[:, :, :, at].reshape(1, -1) - first_start
+        for name, side in sides.items():
+            hot = (row_range == ids - side * plane_step).astype(jnp.bfloat16)
+            spread[name] = spread[name] + plain_dot(hot, got)
+    table_grad = added(spread["mine"], swap(spread["theirs"].astype(jnp.bfloat16), "zb"))
+    piece_one = scatter_last(second_one)
+    piece_zero = scatter_last(second_zero)
+    quarters = jnp.stack([piece_zero, piece_one, piece_two, piece_three])
+    layer_grad = jnp.stack(sent_z([pick(quarters, plane) for plane in planes_from_here()]))
+    squares = jnp.sum(jnp.square(layer_grad.astype(jnp.float32))) + jnp.sum(
+        table_grad * table_grad
+    )
+    totals = total_of(
         jnp.concatenate(
             [
+                grad_bias_q,
+                grad_bias_v,
                 grad_bias_out,
                 grad_bias_up,
                 grad_bias_down,
+                grad_gain_one,
+                grad_shift_one,
                 grad_gain_two,
                 grad_shift_two,
                 grad_gain_final,
                 grad_shift_final,
-                jnp.stack([loss_part, count_part]),
+                jnp.stack([squares, loss_part, count_part]),
             ]
         )
     )
-    late = total_of(jnp.concatenate([grad_bias_q, grad_bias_v, grad_gain_one, grad_shift_one]))
-    cut = 2 * model_dim + hidden_units
-    small_grad = jnp.concatenate([late[: 2 * model_dim], early[:cut], late[2 * model_dim :], early[cut:-2]])
-    loss_sum, loss_count = early[-2], early[-1]
-    squares = total_of(jnp.sum(layer_grad * layer_grad) + jnp.sum(table_grad * table_grad))
+    squares, loss_sum, loss_count = totals[-3], totals[-2], totals[-1] + order.zero()
+    small_grad = totals[:-3]
     gradient_norm = jnp.sqrt(squares + jnp.sum(small_grad * small_grad))
     factor = 1.0 / jnp.maximum(gradient_norm, 1.0)
     out_bias_grad = factor * small_grad[2 * model_dim : 3 * model_dim]
@@ -726,7 +792,7 @@
 
 def solution(mesh):
     vocab, seq = mesh.shape["vocab"], mesh.shape["seq"]
-    inner = Mesh(mesh.devices.reshape(PLANES, vocab // 8, 2, seq // 2, 2), ALL)
+    inner = Mesh(mesh.devices.reshape(2, 2, vocab // 8, 2, seq // 2, 2), ALL)
     in_specs = (
         P(None, SEQ),
         P(),

time: 1610 us -> 1110 us (0.69)
  waiting for transfers between devices: 728 us -> 527 us
  local copies, waits for them, and re-layouts: 249 us -> 106 us
  starting transfers between devices: 210 us -> 77.2 us
  matrix products: 205 us -> 179 us
  other arithmetic: 108 us -> 84.8 us
  between operations: 11.5 us -> 31.3 us
  Pallas kernels: 79.8 us -> 99.4 us
    ppermute x84 -> x36, waiting for transfers between devices: 465 us -> 291 us  [swap(): return lax.ppermute(tensor, axis, [(0, 1), (1, 0)])]
    ppermute x60 -> x13, waiting for transfers between devices: 251 us -> 116 us  [the longest x4 81.4 us: flip(): return lax.ppermute(tensor, ('x', 'y', 'core'), pairs)]
    ppermute x60 -> x13, starting transfers between devices: 109 us -> 17.5 us  [the longest x9 12.6 us: shift(): lax.ppermute(tensor, PLANE, [(i, (i + step) % PLANES) for i in range(PLAN...]
    dynamic_update_slice x79 -> x0, local copies, waits for them, and re-layouts: 77.8 us -> none  [the longest x64 76.9 us: gather_weights(): lax.dynamic_update_slice(whole, both[:, spot:spot + 1], (0, owner, offset...]
    ppermute x84 -> x36, starting transfers between devices: 76.9 us -> 38.6 us  [swap(): return lax.ppermute(tensor, axis, [(0, 1), (1, 0)])]
    all_to_all x1, waiting for transfers between devices: 0.01 us -> 34.4 us  [body(): lax.all_to_all(joined.astype(jnp.bfloat16).reshape(tok_rows, 3, part_coun...]
    all_to_all x1, waiting for transfers between devices: 0.01 us -> 26.9 us  [body(): lax.all_to_all(grad_heads.reshape(part_count, tok_rows, 3, 1, head_width)...]
    another operation x9 -> x5, local copies, waits for them, and re-layouts: 23.5 us -> 2.55 us  [the longest x3 2.44 us: from_groups(): jnp.stack(both + [swap(part, 'x') for part in both])]
  transfers between devices with their start and end apart: 149 -> 57, of which waited for: 61 -> 34; matrix products, arithmetic and copies ran while one was open for 27% -> 25% of each run, Pallas kernels for 3% -> 3%
where the time goes in v2:
time: 1110 us; the launch traced here: 1100 us
  waiting for transfers between devices  527 us (47%)
  matrix products  179 us (16%)
  local copies, waits for them, and re-layouts  106 us (10%)
  Pallas kernels  99.4 us (9%)
  other arithmetic  84.8 us (8%)
  starting transfers between devices  77.2 us (7%)
  between operations  31.3 us (3%)
    ppermute x36, waiting for transfers between devices, swap(): return lax.ppermute(tensor, axis, [(0, 1), (1, 0)])  291 us
    dot_general x14, matrix products, plain_dot(): return jnp.dot(left, right, preferred_element_type=jnp.float32)  89.4 us
    ppermute x4, waiting for transfers between devices, flip(): return lax.ppermute(tensor, ('x', 'y', 'core'), pairs)  81.4 us
    dot_general x5, matrix products, low_dot(): lax.dot_general(left, right, LANES_BOTH, preferred_element_type=jnp.float32)  50.2 us
    ppermute x36, starting transfers between devices, swap(): return lax.ppermute(tensor, axis, [(0, 1), (1, 0)])  38.6 us
    pallas_call x1, Pallas kernels, frame(): pl.pallas_call(frame_kernel, out_shape=jax.ShapeDtypeStruct(gram.shape, j...  37.6 us
    dot_general x10, matrix products, outer_dot(): lax.dot_general(left, right, (((0,), (0,)), ((), ())), preferred_element_...  37 us
    ppermute x9, waiting for transfers between devices, shift(): lax.ppermute(tensor, PLANE, [(i, (i + step) % PLANES) for i in range(PLAN...  34.6 us
  transfers between devices with their start and end apart: 57, of which 34 were waited for; matrix products, arithmetic and copies ran while one was open for 25% of the time, Pallas kernels for 3%

profile of v2, /device:TPU:0, one launch (start us, length us, event | category | flops | bytes accessed | tf_op | source)
XLA Modules:
  0.0 1104.1 jit_solution(8639618533041604012)
XLA Ops:
  13.5 47.8 %collective-permute-done = bf16[1576,320]{0,1:T(8,128)(2,1)} collective-permute-done((bf16[1576,320]{0,1:T(8,128)(2,1)S(1)}, bf16[1576,320]{0,1:T(8,128)(2,1)}, u32[]{:S(2)}, u32[]{:S(2)}) %collective-permute-start) | collective-permute-done | bytes 1008672 | tf_op jit(solution)/shard_map/ppermute | solution.py:69
  77.2 31.3 %collective-permute-done.4 = bf16[1576,320]{0,1:T(8,128)(2,1)} collective-permute-done((bf16[1576,320]{0,1:T(8,128)(2,1)S(1)}, bf16[1576,320]{0,1:T(8,128)(2,1)}, u32[]{:S(2)}, u32[]{:S(2)}) %collective-permute-start.4) | collective-permute-done | bytes 1008672 | tf_op jit(solution)/shard_map/ppermute | solution.py:69
  113.5 17.4 %collective-permute-done.5 = bf16[1576,320]{0,1:T(8,128)(2,1)S(1)} collective-permute-done((bf16[1576,320]{0,1:T(8,128)(2,1)}, bf16[1576,320]{0,1:T(8,128)(2,1)S(1)}, u32[]{:S(2)}, u32[]{:S(2)}) %collective-permute-start.5) | collective-permute-done | bytes 1008672 | tf_op jit(solution)/shard_map/ppermute | solution.py:69
  135.6 41.4 %collective-permute-done.2 = bf16[2,1,384,640]{3,2,1,0:T(8,128)(2,1)S(1)} collective-permute-done((bf16[2,1,384,640]{3,2,1,0:T(8,128)(2,1)S(1)}, bf16[2,1,384,640]{3,2,1,0:T(8,128)(2,1)S(1)}, u32[]{:S(2)}, u32[]{:S(2)}) %collective-permute-start.2) | collective-permute-done | bytes 983072 | tf_op jit(solution)/shard_map/ppermute | solution.py:69
  194.1 35.5 %collective-permute-done.7 = bf16[2,1,384,640]{3,2,1,0:T(8,128)(2,1)S(1)} collective-permute-done((bf16[2,1,384,640]{3,2,1,0:T(8,128)(2,1)S(1)}, bf16[2,1,384,640]{3,2,1,0:T(8,128)(2,1)S(1)}, u32[]{:S(2)}, u32[]{:S(2)}) %collective-permute-start.7) | collective-permute-done | bytes 983072 | tf_op jit(solution)/shard_map/ppermute | solution.py:69
  235.4 44.9 %collective-permute-done.8 = bf16[384,640]{1,0:T(8,128)(2,1)} collective-permute-done((bf16[384,640]{1,0:T(8,128)(2,1)S(1)}, bf16[384,640]{1,0:T(8,128)(2,1)}, u32[]{:S(2)}, u32[]{:S(2)}) %collective-permute-start.8) | collective-permute-done | bytes 491552 | tf_op jit(solution)/shard_map/ppermute | solution.py:69
  282.3 19.2 %all-gather.2.cloned.1.call-done = bf16[15360,1280]{1,0:T(8,128)(2,1)} async-done(((bf16[480,1280]{1,0:T(8,128)(2,1)}), bf16[15360,1280]{1,0:T(8,128)(2,1)}) %all-gather.2.cloned.1.call-update) | async-done | bytes 39321616 | tf_op jit(solution)/shard_map/all_gather | solution.py:515
  325.1 34.4 %all-to-all-done = bf16[384,3,4,320]{0,3,1,2:T(8,128)(2,1)} async-done(((bf16[384,3,4,320]{0,3,1,2:T(8,128)(2,1)}), bf16[384,3,4,320]{0,3,1,2:T(8,128)(2,1)}, u32[]{:S(2)}, u32[]{:S(2)}) %all-to-all-start) | async-done | bytes 2949152 | tf_op jit(solution)/shard_map/all_to_all | solution.py:568
  367.7 14.9 %shard_map.271 = (bf16[1536,320]{1,0:T(8,128)(2,1)S(1)}, f32[1536,320]{1,0:T(8,128)S(1)}, f32[8,1536]{1,0:T(8,128)S(1)}) custom-call(s32[1,1536]{1,0:T(1,128)S(1)} %broadcast_in_dim.58.start_ref, bf16[1536,320]{1,0:T(8,128)(2,1)S(1)} %get-tuple-element.226.q_ref, bf16[1536,320]{1,0:T(8,128)(2,1)S(1)} %get-tuple-element.225.k_ref, ...), custom_call_target="tpu_custom_call" | custom-call | tf_op jit(solution)/shard_map/pallas_call | solution.py:261
  392.7 11.6 %all-to-all-done.1 = bf16[4,384,1,320]{1,3,2,0:T(8,128)(2,1)S(1)} async-done(((bf16[4,384,1,320]{1,3,2,0:T(8,128)(2,1)}), bf16[4,384,1,320]{1,3,2,0:T(8,128)(2,1)S(1)}, u32[]{:S(2)}, u32[]{:S(2)}) %all-to-all-start.1) | async-done | bytes 983072 | tf_op jit(solution)/shard_map/all_to_all | solution.py:577
  408.7 12.0 %multiply_convert_fusion = (bf16[384,5120]{1,0:T(8,128)(2,1)S(1)}, f32[384,5120]{1,0:T(8,128)}) fusion(f32[5120]{0:T(1024)S(1)} %slice.259, bf16[15360,1280]{1,0:T(8,128)(2,1)} %all-gather.2.cloned.1.call-done, f32[384,1280]{1,0:T(8,128)S(1)} %get-tuple-element.285, f32[1280]{0:T(1024)S(1)} %copy-done.86, f32[1280]{0:T(1024)S(1)} %get-tuple-element.247, ...), kind=kOutput, calls=%fused_computation.47 | convolution fusion | flops 5055283200 | bytes 26903552 | tf_op jit(solution)/shard_map/dot_general | solution.py:46
  473.0 11.1 %convolution_convert_fusion.4 = bf16[256,1280]{1,0:T(8,128)(2,1)S(1)} fusion(bf16[256,3152]{0,1:T(8,128)(2,1)S(1)} %multiply_convert_fusion.1, bf16[3152,640]{0,1:T(8,128)(2,1)} %copy-done.48, bf16[3152,640]{0,1:T(8,128)(2,1)S(1)} %copy-done.47, pred[]{:T(512)S(6)} %eq.70), kind=kOutput, calls=%fused_computation.89 | convolution fusion | flops 2102333440 | bytes 10338305 | tf_op jit(solution)/shard_map/dot_general | solution.py:50
  516.2 15.4 %convert_reduce_fusion = (f32[5120]{0:T(1024)}, bf16[384,5120]{1,0:T(8,128)(2,1)}) fusion(f32[384,5120]{1,0:T(8,128)} %get-tuple-element.287, bf16[384,1280]{1,0:T(8,128)(2,1)S(1)} %get-tuple-element.57, bf16[15360,1280]{1,0:T(8,128)(2,1)} %all-gather.2.cloned.1.call-done), kind=kOutput, calls=%fused_computation.46 | convolution fusion | flops 5076413440 | bytes 25907200 | tf_op jit(solution)/shard_map/dot_general | solution.py:46
  577.8 13.3 %all-to-all-done.2 = bf16[384,4,320]{0,2,1:T(8,128)(2,1)} async-done(((bf16[384,4,320]{0,2,1:T(8,128)(2,1)}), bf16[384,4,320]{0,2,1:T(8,128)(2,1)}, u32[]{:S(2)}, u32[]{:S(2)}) %all-to-all-start.2) | async-done | bytes 983072 | tf_op jit(solution)/shard_map/all_to_all | solution.py:679
  597.3 27.6 %shard_map.272 = (bf16[1536,320]{1,0:T(8,128)(2,1)S(1)}, bf16[1536,320]{1,0:T(8,128)(2,1)S(1)}, bf16[1536,320]{1,0:T(8,128)(2,1)S(1)}) custom-call(s32[1,1536]{1,0:T(1,128)S(1)} %copy-done.18, bf16[1536,320]{1,0:T(8,128)(2,1)S(1)} %copy-done.7, bf16[1536,320]{1,0:T(8,128)(2,1)S(1)} %copy-done.5, bf16[1536,320]{1,0:T(8,128)(2,1)S(1)} %copy-done.3, ...), custom_call_target="tpu_custom_call" | custom-call | tf_op jit(solution)/shard_map/pallas_call | solution.py:329
  651.6 26.9 %all-to-all-done.3 = bf16[4,384,3,1,320]{1,4,2,3,0:T(8,128)(2,1)S(1)} async-done(((bf16[4,384,3,1,320]{1,4,2,3,0:T(8,128)(2,1)}), bf16[4,384,3,1,320]{1,4,2,3,0:T(8,128)(2,1)S(1)}, u32[]{:S(2)}, u32[]{:S(2)}) %all-to-all-start.3) | async-done | bytes 2949152 | tf_op jit(solution)/shard_map/all_to_all | solution.py:700
  713.5 55.5 %collective-permute-done.28 = bf16[1,2,480,1280]{3,2,1,0:T(8,128)(2,1)} collective-permute-done((bf16[1,2,480,1280]{3,2,1,0:T(8,128)(2,1)}, bf16[1,2,480,1280]{3,2,1,0:T(8,128)(2,1)}, u32[]{:S(2)}, u32[]{:S(2)}) %collective-permute-start.28) | collective-permute-done | bytes 2457632 | tf_op jit(solution)/shard_map/ppermute | solution.py:130
  774.0 14.2 %collective-permute-done.29 = bf16[1,480,1280]{2,1,0:T(8,128)(2,1)S(1)} collective-permute-done((bf16[1,480,1280]{2,1,0:T(8,128)(2,1)S(1)}, bf16[1,480,1280]{2,1,0:T(8,128)(2,1)S(1)}, u32[]{:S(2)}, u32[]{:S(2)}) %collective-permute-start.29) | collective-permute-done | bytes 1228832 | tf_op jit(solution)/shard_map/ppermute | solution.py:130
  813.1 14.1 %all-to-all-done.4 = bf16[384,4,320]{0,2,1:T(8,128)(2,1)} async-done(((bf16[384,4,320]{0,2,1:T(8,128)(2,1)}), bf16[384,4,320]{0,2,1:T(8,128)(2,1)}, u32[]{:S(2)}, u32[]{:S(2)}) %all-to-all-start.4) | async-done | bytes 983072 | tf_op jit(solution)/shard_map/all_to_all | solution.py:713
  843.1 17.3 %collective-permute-done.37 = bf16[1,768,320]{1,2,0:T(8,128)(2,1)} collective-permute-done((bf16[1,768,320]{1,2,0:T(8,128)(2,1)}, bf16[1,768,320]{1,2,0:T(8,128)(2,1)}, u32[]{:S(2)}, u32[]{:S(2)}) %collective-permute-start.37) | collective-permute-done | bytes 491552 | tf_op jit(solution)/shard_map/ppermute | solution.py:69
  913.1 11.7 %collective-permute-done.24 = bf16[1,480,1280]{2,1,0:T(8,128)(2,1)S(1)} collective-permute-done((bf16[1,480,1280]{2,1,0:T(8,128)(2,1)S(1)}, bf16[1,480,1280]{2,1,0:T(8,128)(2,1)S(1)}, u32[]{:S(2)}, u32[]{:S(2)}) %collective-permute-start.24) | collective-permute-done | bytes 1228832 | tf_op jit(solution)/shard_map/ppermute | solution.py:130
  962.1 22.7 %collective-permute-done.35 = bf16[120,1280]{1,0:T(8,128)(2,1)S(1)} collective-permute-done((bf16[120,1280]{1,0:T(8,128)(2,1)S(1)}, bf16[120,1280]{1,0:T(8,128)(2,1)S(1)}, u32[]{:S(2)}, u32[]{:S(2)}) %collective-permute-start.35) | collective-permute-done | bytes 307232 | tf_op jit(solution)/shard_map/ppermute | solution.py:76
  1029.1 19.2 %shard_map.273 = (f32[480,1280]{1,0:T(8,128)}, f32[480,1280]{1,0:T(8,128)}, f32[480,1280]{1,0:T(8,128)}, f32[1,10,128,128]{3,2,1,0:T(8,128)}, f32[10,128,128]{2,1,0:T(8,128)S(1)}, /*index=5*/f32[10,128,128]{2,1,0:T(8,128)S(1)}) custom-call(s32[1]{0:T(128)} %bitcast.152.place_ref, f32[1,1]{1,0:T(1,128)} %bitcast.153.factor_ref, f32[480,1280]{1,0:T(8,128)S(1)} %copy-done.8, ...), custom_call_target="tpu_custom_call" | custom-call | tf_op jit(solution)/shard_map/pallas_call | solution.py:452
  1048.3 37.6 %shard_map.274 = f32[10,128,128]{2,1,0:T(8,128)S(1)} custom-call(f32[10,128,128]{2,1,0:T(8,128)S(1)} %get-tuple-element.88.gram_ref, f32[10,128,128]{2,1,0:T(8,128)S(1)} %get-tuple-element.89.span_ref), custom_call_target="tpu_custom_call" | custom-call | tf_op jit(solution)/shard_map/pallas_call | solution.py:380
  (511 shorter events, 475.8 us)
Async XLA Ops:
  7.2 294.3 %all-gather.2.cloned.1.call-start = ((), (), s32[]{:S(2)}) async-start(), calls=%async_computation.7 | async-start | bytes 40550400 | tf_op jit(solution)/shard_map/all_gather | solution.py:515
  10.4 50.9 %collective-permute-start = (bf16[1576,320]{0,1:T(8,128)(2,1)S(1)}, bf16[1576,320]{0,1:T(8,128)(2,1)}, u32[]{:S(2)}, u32[]{:S(2)}) collective-permute-start(bf16[1576,320]{0,1:T(8,128)(2,1)S(1)} %convert_element_type.420), channel_id=1, source_target_pairs={{0,8},{8,0},{1,9},{9,1},{2,10},{10,2},{3,11},{11,3},{4,12},{12,4},... | collective-permute-start | bytes 3025928 | tf_op jit(solution)/shard_map/ppermute | solution.py:69
  64.2 44.3 %collective-permute-start.4 = (bf16[1576,320]{0,1:T(8,128)(2,1)S(1)}, bf16[1576,320]{0,1:T(8,128)(2,1)}, u32[]{:S(2)}, u32[]{:S(2)}) collective-permute-start(bf16[1576,320]{0,1:T(8,128)(2,1)S(1)} %convert_element_type.420), channel_id=1, source_target_pairs={{0,2},{2,0},{1,3},{3,1},{4,6},{6,4},{5,7},{7,5},{8,10},{10,8},{9,1... | collective-permute-start | bytes 3025928 | tf_op jit(solution)/shard_map/ppermute | solution.py:69
  67.8 63.1 %collective-permute-start.5 = (bf16[1576,320]{0,1:T(8,128)(2,1)}, bf16[1576,320]{0,1:T(8,128)(2,1)S(1)}, u32[]{:S(2)}, u32[]{:S(2)}) collective-permute-start(bf16[1576,320]{0,1:T(8,128)(2,1)} %collective-permute-done), channel_id=1, source_target_pairs={{0,2},{2,0},{1,3},{3,1},{4,6},{6,4},{5,7},{7,5},{8,10},{10,8},{9,1... | collective-permute-start | bytes 3025928 | tf_op jit(solution)/shard_map/ppermute | solution.py:69
  133.8 43.5 %collective-permute-start.6 = (bf16[3152,320]{0,1:T(8,128)(2,1)S(1)}, bf16[3152,320]{0,1:T(8,128)(2,1)S(1)}, u32[]{:S(2)}, u32[]{:S(2)}) collective-permute-start(bf16[3152,320]{0,1:T(8,128)(2,1)S(1)} %maximum_select_fusion.4), channel_id=1, source_target_pairs={{0,1},{1,0},{2,3},{3,2},{4,5},{5,4},{6,7},{7,6},{8,9},{9,8},{10,11... | collective-permute-start | bytes 6051848 | tf_op jit(solution)/shard_map/ppermute | solution.py:69
  133.9 43.2 %collective-permute-start.2 = (bf16[2,1,384,640]{3,2,1,0:T(8,128)(2,1)S(1)}, bf16[2,1,384,640]{3,2,1,0:T(8,128)(2,1)S(1)}, u32[]{:S(2)}, u32[]{:S(2)}) collective-permute-start(bf16[2,1,384,640]{3,2,1,0:T(8,128)(2,1)S(1)} %bitcast.369), channel_id=1, source_target_pairs={{0,4},{4,0},{1,5},{5,1},{2,6},{6,2},{3,7},{7,3},{8,12},{12,8},{9,1... | collective-permute-start | bytes 2949128 | tf_op jit(solution)/shard_map/ppermute | solution.py:69
  184.0 45.6 %collective-permute-start.7 = (bf16[2,1,384,640]{3,2,1,0:T(8,128)(2,1)S(1)}, bf16[2,1,384,640]{3,2,1,0:T(8,128)(2,1)S(1)}, u32[]{:S(2)}, u32[]{:S(2)}) collective-permute-start(bf16[2,1,384,640]{3,2,1,0:T(8,128)(2,1)S(1)} %bitcast.370), channel_id=1, source_target_pairs={{0,4},{4,0},{1,5},{5,1},{2,6},{6,2},{3,7},{7,3},{8,12},{12,8},{9,1... | collective-permute-start | bytes 2949128 | tf_op jit(solution)/shard_map/ppermute | solution.py:69
  186.6 47.6 %collective-permute-start.3 = (bf16[384,640]{1,0:T(8,128)(2,1)S(1)}, bf16[384,640]{1,0:T(8,128)(2,1)}, u32[]{:S(2)}, u32[]{:S(2)}) collective-permute-start(bf16[384,640]{1,0:T(8,128)(2,1)S(1)} %slice_bitcast_fusion.5), channel_id=1, source_target_pairs={{0,16},{16,0},{1,17},{17,1},{2,18},{18,2},{3,19},{19,3},{4,20},{20... | collective-permute-start | bytes 1474568 | tf_op jit(solution)/shard_map/ppermute | solution.py:69
  229.9 50.4 %collective-permute-start.8 = (bf16[384,640]{1,0:T(8,128)(2,1)S(1)}, bf16[384,640]{1,0:T(8,128)(2,1)}, u32[]{:S(2)}, u32[]{:S(2)}) collective-permute-start(bf16[384,640]{1,0:T(8,128)(2,1)S(1)} %slice_bitcast_fusion.3), channel_id=1, source_target_pairs={{0,16},{16,0},{1,17},{17,1},{2,18},{18,2},{3,19},{19,3},{4,20},{20... | collective-permute-start | bytes 1474568 | tf_op jit(solution)/shard_map/ppermute | solution.py:69
  319.8 39.6 %all-to-all-start = ((bf16[384,3,4,320]{0,3,1,2:T(8,128)(2,1)}), bf16[384,3,4,320]{0,3,1,2:T(8,128)(2,1)}, u32[]{:S(2)}, u32[]{:S(2)}) async-start(bf16[384,3,4,320]{0,3,1,2:T(8,128)(2,1)} %copy.124), calls=%async_computation | async-start | bytes 5898240 | tf_op jit(solution)/shard_map/all_to_all | solution.py:568
  390.6 561.0 %reduce-scatter.5.cloned.1.call-start = ((), (), s32[]{:S(2)}) async-start(), calls=%async_computation.9 | async-start | bytes 10137600 | tf_op jit(solution)/shard_map/reduce_scatter | solution.py:134
  390.7 96.2 %collective-permute-start.19 = (s32[2,2,1,384,1]{3,4,1,0,2:T(1,128)S(1)}, s32[2,2,1,384,1]{3,4,1,0,2:T(1,128)S(1)}, u32[]{:S(2)}, u32[]{:S(2)}) collective-permute-start(s32[2,2,1,384,1]{3,4,1,0,2:T(1,128)S(1)} %pad_add_fusion), channel_id=1, source_target_pairs={{0,1},{1,0},{2,3},{3,2},{4,5},{5,4},{6,7},{7,6},{8,9},{9,8},{10,11... | collective-permute-start | bytes 18440 | tf_op jit(solution)/shard_map/ppermute | solution.py:69
  559.5 66.2 %collective-permute-start.21 = (bf16[1,2,2,480,1280]{4,3,2,1,0:T(8,128)(2,1)}, bf16[1,2,2,480,1280]{4,3,2,1,0:T(8,128)(2,1)}, u32[]{:S(2)}, u32[]{:S(2)}) collective-permute-start(bf16[1,2,2,480,1280]{4,3,2,1,0:T(8,128)(2,1)} %dynamic-slice_bitcast_fusion.1), channel_id=1, source_target_pairs={{0,1},{1,0},{2,3},{3,2},{4,5},{5,4},{6,7},{7,6},{8,9},{9,8},{10,11... | collective-permute-start | bytes 14745608 | tf_op jit(solution)/shard_map/ppermute | solution.py:69
  637.2 41.3 %all-to-all-start.3 = ((bf16[4,384,3,1,320]{1,4,2,3,0:T(8,128)(2,1)}), bf16[4,384,3,1,320]{1,4,2,3,0:T(8,128)(2,1)S(1)}, u32[]{:S(2)}, u32[]{:S(2)}) async-start(bf16[4,384,3,1,320]{1,4,2,3,0:T(8,128)(2,1)} %copy.135), calls=%async_computation.3 | async-start | bytes 5898240 | tf_op jit(solution)/shard_map/all_to_all | solution.py:700
  641.0 310.7 %reduce-scatter.3.cloned.1.call-start = ((), (), s32[]{:S(2)}) async-start(), calls=%async_computation.8 | async-start | bytes 10137600 | tf_op jit(solution)/shard_map/reduce_scatter | solution.py:134
  644.2 188.5 %collective-permute-start.36 = (bf16[3152,320]{0,1:T(8,128)(2,1)}, bf16[3152,320]{0,1:T(8,128)(2,1)}, u32[]{:S(2)}, u32[]{:S(2)}) collective-permute-start(bf16[3152,320]{0,1:T(8,128)(2,1)} %copy-done.50), channel_id=1, source_target_pairs={{0,2},{2,0},{1,3},{3,1},{4,6},{6,4},{5,7},{7,5},{8,10},{10,8},{9,1... | collective-permute-start | bytes 6051848 | tf_op jit(solution)/shard_map/ppermute | solution.py:69
  685.3 83.7 %collective-permute-start.28 = (bf16[1,2,480,1280]{3,2,1,0:T(8,128)(2,1)}, bf16[1,2,480,1280]{3,2,1,0:T(8,128)(2,1)}, u32[]{:S(2)}, u32[]{:S(2)}) collective-permute-start(bf16[1,2,480,1280]{3,2,1,0:T(8,128)(2,1)} %pad_maximum_fusion.4), channel_id=1, source_target_pairs={{0,2},{1,5},{2,0},{3,7},{4,6},{5,1},{6,4},{7,3},{8,10},{9,13},{10,... | collective-permute-start | bytes 7372808 | tf_op jit(solution)/shard_map/ppermute | solution.py:130
  697.2 96.3 %collective-permute-start.22 = (bf16[1,2,2,480,1280]{4,3,2,1,0:T(8,128)(2,1)}, bf16[1,2,2,480,1280]{4,3,2,1,0:T(8,128)(2,1)}, u32[]{:S(2)}, u32[]{:S(2)}) collective-permute-start(bf16[1,2,2,480,1280]{4,3,2,1,0:T(8,128)(2,1)} %dynamic-slice_bitcast_fusion), channel_id=1, source_target_pairs={{0,1},{1,0},{2,3},{3,2},{4,5},{5,4},{6,7},{7,6},{8,9},{9,8},{10,11... | collective-permute-start | bytes 14745608 | tf_op jit(solution)/shard_map/ppermute | solution.py:69
  789.4 71.0 %collective-permute-start.30 = (bf16[120,1280]{1,0:T(8,128)(2,1)}, bf16[120,1280]{1,0:T(8,128)(2,1)S(1)}, u32[]{:S(2)}, u32[]{:S(2)}) collective-permute-start(bf16[120,1280]{1,0:T(8,128)(2,1)} %get-tuple-element.234), channel_id=1, source_target_pairs={{0,8},{8,16},{16,24},{24,0},{1,9},{9,17},{17,25},{25,1},{2,10},{10... | collective-permute-start | bytes 921608 | tf_op jit(solution)/shard_map/ppermute | solution.py:76
  789.4 73.0 %collective-permute-start.32 = (bf16[120,1280]{1,0:T(8,128)(2,1)}, bf16[120,1280]{1,0:T(8,128)(2,1)}, u32[]{:S(2)}, u32[]{:S(2)}) collective-permute-start(bf16[120,1280]{1,0:T(8,128)(2,1)} %get-tuple-element.235), channel_id=1, source_target_pairs={{0,24},{8,0},{16,8},{24,16},{1,25},{9,1},{17,9},{25,17},{2,26},{10... | collective-permute-start | bytes 921608 | tf_op jit(solution)/shard_map/ppermute | solution.py:76
  793.4 69.0 %collective-permute-start.31 = (bf16[120,1280]{1,0:T(8,128)(2,1)}, bf16[120,1280]{1,0:T(8,128)(2,1)}, u32[]{:S(2)}, u32[]{:S(2)}) collective-permute-start(bf16[120,1280]{1,0:T(8,128)(2,1)} %get-tuple-element.236), channel_id=1, source_target_pairs={{0,16},{8,24},{16,0},{24,8},{1,17},{9,25},{17,1},{25,9},{2,18},{10... | collective-permute-start | bytes 921608 | tf_op jit(solution)/shard_map/ppermute | solution.py:76
  811.2 87.8 %collective-permute-start.23 = (bf16[1,2,480,1280]{3,2,1,0:T(8,128)(2,1)}, bf16[1,2,480,1280]{3,2,1,0:T(8,128)(2,1)}, u32[]{:S(2)}, u32[]{:S(2)}) collective-permute-start(bf16[1,2,480,1280]{3,2,1,0:T(8,128)(2,1)} %pad_maximum_fusion.3), channel_id=1, source_target_pairs={{0,2},{1,5},{2,0},{3,7},{4,6},{5,1},{6,4},{7,3},{8,10},{9,13},{10,... | collective-permute-start | bytes 7372808 | tf_op jit(solution)/shard_map/ppermute | solution.py:130
  868.8 40.6 %collective-permute-start.41 = (bf16[1,768,320]{1,2,0:T(8,128)(2,1)}, bf16[1,768,320]{1,2,0:T(8,128)(2,1)}, u32[]{:S(2)}, u32[]{:S(2)}) collective-permute-start(bf16[1,768,320]{1,2,0:T(8,128)(2,1)} %slice.303), channel_id=1, source_target_pairs={{0,4},{4,0},{1,5},{5,1},{2,6},{6,2},{3,7},{7,3},{8,12},{12,8},{9,1... | collective-permute-start | bytes 1474568 | tf_op jit(solution)/shard_map/ppermute | solution.py:69
  942.4 48.1 %collective-permute-start.43 = (bf16[1576,320]{0,1:T(8,128)(2,1)}, bf16[1576,320]{0,1:T(8,128)(2,1)}, u32[]{:S(2)}, u32[]{:S(2)}) collective-permute-start(bf16[1576,320]{0,1:T(8,128)(2,1)} %add_convert_fusion.3), channel_id=1, source_target_pairs={{0,8},{8,0},{1,9},{9,1},{2,10},{10,2},{3,11},{11,3},{4,12},{12,4},... | collective-permute-start | bytes 3025928 | tf_op jit(solution)/shard_map/ppermute | solution.py:69
  (135 other events, 2453.2 us)
Sparse Core Ops, SparseCore 0:
  11.5 289.9 all-gather.1
  516.3 146.3 reduce-scatter.4
  703.8 166.4 reduce-scatter.2

commit v3 on v2

--- a/solution.py
+++ b/solution.py
@@ -130,18 +130,27 @@
     return lax.ppermute(tensor, ("x", "y", "core"), pairs)
 
 
-def reduce_plane(grads):
-    return lax.psum_scatter(grads, OWNERS + PLANE, scatter_dimension=0, tiled=True)
-
-
-def scatter_core(grads):
+def by_owner(grads, planes):
+    shape = (planes, lax.axis_size(ALL), -1, grads.shape[1])
+    return lax.optimization_barrier(grads.reshape(shape))
+
+
+def reduce_planes(grads):
+    return lax.psum_scatter(grads, OWNERS + PLANE, scatter_dimension=1, tiled=False)
+
+
+def as_is(tensor):
+    return tensor
+
+
+def scatter_core(grads, wait=as_is):
     model_dim = grads.shape[1]
     at_c = lax.axis_index("core")
     shaped = grads.reshape(lax.axis_size("w"), 2, 2, 2, -1, model_dim)
-    return lowered(pick(shaped, at_c, 3), swap(pick(shaped, 1 - at_c, 3), "core"))
-
-
-def scatter_first(shaped):
+    return lowered(pick(shaped, at_c, 3), wait(swap(pick(shaped, 1 - at_c, 3), "core")))
+
+
+def scatter_first(shaped, wait=as_is):
     at_x, at_y, at_c = (lax.axis_index(name) for name in ("x", "y", "core"))
     ways, unused, unused, rows, model_dim = shaped.shape
     shaped = shaped.reshape(ways, 4, rows, model_dim)
@@ -150,44 +159,41 @@
         spots = (jnp.where(at_c == 0, y, 2 * x), jnp.where(at_c == 0, 2 + y, 2 * x + 1))
         return jnp.stack([pick(shaped, spot, 1) for spot in spots], 1)
 
-    return lowered(half(at_x, at_y), flip(half(1 - at_x, 1 - at_y), "yx"))
-
-
-def scatter_second(pair):
+    return lowered(half(at_x, at_y), wait(flip(half(1 - at_x, 1 - at_y), "yx")))
+
+
+def scatter_second(pair, wait=as_is):
     spot = jnp.where(lax.axis_index("core") == 0, lax.axis_index("x"), lax.axis_index("y"))
-    own = lowered(pick(pair, spot, 1), flip(pick(pair, 1 - spot, 1), "xy"))
+    own = lowered(pick(pair, spot, 1), wait(flip(pick(pair, 1 - spot, 1), "xy")))
     if lax.axis_size("w") > 1:
         own = lax.psum_scatter(own, "w", scatter_dimension=0, tiled=True)
     return own[0]
 
 
-def scatter_last(own):
+def scatter_last(own, wait=as_is):
     rows, model_dim = own.shape
     quarters = own.reshape(PLANES, rows // PLANES, model_dim)
-    return lowered(*sent_z([pick(quarters, plane) for plane in planes_from_here()]))
+    got = sent_z([pick(quarters, plane) for plane in planes_from_here()])
+    return lowered(got[0], *[wait(part) for part in got[1:]])
 
 
 def own_first(tensor, place, axis):
     return jnp.stack([pick(tensor, place, axis), pick(tensor, 1 - place, axis)])
 
 
-def to_group(theirs, mine):
+def over_x(theirs, mine):
     both = lowered(mine, swap(theirs, "x"))
     if lax.axis_size("w") > 1:
-        both = lax.psum_scatter(both, "w", scatter_dimension=1, tiled=False)
-    else:
-        both = both[:, 0]
-    return added(both[0], swap(both[1], "za"))
-
-
-def from_groups(tensor, order=None, *earlier):
+        return lax.psum_scatter(both, "w", scatter_dimension=1, tiled=False)
+    return both[:, 0]
+
+
+def from_groups(tensor, wait=as_is):
     if lax.axis_size("w") > 1:
         tensor = lax.all_gather(tensor, "w", axis=0, tiled=False)
     else:
         tensor = tensor[None]
-    both = [tensor, swap(tensor, "za")]
-    if order is not None:
-        both[1] = order.hold(both[1], *earlier)
+    both = [tensor, wait(swap(tensor, "za"))]
     return jnp.stack(both + [swap(part, "x") for part in both]).reshape((2, 2) + tensor.shape)
 
 
@@ -197,6 +203,11 @@
     return lax.psum(values, "w") if lax.axis_size("w") > 1 else values
 
 
+def total_at_once(value):
+    spread = jnp.broadcast_to(value, (lax.axis_size(ALL), 1))
+    return jnp.sum(lax.all_to_all(spread, ALL, split_axis=0, concat_axis=0, tiled=True))
+
+
 def _groups(width):
     return [(at,min(128,width-at)) for at in range(0,width,128)]
 
@@ -204,13 +215,15 @@
     lane=lax.broadcasted_iota(jnp.int32,rows.shape,1)
     return jnp.where((lane>=at)&(lane<at+wide),rows,jnp.zeros_like(rows))
 
-def attend_kernel(block, start_ref, q_ref, k_ref, v_ref, low_ref, out_ref, lse_ref, vt_ref):
+def attend_kernel(start_ref, q_ref, k_ref, v_ref, low_ref, out_ref, lse_ref, vt_ref):
+    block=q_ref.shape[2]
     step=pl.program_id(0)
-    width=q_ref.shape[1]
+    width=q_ref.shape[3]
     for at,wide in _groups(width):
         @pl.when(step==0)
         def _():
-            vt_ref[at:at+wide,:]=v_ref[:,at:at+wide].astype(jnp.float32).T.astype(jnp.bfloat16)
+            for part in range(v_ref.shape[0]):
+                vt_ref[part,at:at+wide,:]=v_ref[part,0,:,at:at+wide].astype(jnp.float32).T.astype(jnp.bfloat16)
     start=start_ref[...]
     sub=lax.broadcasted_iota(jnp.int32,(block,block),0)
     lane=lax.broadcasted_iota(jnp.int32,(block,block),1)
@@ -218,17 +231,17 @@
     heads=[(at,h) for at,wide in groups for h in range(wide//HEAD_SIZE)]
     parts=[]
     for at,wide in groups:
-        queries=q_ref[:,at:at+wide]*jnp.bfloat16(HEAD_SIZE**-0.5)
+        queries=q_ref[0,0,:,at:at+wide]*jnp.bfloat16(HEAD_SIZE**-0.5)
         parts+=[_head_part(queries,h*HEAD_SIZE,HEAD_SIZE) for h in range(wide//HEAD_SIZE)]
     def chunk(place, carry, diag):
-        offset=pl.multiple_of(place*block,block)
+        offset=place*block
         allowed=sub>=start-offset
         if diag:
             allowed=allowed&(sub<=lane)
         fresh=[]
         scored=[]
         for i,(at,h) in enumerate(heads):
-            keys=k_ref[pl.ds(offset,block),at:min(at+128,width)]
+            keys=k_ref[place,0,:,at:min(at+128,width)]
             scores=lax.dot_general(keys,parts[i],LANES_BOTH,preferred_element_type=jnp.float32)
             scored.append(jnp.where(allowed,scores,MASKED))
         for i,(at,h) in enumerate(heads):
@@ -237,7 +250,7 @@
             higher=jnp.maximum(peak,jnp.max(scores,0,keepdims=True))
             raised=jnp.exp(scores-higher)
             shrink=jnp.exp(peak-higher)
-            vt=vt_ref[i*HEAD_SIZE:(i+1)*HEAD_SIZE,pl.ds(offset,block)]
+            vt=vt_ref[place,i*HEAD_SIZE:(i+1)*HEAD_SIZE,:]
             acc=acc*shrink+jnp.dot(vt,raised.astype(jnp.bfloat16),preferred_element_type=jnp.float32)
             fresh.append((higher,total*shrink+jnp.sum(raised,0,keepdims=True),acc))
         return tuple(fresh)
@@ -247,34 +260,38 @@
     for at,wide in groups:
         own=carry[at//HEAD_SIZE:(at+wide)//HEAD_SIZE]
         mixed=jnp.concatenate([acc*(1.0/total) for peak,total,acc in own],0).T
-        out_ref[:,at:at+wide]=mixed
-        low_ref[:,at:at+wide]=mixed.astype(jnp.bfloat16)
+        out_ref[0,:,at:at+wide]=mixed
+        low_ref[0,:,at:at+wide]=mixed.astype(jnp.bfloat16)
     for i in range(len(heads)):
         peak,total,acc=carry[i]
         lse_ref[i:i+1,:]=peak+jnp.log(total)
 
-def attend(start, queries, keys, values, block=512):
-    length,width=queries.shape
-    whole=lambda i:(0,0)
-    rows=lambda i:(i,0)
+def attend(start, joined):
+    parts,_,block,width=joined.shape
+    length=parts*block
+    rows=lambda i:(i,0,0)
     cols=lambda i:(0,i)
+    one=pl.BlockSpec((1,1,block,width),lambda i:(i,0,0,0))
+    every=[pl.BlockSpec((parts,1,block,width),lambda i,at=at:(0,at,0,0)) for at in (1,2)]
     return pl.pallas_call(
-        partial(attend_kernel,block),
-        grid=(length//block,),
-        in_specs=[pl.BlockSpec((1,block),cols),pl.BlockSpec((block,width),rows),pl.BlockSpec((length,width),whole),pl.BlockSpec((length,width),whole)],
-        out_specs=[pl.BlockSpec((block,width),rows),pl.BlockSpec((block,width),rows),pl.BlockSpec((8,block),cols)],
-        out_shape=[jax.ShapeDtypeStruct((length,width),jnp.bfloat16),jax.ShapeDtypeStruct((length,width),jnp.float32),jax.ShapeDtypeStruct((8,length),jnp.float32)],
-        scratch_shapes=[pltpu.VMEM((width,length),jnp.bfloat16)],
+        attend_kernel,
+        grid=(parts,),
+        in_specs=[pl.BlockSpec((1,block),cols),one]+every,
+        out_specs=[pl.BlockSpec((1,block,width),rows),pl.BlockSpec((1,block,width),rows),pl.BlockSpec((8,block),cols)],
+        out_shape=[jax.ShapeDtypeStruct((parts,block,width),jnp.bfloat16),jax.ShapeDtypeStruct((parts,block,width),jnp.float32),jax.ShapeDtypeStruct((8,length),jnp.float32)],
+        scratch_shapes=[pltpu.VMEM((parts,width,block),jnp.bfloat16)],
         compiler_params=pltpu.CompilerParams(vmem_limit_bytes=40<<20,dimension_semantics=("arbitrary",)),
-    )(start,queries,keys,values)
-
-def attend_back_kernel(block, start_ref, q_ref, k_ref, v_ref, do_ref, out_ref, lse_ref, dq_ref, dk_ref, dv_ref, kt_ref, dka_ref, dva_ref):
+    )(start,joined,joined,joined)
+
+def attend_back_kernel(start_ref, q_ref, k_ref, v_ref, do_ref, out_ref, lse_ref, grad_ref, kt_ref, dka_ref, dva_ref):
+    block=q_ref.shape[2]
     step=pl.program_id(0)
-    width=q_ref.shape[1]
+    width=q_ref.shape[3]
     @pl.when(step==0)
     def _():
         for at,wide in _groups(width):
-            kt_ref[at:at+wide,:]=k_ref[:,at:at+wide].astype(jnp.float32).T.astype(jnp.bfloat16)
+            for part in range(k_ref.shape[0]):
+                kt_ref[part,at:at+wide,:]=k_ref[part,0,:,at:at+wide].astype(jnp.float32).T.astype(jnp.bfloat16)
         dka_ref[...]=jnp.zeros_like(dka_ref)
         dva_ref[...]=jnp.zeros_like(dva_ref)
     start=start_ref[...]
@@ -282,18 +299,18 @@
     lane=lax.broadcasted_iota(jnp.int32,(block,block),1)
     temper=HEAD_SIZE**-0.5
     for at,wide in _groups(width):
-        queries=q_ref[:,at:at+wide]*jnp.bfloat16(temper)
-        grads=do_ref[:,at:at+wide]
+        queries=q_ref[0,0,:,at:at+wide]*jnp.bfloat16(temper)
+        grads=do_ref[0,:,at:at+wide]
         heads=range(wide//HEAD_SIZE)
         parts=[_head_part(queries,h*HEAD_SIZE,HEAD_SIZE) for h in heads]
         dparts=[_head_part(grads,h*HEAD_SIZE,HEAD_SIZE) for h in heads]
-        crossed=(grads.astype(jnp.float32)*out_ref[:,at:at+wide]).T
+        crossed=(grads.astype(jnp.float32)*out_ref[0,:,at:at+wide]).T
         deltas=[jnp.sum(crossed[h*HEAD_SIZE:(h+1)*HEAD_SIZE],0,keepdims=True) for h in heads]
         lses=[lse_ref[at//HEAD_SIZE+h:at//HEAD_SIZE+h+1,:] for h in heads]
         def chunk(place, carry, diag):
-            offset=pl.multiple_of(place*block,block)
-            keys=k_ref[pl.ds(offset,block),at:at+wide]
-            values=v_ref[pl.ds(offset,block),at:at+wide]
+            offset=place*block
+            keys=k_ref[place,0,:,at:at+wide]
+            values=v_ref[place,0,:,at:at+wide]
             allowed=sub>=start-offset
             if diag:
                 allowed=allowed&(sub<=lane)
@@ -307,80 +324,99 @@
                 one=jnp.dot(dscores,parts[h],preferred_element_type=jnp.float32)
                 two=jnp.dot(chance.astype(jnp.bfloat16),dparts[h],preferred_element_type=jnp.float32)
                 dkey,dval=(one,two) if dkey is None else (dkey+one,dval+two)
-                kt=kt_ref[at+h*HEAD_SIZE:at+(h+1)*HEAD_SIZE,pl.ds(offset,block)]
+                kt=kt_ref[place,at+h*HEAD_SIZE:at+(h+1)*HEAD_SIZE,:]
                 fresh.append(carry[h]+jnp.dot(kt,dscores,preferred_element_type=jnp.float32))
-            dka_ref[pl.ds(offset,block),at:at+wide]+=dkey
-            dva_ref[pl.ds(offset,block),at:at+wide]+=dval
+            dka_ref[place,:,at:at+wide]+=dkey
+            dva_ref[place,:,at:at+wide]+=dval
             return tuple(fresh)
         carry=tuple(jnp.zeros((HEAD_SIZE,block),jnp.float32) for h in heads)
         carry=lax.fori_loop(0,step,lambda c,x:chunk(c,x,False),carry)
         carry=chunk(step,carry,True)
-        dq_ref[:,at:at+wide]=(jnp.concatenate(carry,0).T*temper).astype(jnp.bfloat16)
+        grad_ref[step,0,:,at:at+wide]=(jnp.concatenate(carry,0).T*temper).astype(jnp.bfloat16)
     @pl.when(step==pl.num_programs(0)-1)
     def _():
-        dk_ref[...]=dka_ref[...].astype(jnp.bfloat16)
-        dv_ref[...]=dva_ref[...].astype(jnp.bfloat16)
-
-def attend_back(start, queries, keys, values, grad, out, lse, block=512):
-    length,width=queries.shape
-    whole=lambda i:(0,0)
-    rows=lambda i:(i,0)
+        grad_ref[:,1]=dka_ref[...].astype(jnp.bfloat16)
+        grad_ref[:,2]=dva_ref[...].astype(jnp.bfloat16)
+
+def attend_back(start, joined, grad, out, lse):
+    parts,_,block,width=joined.shape
+    rows=lambda i:(i,0,0)
     cols=lambda i:(0,i)
+    one=pl.BlockSpec((1,1,block,width),lambda i:(i,0,0,0))
+    every=[pl.BlockSpec((parts,1,block,width),lambda i,at=at:(0,at,0,0)) for at in (1,2)]
     return pl.pallas_call(
-        partial(attend_back_kernel,block),
-        grid=(length//block,),
-        in_specs=[pl.BlockSpec((1,block),cols),pl.BlockSpec((block,width),rows),pl.BlockSpec((length,width),whole),pl.BlockSpec((length,width),whole),
-                  pl.BlockSpec((block,width),rows),pl.BlockSpec((block,width),rows),pl.BlockSpec((8,block),cols)],
-        out_specs=[pl.BlockSpec((block,width),rows),pl.BlockSpec((length,width),whole),pl.BlockSpec((length,width),whole)],
-        out_shape=[jax.ShapeDtypeStruct((length,width),jnp.bfloat16)]*3,
-        scratch_shapes=[pltpu.VMEM((width,length),jnp.bfloat16),pltpu.VMEM((length,width),jnp.float32),pltpu.VMEM((length,width),jnp.float32)],
+        attend_back_kernel,
+        grid=(parts,),
+        in_specs=[pl.BlockSpec((1,block),cols),one]+every+[pl.BlockSpec((1,block,width),rows),pl.BlockSpec((1,block,width),rows),pl.BlockSpec((8,block),cols)],
+        out_specs=pl.BlockSpec(joined.shape,lambda i:(0,0,0,0)),
+        out_shape=jax.ShapeDtypeStruct(joined.shape,jnp.bfloat16),
+        scratch_shapes=[pltpu.VMEM((parts,width,block),jnp.bfloat16),pltpu.VMEM((parts,block,width),jnp.float32),pltpu.VMEM((parts,block,width),jnp.float32)],
         compiler_params=pltpu.CompilerParams(vmem_limit_bytes=40<<20,dimension_semantics=("arbitrary",)),
-    )(start,queries,keys,values,grad,out,lse)
-
-def frame_kernel(gram_ref, span_ref, out_ref, work_ref, turn_ref):
+    )(start,joined,joined,joined,grad,out,lse)
+
+
+def join_kernel(rows_ref, weight_ref, bias_ref, out_ref):
+    width=out_ref.shape[3]
+    joined=lax.dot_general(rows_ref[...],weight_ref[...],LANES_BOTH,preferred_element_type=jnp.float32)
+    joined=(joined+bias_ref[...]).astype(jnp.bfloat16)
+    for place in range(out_ref.shape[0]):
+        out_ref[place,0]=joined[:,place*width:(place+1)*width]
+
+
+def join(rows, weights, bias, parts):
+    count,model_dim=rows.shape
+    width=model_dim//parts
+    pairs=parts//2
+    return pl.pallas_call(
+        join_kernel,
+        grid=(3,pairs),
+        in_specs=[pl.BlockSpec((count,model_dim),lambda p,h:(0,0)),
+                  pl.BlockSpec((2*width,model_dim),lambda p,h:(p*pairs+h,0)),
+                  pl.BlockSpec((1,2*width),lambda p,h:(0,p*pairs+h))],
+        out_specs=pl.BlockSpec((2,1,count,width),lambda p,h:(h,p,0,0)),
+        out_shape=jax.ShapeDtypeStruct((parts,3,count,width),jnp.bfloat16),
+        compiler_params=pltpu.CompilerParams(vmem_limit_bytes=40<<20,dimension_semantics=("arbitrary","arbitrary")),
+    )(rows,weights,bias)
+
+
+def frame_kernel(gram_ref, span_ref, out_ref, work_ref):
     count,size,_=gram_ref.shape
     work_ref[...]=gram_ref[...]
     out_ref[...]=span_ref[...]
-    sub=lax.broadcasted_iota(jnp.int32,(count,8,size),1)
+    rows=lax.broadcasted_iota(jnp.int32,(size,size),0)
+    sub=lax.broadcasted_iota(jnp.int32,(count,32,size),1)
     def panel(step, unused):
-        top=pl.multiple_of(step*8,8)
-        left=work_ref[:,pl.ds(top,8),:]
-        right=out_ref[:,pl.ds(top,8),:]
-        for k in range(8):
+        top=pl.multiple_of(step*32,32)
+        left=work_ref[:,pl.ds(top,32),:].reshape(count*32,size)
+        left=pltpu.roll(left,(size-top)%size,1).reshape(count,32,size)
+        right=out_ref[:,pl.ds(top,32),:]
+        for k in range(32):
             column=left[:,:,k:k+1]
             pivot=column[:,k:k+1,:]
             inverse=lax.rsqrt(pivot)
             inverse=inverse*(1.5-0.5*pivot*inverse*inverse)
             row_left=left[:,k:k+1,:]*inverse
             row_right=right[:,k:k+1,:]*inverse
-            share=column*inverse
-            left=jnp.where(sub>k,left-share*row_left,jnp.where(sub==k,row_left,left))
-            right=jnp.where(sub>k,right-share*row_right,jnp.where(sub==k,row_right,right))
-        out_ref[:,pl.ds(top,8),:]=right
-        for b in range(count):
-            spread=jnp.concatenate([left[b],jnp.zeros((size-8,size),jnp.float32)],0)
-            turn_ref[b]=spread.T
-        turned_left=pltpu.roll(left.reshape(count*8,size),size-8,1).reshape(count,8,size)
-        def trail(place, unused):
-            row=pl.multiple_of(place*8,8)
-            shares=turn_ref[:,pl.ds(pl.multiple_of(row-top,8),8),:]
-            below_left=pltpu.roll(work_ref[:,pl.ds(row,8),:].reshape(count*8,size),size-8,1).reshape(count,8,size)
-            below_right=out_ref[:,pl.ds(row,8),:]
-            for k in range(8):
-                share=shares[:,:,k:k+1]
-                below_left=below_left-share*turned_left[:,k:k+1,:]
-                below_right=below_right-share*right[:,k:k+1,:]
-            work_ref[:,pl.ds(row,8),:]=below_left
-            out_ref[:,pl.ds(row,8),:]=below_right
-            return unused
-        return lax.fori_loop(step+1,size//8,trail,unused)
-    lax.fori_loop(0,size//8,panel,0)
+            share=jnp.where(sub>k,column*inverse,0.0)
+            left=jnp.where(sub==k,row_left,left-share*row_left)
+            right=jnp.where(sub==k,row_right,right-share*row_right)
+        out_ref[:,pl.ds(top,32),:]=right
+        left=pltpu.roll(left.reshape(count*32,size),top,1).reshape(count,32,size)
+        below=rows>=top+32
+        @pl.when(step<size//32-1)
+        def _():
+            for b in range(count):
+                for ref,part in ((work_ref,left[b]),(out_ref,right[b])):
+                    change=lax.dot_general(left[b],part,(((0,),(0,)),((),())),precision=lax.Precision.HIGHEST,preferred_element_type=jnp.float32)
+                    ref[b]=jnp.where(below,ref[b]-change,ref[b])
+        return unused
+    lax.fori_loop(0,size//32,panel,0)
 
 def frame(gram, span):
     return pl.pallas_call(
         frame_kernel,
         out_shape=jax.ShapeDtypeStruct(gram.shape,jnp.float32),
-        scratch_shapes=[pltpu.VMEM(gram.shape,jnp.float32),pltpu.VMEM(gram.shape,jnp.float32)],
+        scratch_shapes=[pltpu.VMEM(gram.shape,jnp.float32)],
         compiler_params=pltpu.CompilerParams(vmem_limit_bytes=40<<20),
     )(gram,span)
 
@@ -531,10 +567,9 @@
         return jnp.where(inside, one, jnp.where(both, two + vocab_rows, -1))
 
     def of_this_b(tensor):
-        shaped = pick(tensor.reshape(2, 2, ways, 2, -1, tensor.shape[-1]), at_b, 1)
-        return own_first(own_first(shaped, at_a, 0), at_x, 2)
-
-    own_ids = of_this_b(token_ids)
+        return pick(tensor.reshape(2, 2, ways, 2, -1, tensor.shape[-1]), at_b, 1)
+
+    own_ids = own_first(own_first(of_this_b(token_ids), at_a, 0), at_x, 2)
     near_ids = in_order(at_c, own_ids, swap(own_ids, "core"), 4)
     all_ids = in_order(at_y, near_ids, swap(near_ids, "y"), 4).swapaxes(3, 4)
 
@@ -544,13 +579,15 @@
         return got.reshape(2, ways, tok_rows, -1)
 
     near = [looked_up(own_ids[at], table_near) for at in (1, 0)]
-    far_low = order.hold(far_low, near[0])
-    far_other = order.hold(swap(other_low, "y"), near[1])
+    near = over_x(*near)
+    far_low = order.hold(far_low, near)
+    far_other = order.hold(swap(other_low, "y"), near)
     pair = in_order(at_b, far_low, far_other, 0)
     table_far = in_order(at_c, pair, swap(pair, "core"), 1)
     far = [looked_up(own_ids[at], table_far) for at in (1, 0)]
-    half_near = to_group(*near)
-    half_far = to_group(*far)
+    far = over_x(*far)
+    half_near = added(near[0], swap(near[1], "za"))
+    half_far = added(far[0], swap(far[1], "za"))
     embedded = in_order(at_y, half_near, half_far, 1)
     table_full = in_order(at_y, table_near, table_far, 1)
 
@@ -562,25 +599,12 @@
     ).astype(jnp.int32)[None]
 
     normed_low = layer_norm(embedded, gain_one, shift_one).astype(jnp.bfloat16)
-    joined = low_dot(normed_low, gathered[: 3 * model_dim]) + jnp.concatenate(
-        [bias_q, jnp.zeros_like(bias_q), bias_v]
-    )
-    joined_heads = lax.all_to_all(
-        joined.astype(jnp.bfloat16).reshape(tok_rows, 3, part_count, head_width),
-        SEQ,
-        split_axis=2,
-        concat_axis=0,
-        tiled=True,
-    )
-    queries, key_rows, values = (joined_heads[:, at, 0] for at in range(3))
-    mixture, mixture_wide, logsum = attend(starts, queries, key_rows, values)
-    mixed_low = lax.all_to_all(
-        mixture.reshape(part_count, tok_rows, 1, head_width),
-        SEQ,
-        split_axis=0,
-        concat_axis=2,
-        tiled=True,
-    ).reshape(tok_rows, model_dim)
+    bias_joined = jnp.concatenate([bias_q, jnp.zeros_like(bias_q), bias_v])[None]
+    joined = join(normed_low, gathered, bias_joined, part_count)
+    joined = lax.all_to_all(joined, SEQ, split_axis=0, concat_axis=0, tiled=True)
+    mixture, mixture_wide, logsum = attend(starts, joined)
+    mixed_low = lax.all_to_all(mixture, SEQ, split_axis=0, concat_axis=0, tiled=True)
+    mixed_low = mixed_low.swapaxes(0, 1).reshape(tok_rows, model_dim)
     project_out = gathered[3 * model_dim : 4 * model_dim]
     expand_weight = gathered[4 * model_dim : 4 * model_dim + hidden_units]
     reduce_weight = gathered[4 * model_dim + hidden_units :]
@@ -596,36 +620,50 @@
         jnp.bfloat16
     )
 
-    head_rows = from_groups(chosen).reshape(-1, model_dim)
+    head_rows = in_order(at_a, chosen[None], swap(chosen, "za")[None], 0)
+    head_rows = in_order(at_x, head_rows[None], swap(head_rows, "x")[None], 0)
+    if ways > 1:
+        head_rows = lax.all_gather(head_rows, "w", axis=0, tiled=False)
+    head_rows = head_rows.reshape(-1, model_dim)
+
+    def of_rows(tensor):
+        return lax.optimization_barrier(of_this_b(tensor).transpose(1, 2, 0, 3, 4).reshape(-1))
+
     logits = low_dot(head_rows, table_full)
     if groups * vocab_rows > vocab_live:
         live = jnp.minimum(vocab_live - first_start, vocab_rows)
         live_two = vocab_live - first_start - plane_step
         kept = jnp.where(pair_range < vocab_rows, pair_range < live, pair_range - vocab_rows < live_two)
         logits = jnp.where(kept[None, :], logits, MASKED)
-    target_hot = pair_range[None, :] == in_pair(of_this_b(targets)).reshape(-1, 1)
+    target_hot = pair_range[None, :] == lax.optimization_barrier(in_pair(of_rows(targets)))[:, None]
     target_part = jnp.sum(jnp.where(target_hot, logits, 0.0), 1)
     local_peak = jnp.max(logits, 1)
     local_sum = jnp.sum(jnp.exp(logits - local_peak[:, None]), 1)
-    everyone = from_groups(jnp.stack([local_peak, local_sum, target_part]))
-    everyone = everyone.reshape(2, 2, ways, 3, 2, 2, -1)
-    aligned = []
-    for by_x in (0, 1):
-        for by_a in (0, 1):
-            turned = jnp.roll(everyone[by_x, by_a], (by_x, by_a), (2, 3))
-            aligned.append(turned.reshape(ways, 3, -1))
-    everyone = jnp.concatenate(aligned, 0)
-    peak_all = jnp.max(everyone[:, 0], 0)
-    sum_all = jnp.sum(everyone[:, 1] * jnp.exp(everyone[:, 0] - peak_all[None]), 0)
-    target_logit = jnp.sum(everyone[:, 2], 0)
-    logsum_all = peak_all + jnp.log(sum_all)
-    weight_rows = of_this_b(loss_flag).reshape(-1).astype(jnp.float32)
+    sums = jnp.stack([local_peak, local_sum, target_part])
+
+    def merged(one, two):
+        peak = jnp.maximum(one[0], two[0])
+        summed = one[1] * jnp.exp(one[0] - peak) + two[1] * jnp.exp(two[0] - peak)
+        return jnp.stack([peak, summed, one[2] + two[2]])
+
+    for name in ("za", "x"):
+        sums = merged(sums, swap(sums, name))
+    if ways > 1:
+        everyone = lax.all_gather(sums, "w", axis=0, tiled=False)
+        sums = everyone[0]
+        for way in range(1, ways):
+            sums = merged(sums, everyone[way])
+    logsum_all = sums[0] + jnp.log(sums[1])
+    target_logit = sums[2]
+    weight_rows = of_rows(loss_flag).astype(jnp.float32)
     chance = jnp.exp(logits - logsum_all[:, None])
     grad_logits = weight_rows[:, None] * (chance - target_hot.astype(jnp.float32))
     grad_low = grad_logits.astype(jnp.bfloat16)
     grad_rows = plain_dot(grad_low, table_full).astype(jnp.bfloat16)
-    grad_rows = grad_rows.reshape(2, 2, ways, loss_rows, model_dim)
-    grad_chosen = to_group(grad_rows[1], grad_rows[0])
+    grad_rows = grad_rows.reshape(ways, 2, 2, loss_rows, model_dim)
+    grad_rows = [pick(grad_rows, side, 1).swapaxes(0, 1) for side in (1 - at_x, at_x)]
+    grad_chosen = over_x(*grad_rows)
+    grad_chosen = added(pick(grad_chosen, at_a), swap(pick(grad_chosen, 1 - at_a), "za"))
 
     def table_part(by_y, by_c):
         place = (at_y ^ by_y) * 2 + (at_c ^ by_c)
@@ -655,21 +693,13 @@
     plane_rows = layer_weight.shape[0] * groups * part_count // PLANES
     reduce_cut = hidden_units - plane_rows
     plane_three = outer_dot(active_low[:, reduce_cut:], resid_low, jnp.bfloat16)
-    piece_three = reduce_plane(plane_three)
+    piece_three = reduce_planes(by_owner(plane_three, 1))
     resid_low = order.hold(resid_low, plane_three)
     grad_active = low_dot(resid_low, reduce_weight)
     unused, gelu_back = jax.vjp(smooth, hidden)
     hidden_low = gelu_back(grad_active)[0].astype(jnp.bfloat16)
     grad_bias_up = column_sum(hidden_low)
-    half = plane_rows - model_dim
-    plane_two = jnp.concatenate(
-        [
-            outer_dot(hidden_low[:, half:], normed_two_low, jnp.bfloat16),
-            outer_dot(active_low[:, :reduce_cut], resid_low, jnp.bfloat16),
-        ],
-        0,
-    )
-    piece_two = reduce_plane(plane_two)
+    hidden_low = order.hold(hidden_low, head_table_grad)
     unused, two_back = jax.vjp(layer_norm, middle, gain_two, shift_two)
     grad_middle_part, grad_gain_two, grad_shift_two = two_back(plain_dot(hidden_low, expand_weight))
     grad_middle = grad_resid + grad_middle_part
@@ -677,88 +707,86 @@
     grad_bias_out = column_sum(middle_low)
     grad_mixed = plain_dot(middle_low, project_out)
     grad_heads = lax.all_to_all(
-        grad_mixed.astype(jnp.bfloat16).reshape(tok_rows, part_count, head_width),
+        grad_mixed.astype(jnp.bfloat16).reshape(tok_rows, part_count, head_width).swapaxes(0, 1),
         SEQ,
-        split_axis=1,
+        split_axis=0,
         concat_axis=0,
         tiled=True,
-    )[:, 0]
-    core_one = scatter_core(
+    )
+    def once(*earlier):
+        return lambda tensor: order.hold(tensor, *earlier)
+
+    between = by_owner(
         jnp.concatenate(
             [
                 outer_dot(middle_low, mixed_low, jnp.bfloat16),
-                outer_dot(hidden_low[:, :half], normed_two_low, jnp.bfloat16),
+                outer_dot(hidden_low, normed_two_low, jnp.bfloat16),
+                outer_dot(active_low[:, :reduce_cut], resid_low, jnp.bfloat16),
             ],
             0,
-        )
-    )
-    grad_heads = order.hold(grad_heads, plane_two)
-    grad_query, grad_keys, grad_values = attend_back(
-        starts, queries, key_rows, values, grad_heads, mixture_wide, logsum
-    )
-    grad_heads = order.hold(jnp.stack([grad_query, grad_keys, grad_values], 1), core_one)
-    grad_joined = lax.all_to_all(
-        grad_heads.reshape(part_count, tok_rows, 3, 1, head_width),
-        SEQ,
-        split_axis=0,
-        concat_axis=3,
-        tiled=True,
-    ).reshape(tok_rows, 3 * model_dim)
+        ),
+        2,
+    )
+    pieces_between = reduce_planes(between)
+    grad_heads = order.hold(grad_heads, between)
+    grad_joined = attend_back(starts, joined, grad_heads, mixture_wide, logsum)
+    grad_joined = lax.all_to_all(grad_joined, SEQ, split_axis=0, concat_axis=0, tiled=True)
+    grad_joined = order.hold(grad_joined, piece_three)
+    grad_joined = grad_joined.transpose(2, 1, 0, 3).reshape(tok_rows, 3 * model_dim)
     core_zero = scatter_core(outer_dot(grad_joined, normed_low, jnp.bfloat16))
     unused, one_back = jax.vjp(layer_norm, embedded, gain_one, shift_one)
-    grad_embed_part, grad_gain_one, grad_shift_one = one_back(plain_dot(grad_joined, gathered[: 3 * model_dim]))
+    grad_embed_part, grad_gain_one, grad_shift_one = one_back(
+        plain_dot(grad_joined, gathered[: 3 * model_dim])
+    )
     rows_back = (grad_middle + grad_embed_part).astype(jnp.bfloat16)
-    first_one = scatter_first(order.hold(core_one, grad_joined))
-    rows_back = order.hold(rows_back, core_zero)
     rows_back = lax.all_to_all(rows_back, SEQ, split_axis=1, concat_axis=0, tiled=True)
     grad_bias_q = column_sum(grad_joined[:, :model_dim])
     grad_bias_v = column_sum(grad_joined[:, 2 * model_dim :])
-    first_zero = scatter_first(core_zero)
-    second_one = scatter_second(first_one)
-    second_zero = scatter_second(first_zero)
+    rows_back = rows_back.reshape(2, length // 2, slice_width)
+
+    from_all = [from_groups(rows_back[0])]
+    first_zero = scatter_first(order.hold(core_zero, rows_back))
+    from_all.append(from_groups(order.hold(rows_back[1], core_zero), once(first_zero)))
+    second_zero = scatter_second(first_zero, once(from_all[0]))
+    piece_zero = scatter_last(second_zero, once(from_all[1]))
+    totals = jnp.concatenate(
+        [
+            grad_bias_q,
+            grad_bias_v,
+            grad_bias_out,
+            grad_bias_up,
+            grad_bias_down,
+            grad_gain_one,
+            grad_shift_one,
+            grad_gain_two,
+            grad_shift_two,
+            grad_gain_final,
+            grad_shift_final,
+            jnp.stack([loss_part, count_part]),
+        ]
+    )
+    totals = total_of(order.hold(totals, from_all[1]))
+    small_grad, loss_sum, loss_count = totals[:-2], totals[-2], totals[-1]
     row_range = jnp.arange(vocab_rows, dtype=jnp.int32)[:, None]
     sides = {"mine": at_b, "theirs": 1 - at_b}
     spread = {
         name: lax.dynamic_slice_in_dim(head_table_grad, side * vocab_rows, vocab_rows, 0)
         for name, side in sides.items()
     }
-    rows_back = rows_back.reshape(2, length // 2, slice_width)
     id_halves = all_ids.reshape(2, 2, ways, 2, length // 2)
     for at in range(2):
-        got = from_groups(rows_back[at], order, (first_one, first_zero)[at])
-        got = order.hold(got, (second_one, second_zero)[at]).reshape(-1, slice_width)
+        got = from_all[at].reshape(-1, slice_width)
         ids = id_halves[:, :, :, at].reshape(1, -1) - first_start
         for name, side in sides.items():
             hot = (row_range == ids - side * plane_step).astype(jnp.bfloat16)
             spread[name] = spread[name] + plain_dot(hot, got)
     table_grad = added(spread["mine"], swap(spread["theirs"].astype(jnp.bfloat16), "zb"))
-    piece_one = scatter_last(second_one)
-    piece_zero = scatter_last(second_zero)
-    quarters = jnp.stack([piece_zero, piece_one, piece_two, piece_three])
+    quarters = jnp.concatenate([piece_zero[None], pieces_between, piece_three], 0)
     layer_grad = jnp.stack(sent_z([pick(quarters, plane) for plane in planes_from_here()]))
-    squares = jnp.sum(jnp.square(layer_grad.astype(jnp.float32))) + jnp.sum(
-        table_grad * table_grad
-    )
-    totals = total_of(
-        jnp.concatenate(
-            [
-                grad_bias_q,
-                grad_bias_v,
-                grad_bias_out,
-                grad_bias_up,
-                grad_bias_down,
-                grad_gain_one,
-                grad_shift_one,
-                grad_gain_two,
-                grad_shift_two,
-                grad_gain_final,
-                grad_shift_final,
-                jnp.stack([squares, loss_part, count_part]),
-            ]
-        )
-    )
-    squares, loss_sum, loss_count = totals[-3], totals[-2], totals[-1] + order.zero()
-    small_grad = totals[:-3]
+    squares = total_at_once(
+        jnp.sum(jnp.square(layer_grad.astype(jnp.float32))) + jnp.sum(table_grad * table_grad)
+    )
+    loss_count = loss_count + order.zero()
     gradient_norm = jnp.sqrt(squares + jnp.sum(small_grad * small_grad))
     factor = 1.0 / jnp.maximum(gradient_norm, 1.0)
     out_bias_grad = factor * small_grad[2 * model_dim : 3 * model_dim]

time: 1110 us -> 1100 us (level); the launches traced: 1100 us -> 1080 us
  waiting for transfers between devices: 527 us -> 500 us
    ppermute x4 -> x2, waiting for transfers between devices: 81.4 us -> 11.1 us  [flip(): return lax.ppermute(tensor, ('x', 'y', 'core'), pairs)]
    all_gather x1, waiting for transfers between devices: 19.2 us -> 49.7 us  [body(): gathered = lax.all_gather(weight_low, ALL, axis=0, tiled=True)]
    pallas_call x1, Pallas kernels: 37.6 us -> 18.1 us  [frame(): pl.pallas_call(frame_kernel, out_shape=jax.ShapeDtypeStruct(gram.shape, j...]
    ppermute x9 -> x6, waiting for transfers between devices: 34.6 us -> 17.3 us  [shift(): lax.ppermute(tensor, PLANE, [(i, (i + step) % PLANES) for i in range(PLAN...]
    ppermute x36 -> x33, waiting for transfers between devices: 291 us -> 307 us  [swap(): return lax.ppermute(tensor, axis, [(0, 1), (1, 0)])]
    pallas_call x2 -> x3, Pallas kernels: 42.6 us -> 55.8 us  [the longest x1 31.4 us: attend_back(): pl.pallas_call(attend_back_kernel, grid=(parts,), in_specs=[pl.BlockSpec(...]
    all_to_all x3 -> x4, waiting for transfers between devices: 72.9 us -> 85.6 us  [the longest x1 34.4 us: body(): lax.all_to_all(joined, SEQ, split_axis=0, concat_axis=0, tiled=True)]
    unnamed x207 -> x231, local copies, waits for them, and re-layouts: 33.4 us -> 45.5 us
  transfers between devices with their start and end apart: 57 -> 50, of which waited for: 34 -> 28; matrix products, arithmetic and copies ran while one was open for 25% -> 24% of each run, Pallas kernels for 3% -> 3%
where the time goes in v3:
time: 1100 us; the launch traced here: 1080 us
  waiting for transfers between devices  500 us (45%)
  matrix products  179 us (16%)
  local copies, waits for them, and re-layouts  115 us (10%)
  Pallas kernels  93.1 us (8%)
  other arithmetic  92.3 us (8%)
  starting transfers between devices  70.3 us (6%)
  between operations  33.3 us (3%)
    ppermute x33, waiting for transfers between devices, swap(): return lax.ppermute(tensor, axis, [(0, 1), (1, 0)])  307 us
    dot_general x14, matrix products, plain_dot(): return jnp.dot(left, right, preferred_element_type=jnp.float32)  88.5 us
    all_gather x1, waiting for transfers between devices, body(): gathered = lax.all_gather(weight_low, ALL, axis=0, tiled=True)  49.7 us
    unnamed x231, local copies, waits for them, and re-layouts  45.5 us
    dot_general x9, matrix products, outer_dot(): lax.dot_general(left, right, (((0,), (0,)), ((), ())), preferred_element_...  44.7 us
    dot_general x4, matrix products, low_dot(): lax.dot_general(left, right, LANES_BOTH, preferred_element_type=jnp.float32)  43.4 us
    ppermute x33, starting transfers between devices, swap(): return lax.ppermute(tensor, axis, [(0, 1), (1, 0)])  35 us
    all_to_all x1, waiting for transfers between devices, body(): lax.all_to_all(joined, SEQ, split_axis=0, concat_axis=0, tiled=True)  34.4 us
  transfers between devices with their start and end apart: 50, of which 28 were waited for; matrix products, arithmetic and copies ran while one was open for 24% of the time, Pallas kernels for 3%

profile of v3, /device:TPU:0, one launch (start us, length us, event | category | flops | bytes accessed | tf_op | source)
XLA Modules:
  0.0 1082.9 jit_solution(974005492770980357)
XLA Ops:
  13.5 47.8 %collective-permute-done = bf16[1576,320]{0,1:T(8,128)(2,1)} collective-permute-done((bf16[1576,320]{0,1:T(8,128)(2,1)S(1)}, bf16[1576,320]{0,1:T(8,128)(2,1)}, u32[]{:S(2)}, u32[]{:S(2)}) %collective-permute-start) | collective-permute-done | bytes 1008672 | tf_op jit(solution)/shard_map/ppermute | solution.py:69
  85.4 37.0 %collective-permute-done.2 = bf16[2,1,384,640]{3,2,1,0:T(8,128)(2,1)S(1)} collective-permute-done((bf16[2,1,384,640]{3,2,1,0:T(8,128)(2,1)S(1)}, bf16[2,1,384,640]{3,2,1,0:T(8,128)(2,1)S(1)}, u32[]{:S(2)}, u32[]{:S(2)}) %collective-permute-start.2) | collective-permute-done | bytes 983072 | tf_op jit(solution)/shard_map/ppermute | solution.py:69
  123.2 12.7 %collective-permute-done.5 = bf16[1576,320]{0,1:T(8,128)(2,1)S(1)} collective-permute-done((bf16[1576,320]{0,1:T(8,128)(2,1)}, bf16[1576,320]{0,1:T(8,128)(2,1)S(1)}, u32[]{:S(2)}, u32[]{:S(2)}) %collective-permute-start.5) | collective-permute-done | bytes 1008672 | tf_op jit(solution)/shard_map/ppermute | solution.py:69
  156.8 32.0 %collective-permute-done.7 = bf16[2,1,384,640]{3,2,1,0:T(8,128)(2,1)S(1)} collective-permute-done((bf16[2,1,384,640]{3,2,1,0:T(8,128)(2,1)S(1)}, bf16[2,1,384,640]{3,2,1,0:T(8,128)(2,1)S(1)}, u32[]{:S(2)}, u32[]{:S(2)}) %collective-permute-start.7) | collective-permute-done | bytes 983072 | tf_op jit(solution)/shard_map/ppermute | solution.py:69
  192.7 25.8 %collective-permute-done.3 = bf16[384,640]{1,0:T(8,128)(2,1)S(1)} collective-permute-done((bf16[384,640]{1,0:T(8,128)(2,1)S(1)}, bf16[384,640]{1,0:T(8,128)(2,1)S(1)}, u32[]{:S(2)}, u32[]{:S(2)}) %collective-permute-start.3) | collective-permute-done | bytes 491552 | tf_op jit(solution)/shard_map/ppermute | solution.py:69
  218.5 33.3 %collective-permute-done.8 = bf16[384,640]{1,0:T(8,128)(2,1)} collective-permute-done((bf16[384,640]{1,0:T(8,128)(2,1)S(1)}, bf16[384,640]{1,0:T(8,128)(2,1)}, u32[]{:S(2)}, u32[]{:S(2)}) %collective-permute-start.8) | collective-permute-done | bytes 491552 | tf_op jit(solution)/shard_map/ppermute | solution.py:69
  255.4 49.7 %all-gather.2.cloned.1.call-done.weight_ref = bf16[15360,1280]{1,0:T(8,128)(2,1)} async-done(((bf16[480,1280]{1,0:T(8,128)(2,1)}), bf16[15360,1280]{1,0:T(8,128)(2,1)}) %all-gather.2.cloned.1.call-update) | async-done | bytes 39321616 | tf_op jit(solution)/shard_map/all_gather | solution.py:551
  324.8 34.4 %all-to-all-done = bf16[4,3,384,320]{2,3,1,0:T(8,128)(2,1)} async-done(((bf16[4,3,384,320]{2,3,1,0:T(8,128)(2,1)}), bf16[4,3,384,320]{2,3,1,0:T(8,128)(2,1)}, u32[]{:S(2)}, u32[]{:S(2)}) %all-to-all-start) | async-done | bytes 2949152 | tf_op jit(solution)/shard_map/all_to_all | solution.py:604
  363.6 15.6 %shard_map.272 = (bf16[4,384,320]{2,1,0:T(8,128)(2,1)S(1)}, f32[4,384,320]{2,1,0:T(8,128)S(1)}, f32[8,1536]{1,0:T(8,128)S(1)}) custom-call(s32[1,1536]{1,0:T(1,128)S(1)} %broadcast_in_dim.68.start_ref, bf16[4,3,384,320]{3,2,1,0:T(8,128)(2,1)S(1)} %copy.117.q_ref.k_ref.v_ref, bf16[4,3,384,320]{3,2,1,0:T(8,128)(2,1)S(1)} %copy.117.q_ref.k_ref.v_ref, ...), custom_call_target="tpu_custom_call" | custom-call | tf_op jit(solution)/shard_map/pallas_call | solution.py:276
  390.8 11.8 %all-to-all-done.1 = bf16[4,384,320]{1,2,0:T(8,128)(2,1)} async-done(((bf16[4,384,320]{1,2,0:T(8,128)(2,1)}), bf16[4,384,320]{1,2,0:T(8,128)(2,1)}, u32[]{:S(2)}, u32[]{:S(2)}) %all-to-all-start.1) | async-done | bytes 983072 | tf_op jit(solution)/shard_map/all_to_all | solution.py:606
  408.1 12.0 %multiply_convert_fusion = (bf16[384,5120]{1,0:T(8,128)(2,1)S(1)}, f32[384,5120]{1,0:T(8,128)}) fusion(f32[5120]{0:T(1024)S(1)} %copy-done.78, bf16[15360,1280]{1,0:T(8,128)(2,1)} %all-gather.2.cloned.1.call-done.weight_ref, f32[384,1280]{1,0:T(8,128)S(1)} %get-tuple-element.279, f32[1280]{0:T(1024)S(1)} %copy-done.102, f32[1280]{0:T(1024)S(1)} %copy-done.74, ...), kind=kOutput, calls=%fused_computation.42 | convolution fusion | flops 5055283200 | bytes 26903552 | tf_op jit(solution)/shard_map/dot_general | solution.py:46
  484.6 12.0 %convolution_convert_fusion.4 = bf16[256,1280]{1,0:T(8,128)(2,1)S(1)} fusion(bf16[256,3152]{0,1:T(8,128)(2,1)S(1)} %multiply_convert_fusion.1, bf16[3152,640]{0,1:T(8,128)(2,1)} %copy-done.48, bf16[3152,640]{0,1:T(8,128)(2,1)S(1)} %copy-done.47, pred[]{:T(512)S(6)} %eq.71), kind=kOutput, calls=%fused_computation.79 | convolution fusion | flops 2102333440 | bytes 10338305 | tf_op jit(solution)/shard_map/dot_general | solution.py:50
  544.7 17.3 %convert_reduce_fusion = (f32[5120]{0:T(1024)}, bf16[384,5120]{1,0:T(8,128)(2,1)S(1)}) fusion(f32[384,5120]{1,0:T(8,128)} %get-tuple-element.281, bf16[384,1280]{1,0:T(8,128)(2,1)} %copy-done.53, bf16[15360,1280]{1,0:T(8,128)(2,1)} %all-gather.2.cloned.1.call-done.weight_ref), kind=kOutput, calls=%fused_computation.41 | convolution fusion | flops 5076413440 | bytes 25907200 | tf_op jit(solution)/shard_map/dot_general | solution.py:46
  567.8 16.3 %collective-permute-done.19 = bf16[3152,320]{0,1:T(8,128)(2,1)S(1)} collective-permute-done((bf16[3152,320]{0,1:T(8,128)(2,1)}, bf16[3152,320]{0,1:T(8,128)(2,1)S(1)}, u32[]{:S(2)}, u32[]{:S(2)}) %collective-permute-start.19) | collective-permute-done | bytes 2017312 | tf_op jit(solution)/shard_map/ppermute | solution.py:69
  650.4 12.6 %all-to-all-done.2 = bf16[4,384,320]{1,2,0:T(8,128)(2,1)} async-done(((bf16[4,384,320]{1,2,0:T(8,128)(2,1)}), bf16[4,384,320]{1,2,0:T(8,128)(2,1)}, u32[]{:S(2)}, u32[]{:S(2)}) %all-to-all-start.2) | async-done | bytes 983072 | tf_op jit(solution)/shard_map/all_to_all | solution.py:709
  669.1 31.4 %shard_map.273 = bf16[4,3,384,320]{3,2,1,0:T(8,128)(2,1)S(1)} custom-call(s32[1,1536]{1,0:T(1,128)S(1)} %broadcast_in_dim.68.start_ref, bf16[4,3,384,320]{3,2,1,0:T(8,128)(2,1)S(1)} %copy.117.q_ref.k_ref.v_ref, bf16[4,3,384,320]{3,2,1,0:T(8,128)(2,1)S(1)} %copy.117.q_ref.k_ref.v_ref, bf16[4,3,384,320]{3,2,1,0:T(8,128)(2,1)S(1)} %copy.117.q_ref.k_ref.v_ref, ...), custom_call_target="tpu_custom_call" | custom-call | tf_op jit(solution)/shard_map/pallas_call | solution.py:347
  713.9 33.6 %all-to-all-done.3 = bf16[4,3,384,320]{2,3,1,0:T(8,128)(2,1)S(1)} async-done(((bf16[4,3,384,320]{2,3,1,0:T(8,128)(2,1)}), bf16[4,3,384,320]{2,3,1,0:T(8,128)(2,1)S(1)}, u32[]{:S(2)}, u32[]{:S(2)}) %all-to-all-start.3) | async-done | bytes 2949152 | tf_op jit(solution)/shard_map/all_to_all | solution.py:733
  775.6 16.8 %all-to-all-done.4 = bf16[384,4,320]{0,2,1:T(8,128)(2,1)S(1)} async-done(((bf16[384,4,320]{0,2,1:T(8,128)(2,1)}), bf16[384,4,320]{0,2,1:T(8,128)(2,1)S(1)}, u32[]{:S(2)}, u32[]{:S(2)}) %all-to-all-start.4) | async-done | bytes 983072 | tf_op jit(solution)/shard_map/all_to_all | solution.py:742
  809.5 22.6 %collective-permute-done.31 = bf16[1,768,320]{1,2,0:T(8,128)(2,1)} collective-permute-done((bf16[1,768,320]{1,2,0:T(8,128)(2,1)}, bf16[1,768,320]{1,2,0:T(8,128)(2,1)}, u32[]{:S(2)}, u32[]{:S(2)}) %collective-permute-start.31) | collective-permute-done | bytes 491552 | tf_op jit(solution)/shard_map/ppermute | solution.py:69
  847.7 35.4 %collective-permute-done.21 = bf16[1,768,320]{1,2,0:T(8,128)(2,1)} collective-permute-done((bf16[1,768,320]{1,2,0:T(8,128)(2,1)S(1)}, bf16[1,768,320]{1,2,0:T(8,128)(2,1)}, u32[]{:S(2)}, u32[]{:S(2)}) %collective-permute-start.21) | collective-permute-done | bytes 491552 | tf_op jit(solution)/shard_map/ppermute | solution.py:69
  951.7 13.6 %collective-permute-done.35 = bf16[120,1280]{1,0:T(8,128)(2,1)S(1)} collective-permute-done((bf16[120,1280]{1,0:T(8,128)(2,1)S(1)}, bf16[120,1280]{1,0:T(8,128)(2,1)S(1)}, u32[]{:S(2)}, u32[]{:S(2)}) %collective-permute-start.35) | collective-permute-done | bytes 307232 | tf_op jit(solution)/shard_map/ppermute | solution.py:76
  974.4 18.3 %collective-permute-done.40 = bf16[1576,320]{0,1:T(8,128)(2,1)} collective-permute-done((bf16[1576,320]{0,1:T(8,128)(2,1)}, bf16[1576,320]{0,1:T(8,128)(2,1)}, u32[]{:S(2)}, u32[]{:S(2)}) %collective-permute-start.40) | collective-permute-done | bytes 1008672 | tf_op jit(solution)/shard_map/ppermute | solution.py:69
  1028.1 19.2 %shard_map.274 = (f32[480,1280]{1,0:T(8,128)}, f32[480,1280]{1,0:T(8,128)}, f32[480,1280]{1,0:T(8,128)}, f32[1,10,128,128]{3,2,1,0:T(8,128)}, f32[10,128,128]{2,1,0:T(8,128)S(1)}, /*index=5*/f32[10,128,128]{2,1,0:T(8,128)S(1)}) custom-call(s32[1]{0:T(128)} %bitcast.107.place_ref, f32[1,1]{1,0:T(1,128)} %bitcast.108.factor_ref, f32[480,1280]{1,0:T(8,128)S(1)} %copy-done.3, ...), custom_call_target="tpu_custom_call" | custom-call | tf_op jit(solution)/shard_map/pallas_call | solution.py:488
  1047.3 18.1 %shard_map.275 = f32[10,128,128]{2,1,0:T(8,128)S(1)} custom-call(f32[10,128,128]{2,1,0:T(8,128)S(1)} %get-tuple-element.94.gram_ref, f32[10,128,128]{2,1,0:T(8,128)S(1)} %get-tuple-element.95.span_ref), custom_call_target="tpu_custom_call" | custom-call | tf_op jit(solution)/shard_map/pallas_call | solution.py:416
  (491 shorter events, 470.6 us)
Async XLA Ops:
  7.2 297.9 %all-gather.2.cloned.1.call-start = ((), (), s32[]{:S(2)}) async-start(), calls=%async_computation.8 | async-start | bytes 40550400 | tf_op jit(solution)/shard_map/all_gather | solution.py:551
  10.4 50.9 %collective-permute-start = (bf16[1576,320]{0,1:T(8,128)(2,1)S(1)}, bf16[1576,320]{0,1:T(8,128)(2,1)}, u32[]{:S(2)}, u32[]{:S(2)}) collective-permute-start(bf16[1576,320]{0,1:T(8,128)(2,1)S(1)} %convert_element_type.331), channel_id=1, source_target_pairs={{0,8},{8,0},{1,9},{9,1},{2,10},{10,2},{3,11},{11,3},{4,12},{12,4},... | collective-permute-start | bytes 3025928 | tf_op jit(solution)/shard_map/ppermute | solution.py:69
  76.7 45.7 %collective-permute-start.2 = (bf16[2,1,384,640]{3,2,1,0:T(8,128)(2,1)S(1)}, bf16[2,1,384,640]{3,2,1,0:T(8,128)(2,1)S(1)}, u32[]{:S(2)}, u32[]{:S(2)}) collective-permute-start(bf16[2,1,384,640]{3,2,1,0:T(8,128)(2,1)S(1)} %bitcast.276), channel_id=1, source_target_pairs={{0,4},{4,0},{1,5},{5,1},{2,6},{6,2},{3,7},{7,3},{8,12},{12,8},{9,1... | collective-permute-start | bytes 2949128 | tf_op jit(solution)/shard_map/ppermute | solution.py:69
  78.9 57.0 %collective-permute-start.4 = (bf16[1576,320]{0,1:T(8,128)(2,1)S(1)}, bf16[1576,320]{0,1:T(8,128)(2,1)S(1)}, u32[]{:S(2)}, u32[]{:S(2)}) collective-permute-start(bf16[1576,320]{0,1:T(8,128)(2,1)S(1)} %convert_element_type.331), channel_id=1, source_target_pairs={{0,2},{2,0},{1,3},{3,1},{4,6},{6,4},{5,7},{7,5},{8,10},{10,8},{9,1... | collective-permute-start | bytes 3025928 | tf_op jit(solution)/shard_map/ppermute | solution.py:69
  80.5 55.4 %collective-permute-start.5 = (bf16[1576,320]{0,1:T(8,128)(2,1)}, bf16[1576,320]{0,1:T(8,128)(2,1)S(1)}, u32[]{:S(2)}, u32[]{:S(2)}) collective-permute-start(bf16[1576,320]{0,1:T(8,128)(2,1)} %collective-permute-done), channel_id=1, source_target_pairs={{0,2},{2,0},{1,3},{3,1},{4,6},{6,4},{5,7},{7,5},{8,10},{10,8},{9,1... | collective-permute-start | bytes 3025928 | tf_op jit(solution)/shard_map/ppermute | solution.py:69
  148.2 40.5 %collective-permute-start.7 = (bf16[2,1,384,640]{3,2,1,0:T(8,128)(2,1)S(1)}, bf16[2,1,384,640]{3,2,1,0:T(8,128)(2,1)S(1)}, u32[]{:S(2)}, u32[]{:S(2)}) collective-permute-start(bf16[2,1,384,640]{3,2,1,0:T(8,128)(2,1)S(1)} %bitcast.277), channel_id=1, source_target_pairs={{0,4},{4,0},{1,5},{5,1},{2,6},{6,2},{3,7},{7,3},{8,12},{12,8},{9,1... | collective-permute-start | bytes 2949128 | tf_op jit(solution)/shard_map/ppermute | solution.py:69
  149.8 68.6 %collective-permute-start.3 = (bf16[384,640]{1,0:T(8,128)(2,1)S(1)}, bf16[384,640]{1,0:T(8,128)(2,1)S(1)}, u32[]{:S(2)}, u32[]{:S(2)}) collective-permute-start(bf16[384,640]{1,0:T(8,128)(2,1)S(1)} %slice_bitcast_fusion.3), channel_id=1, source_target_pairs={{0,16},{16,0},{1,17},{17,1},{2,18},{18,2},{3,19},{19,3},{4,20},{20... | collective-permute-start | bytes 1474568 | tf_op jit(solution)/shard_map/ppermute | solution.py:69
  189.1 62.8 %collective-permute-start.8 = (bf16[384,640]{1,0:T(8,128)(2,1)S(1)}, bf16[384,640]{1,0:T(8,128)(2,1)}, u32[]{:S(2)}, u32[]{:S(2)}) collective-permute-start(bf16[384,640]{1,0:T(8,128)(2,1)S(1)} %slice_bitcast_fusion.1), channel_id=1, source_target_pairs={{0,16},{16,0},{1,17},{17,1},{2,18},{18,2},{3,19},{19,3},{4,20},{20... | collective-permute-start | bytes 1474568 | tf_op jit(solution)/shard_map/ppermute | solution.py:69
  319.4 39.8 %all-to-all-start = ((bf16[4,3,384,320]{2,3,1,0:T(8,128)(2,1)}), bf16[4,3,384,320]{2,3,1,0:T(8,128)(2,1)}, u32[]{:S(2)}, u32[]{:S(2)}) async-start(bf16[4,3,384,320]{2,3,1,0:T(8,128)(2,1)} %copy.109), calls=%async_computation | async-start | bytes 5898240 | tf_op jit(solution)/shard_map/all_to_all | solution.py:604
  388.8 323.9 %reduce-scatter.3.cloned.1.call-start = ((), (), s32[]{:S(2)}) async-start(), calls=%async_computation.9 | async-start | bytes 10137600 | tf_op jit(solution)/shard_map/reduce_scatter | solution.py:139
  475.5 28.7 %collective-permute-start.17 = (s32[2,2,1,384,1]{3,4,1,0,2:T(1,128)}, s32[2,2,1,384,1]{3,4,1,0,2:T(1,128)}, u32[]{:S(2)}, u32[]{:S(2)}) collective-permute-start(s32[2,2,1,384,1]{3,4,1,0,2:T(1,128)} %pad_add_fusion), channel_id=1, source_target_pairs={{0,1},{1,0},{2,3},{3,2},{4,5},{5,4},{6,7},{7,6},{8,9},{9,8},{10,11... | collective-permute-start | bytes 18440 | tf_op jit(solution)/shard_map/ppermute | solution.py:69
  542.7 424.0 %reduce-scatter.5.cloned.1.call-start = ((), (), s32[]{:S(2)}) async-start(), calls=%async_computation.10 | async-start | bytes 20275200 | tf_op jit(solution)/shard_map/reduce_scatter | solution.py:139
  542.8 41.3 %collective-permute-start.19 = (bf16[3152,320]{0,1:T(8,128)(2,1)}, bf16[3152,320]{0,1:T(8,128)(2,1)S(1)}, u32[]{:S(2)}, u32[]{:S(2)}) collective-permute-start(bf16[3152,320]{0,1:T(8,128)(2,1)} %copy-done.52), channel_id=1, source_target_pairs={{0,2},{2,0},{1,3},{3,1},{4,6},{6,4},{5,7},{7,5},{8,10},{10,8},{9,1... | collective-permute-start | bytes 6051848 | tf_op jit(solution)/shard_map/ppermute | solution.py:69
  708.4 39.0 %all-to-all-start.3 = ((bf16[4,3,384,320]{2,3,1,0:T(8,128)(2,1)}), bf16[4,3,384,320]{2,3,1,0:T(8,128)(2,1)S(1)}, u32[]{:S(2)}, u32[]{:S(2)}) async-start(bf16[4,3,384,320]{2,3,1,0:T(8,128)(2,1)} %copy.121), calls=%async_computation.3 | async-start | bytes 5898240 | tf_op jit(solution)/shard_map/all_to_all | solution.py:733
  759.8 34.6 %collective-permute-start.20 = (bf16[1,2,2,480,1280]{4,3,2,1,0:T(8,128)(2,1)}, bf16[1,2,2,480,1280]{4,3,2,1,0:T(8,128)(2,1)}, u32[]{:S(2)}, u32[]{:S(2)}) collective-permute-start(bf16[1,2,2,480,1280]{4,3,2,1,0:T(8,128)(2,1)} %dynamic-slice_bitcast_fusion), channel_id=1, source_target_pairs={{0,1},{1,0},{2,3},{3,2},{4,5},{5,4},{6,7},{7,6},{8,9},{9,8},{10,11... | collective-permute-start | bytes 14745608 | tf_op jit(solution)/shard_map/ppermute | solution.py:69
  804.1 39.3 %collective-permute-start.22 = (bf16[1,2,480,1280]{3,2,1,0:T(8,128)(2,1)}, bf16[1,2,480,1280]{3,2,1,0:T(8,128)(2,1)}, u32[]{:S(2)}, u32[]{:S(2)}) collective-permute-start(bf16[1,2,480,1280]{3,2,1,0:T(8,128)(2,1)} %pad_maximum_fusion.1), channel_id=1, source_target_pairs={{0,2},{1,5},{2,0},{3,7},{4,6},{5,1},{6,4},{7,3},{8,10},{9,13},{10,... | collective-permute-start | bytes 7372808 | tf_op jit(solution)/shard_map/ppermute | solution.py:130
  807.9 87.8 %collective-permute-start.32 = (bf16[1,768,320]{1,2,0:T(8,128)(2,1)}, bf16[1,768,320]{1,2,0:T(8,128)(2,1)}, u32[]{:S(2)}, u32[]{:S(2)}) collective-permute-start(bf16[1,768,320]{1,2,0:T(8,128)(2,1)} %slice.215), channel_id=1, source_target_pairs={{0,4},{4,0},{1,5},{5,1},{2,6},{6,2},{3,7},{7,3},{8,12},{12,8},{9,1... | collective-permute-start | bytes 1474568 | tf_op jit(solution)/shard_map/ppermute | solution.py:69
  832.1 63.5 %collective-permute-start.33 = (bf16[1,768,320]{1,2,0:T(8,128)(2,1)}, bf16[1,768,320]{1,2,0:T(8,128)(2,1)}, u32[]{:S(2)}, u32[]{:S(2)}) collective-permute-start(bf16[1,768,320]{1,2,0:T(8,128)(2,1)} %collective-permute-done.31), channel_id=1, source_target_pairs={{0,4},{4,0},{1,5},{5,1},{2,6},{6,2},{3,7},{7,3},{8,12},{12,8},{9,1... | collective-permute-start | bytes 1474568 | tf_op jit(solution)/shard_map/ppermute | solution.py:69
  833.9 65.4 %collective-permute-start.23 = (bf16[1,768,320]{1,2,0:T(8,128)(2,1)S(1)}, bf16[1,768,320]{1,2,0:T(8,128)(2,1)}, u32[]{:S(2)}, u32[]{:S(2)}) collective-permute-start(bf16[1,768,320]{1,2,0:T(8,128)(2,1)S(1)} %bitcast.247), channel_id=1, source_target_pairs={{0,4},{4,0},{1,5},{5,1},{2,6},{6,2},{3,7},{7,3},{8,12},{12,8},{9,1... | collective-permute-start | bytes 1474568 | tf_op jit(solution)/shard_map/ppermute | solution.py:69
  835.3 47.8 %collective-permute-start.21 = (bf16[1,768,320]{1,2,0:T(8,128)(2,1)S(1)}, bf16[1,768,320]{1,2,0:T(8,128)(2,1)}, u32[]{:S(2)}, u32[]{:S(2)}) collective-permute-start(bf16[1,768,320]{1,2,0:T(8,128)(2,1)S(1)} %bitcast.248), channel_id=1, source_target_pairs={{0,16},{16,0},{1,17},{17,1},{2,18},{18,2},{3,19},{19,3},{4,20},{20... | collective-permute-start | bytes 1474568 | tf_op jit(solution)/shard_map/ppermute | solution.py:69
  946.9 45.7 %collective-permute-start.40 = (bf16[1576,320]{0,1:T(8,128)(2,1)}, bf16[1576,320]{0,1:T(8,128)(2,1)}, u32[]{:S(2)}, u32[]{:S(2)}) collective-permute-start(bf16[1576,320]{0,1:T(8,128)(2,1)} %add_convert_fusion.2), channel_id=1, source_target_pairs={{0,8},{8,0},{1,9},{9,1},{2,10},{10,2},{3,11},{11,3},{4,12},{12,4},... | collective-permute-start | bytes 3025928 | tf_op jit(solution)/shard_map/ppermute | solution.py:69
  969.0 34.1 %collective-permute-start.39 = (bf16[120,1280]{1,0:T(8,128)(2,1)}, bf16[120,1280]{1,0:T(8,128)(2,1)}, u32[]{:S(2)}, u32[]{:S(2)}) collective-permute-start(bf16[120,1280]{1,0:T(8,128)(2,1)} %get-tuple-element.241), channel_id=1, source_target_pairs={{0,24},{8,0},{16,8},{24,16},{1,25},{9,1},{17,9},{25,17},{2,26},{10... | collective-permute-start | bytes 921608 | tf_op jit(solution)/shard_map/ppermute | solution.py:76
  969.1 34.1 %collective-permute-start.38 = (bf16[120,1280]{1,0:T(8,128)(2,1)}, bf16[120,1280]{1,0:T(8,128)(2,1)}, u32[]{:S(2)}, u32[]{:S(2)}) collective-permute-start(bf16[120,1280]{1,0:T(8,128)(2,1)} %get-tuple-element.242), channel_id=1, source_target_pairs={{0,16},{8,24},{16,0},{24,8},{1,17},{9,25},{17,1},{25,9},{2,18},{10... | collective-permute-start | bytes 921608 | tf_op jit(solution)/shard_map/ppermute | solution.py:76
  972.4 30.8 %collective-permute-start.37 = (bf16[120,1280]{1,0:T(8,128)(2,1)}, bf16[120,1280]{1,0:T(8,128)(2,1)}, u32[]{:S(2)}, u32[]{:S(2)}) collective-permute-start(bf16[120,1280]{1,0:T(8,128)(2,1)} %get-tuple-element.243), channel_id=1, source_target_pairs={{0,8},{8,16},{16,24},{24,0},{1,9},{9,17},{17,25},{25,1},{2,10},{10... | collective-permute-start | bytes 921608 | tf_op jit(solution)/shard_map/ppermute | solution.py:76
  (139 other events, 1937.4 us)
Sparse Core Ops, SparseCore 0:
  11.5 293.5 all-gather.1
  542.9 137.1 reduce-scatter.2
  687.6 232.3 reduce-scatter.4

commit v4 on v3

--- a/solution.py
+++ b/solution.py
@@ -132,11 +132,11 @@
 
 def by_owner(grads, planes):
     shape = (planes, lax.axis_size(ALL), -1, grads.shape[1])
-    return lax.optimization_barrier(grads.reshape(shape))
+    return lax.optimization_barrier(grads.reshape(shape).swapaxes(0, 1))
 
 
 def reduce_planes(grads):
-    return lax.psum_scatter(grads, OWNERS + PLANE, scatter_dimension=1, tiled=False)
+    return lax.psum_scatter(grads, OWNERS + PLANE, scatter_dimension=0, tiled=False)
 
 
 def as_is(tensor):
@@ -430,13 +430,71 @@
     return (weight - step_rate * (direction + WEIGHT_DECAY * weight), first_mom, second)
 
 
+def precise(left, right, dims):
+    return lax.dot_general(
+        left, right, (dims, ((), ())), precision=HIGHEST, preferred_element_type=jnp.float32
+    )
+
+
+def pair_basis(basis_ref):
+    size = basis_ref.shape[2]
+    blocks = range(basis_ref.shape[1])
+    nothing = jnp.zeros((size, size), jnp.float32)
+    rows = [
+        jnp.concatenate([basis_ref[0, at] if at == other else nothing for other in blocks], 1)
+        for at in blocks
+    ]
+    return jnp.concatenate(rows, 0)
+
+
+def turn_kernel(place_ref, grad_ref, basis_ref, turned_ref, outer_ref):
+    gradient = jnp.concatenate(
+        [grad_ref[(place_ref[0] + PLANES - piece) % PLANES] for piece in range(PLANES)], 0
+    ).astype(jnp.float32)
+    turned_ref[...] = precise(gradient, pair_basis(basis_ref), ((1,), (0,)))
+    outer = precise(gradient, gradient, ((0,), (0,)))
+    size = basis_ref.shape[2]
+    for at in range(basis_ref.shape[1]):
+        part = slice(at * size, (at + 1) * size)
+        outer_ref[at] = outer[part, part]
+
+
+def turned_gradient(gradient, basis):
+    blocks, block_len = basis.shape[1], basis.shape[2]
+    quarter = gradient.shape[1]
+    rows = PLANES * quarter
+    return pl.pallas_call(
+        turn_kernel,
+        grid=(blocks // 2,),
+        in_specs=[
+            pl.BlockSpec(memory_space=pltpu.SMEM),
+            pl.BlockSpec((PLANES, quarter, 2 * block_len), lambda b: (0, 0, b)),
+            pl.BlockSpec((1, 2, block_len, block_len), lambda b: (0, b, 0, 0)),
+        ],
+        out_specs=[
+            pl.BlockSpec((rows, 2 * block_len), lambda b: (0, b)),
+            pl.BlockSpec((2, block_len, block_len), lambda b: (b, 0, 0)),
+        ],
+        out_shape=[
+            jax.ShapeDtypeStruct((rows, blocks * block_len), jnp.float32),
+            jax.ShapeDtypeStruct((blocks, block_len, block_len), jnp.float32),
+        ],
+        compiler_params=pltpu.CompilerParams(vmem_limit_bytes=40 << 20),
+        cost_estimate=pl.CostEstimate(
+            flops=8 * rows * blocks * block_len * block_len,
+            bytes_accessed=8 * rows * blocks * block_len,
+            transcendentals=0,
+        ),
+    )(lax.axis_index(PLANE).reshape(1), gradient, basis)
+
+
 def rotated_kernel(
-    place_ref,
     factor_ref,
     weight_ref,
     first_ref,
     second_ref,
-    grad_ref,
+    turned_ref,
+    outer_ref,
     stat_ref,
     basis_ref,
     weight_out,
@@ -446,56 +504,44 @@
     gram_ref,
     span_ref,
 ):
-    def product(left, right, dims):
-        return lax.dot_general(
-            left, right, (dims, ((), ())), precision=HIGHEST, preferred_element_type=jnp.float32
-        )
-
-    basis = basis_ref[0, 0]
-    gradient = jnp.concatenate(
-        [grad_ref[(place_ref[0] + PLANES - piece) % PLANES] for piece in range(PLANES)], 0
-    )
-    gradient = gradient.astype(jnp.float32) * factor_ref[0, 0]
-    turned = product(gradient, basis, ((1,), (0,)))
+    factor = factor_ref[0, 0]
+    turned = turned_ref[...] * factor
     first_mom = BETA_ONE * first_ref[...] + (1.0 - BETA_ONE) * turned
     second = BETA_TWO * second_ref[...] + (1.0 - BETA_TWO) * turned * turned
     direction = (
         first_mom / (1.0 - BETA_ONE**STEP) / (jnp.sqrt(second / (1.0 - BETA_TWO**STEP)) + ADAM_EPS)
     )
-    back = product(direction, basis, ((1,), (1,)))
+    back = precise(direction, pair_basis(basis_ref), ((1,), (1,)))
     weight = weight_ref[...]
     weight_out[...] = weight - RATE_LAYER * (back + WEIGHT_DECAY * weight)
     first_out[...] = first_mom
     second_out[...] = second
-    stat_next = BETA_STAT * stat_ref[0, 0] + (1.0 - BETA_STAT) * product(
-        gradient, gradient, ((0,), (0,))
-    )
-    stat_out[0, 0] = stat_next
-    spanned = product(stat_next, basis, ((1,), (0,)))
-    turned_span = spanned.T
-    span_ref[0] = turned_span
-    gram_ref[0] = product(turned_span, spanned, ((1,), (0,)))
-
-
-def rotated_update(weight, first_mom, second, gradient, factor, stat, basis):
+    for at in range(basis_ref.shape[1]):
+        clipped = outer_ref[at] * factor * factor
+        stat_next = BETA_STAT * stat_ref[0, at] + (1.0 - BETA_STAT) * clipped
+        stat_out[0, at] = stat_next
+        spanned = precise(stat_next, basis_ref[0, at], ((1,), (0,)))
+        turned_span = spanned.T
+        span_ref[at] = turned_span
+        gram_ref[at] = precise(turned_span, spanned, ((1,), (0,)))
+
+
+def rotated_update(weight, first_mom, second, turned, outer, factor, stat, basis):
     blocks, block_len = basis.shape[1], basis.shape[2]
     rows = weight.shape[0]
-    column = pl.BlockSpec((rows, block_len), lambda b: (0, b))
-    square = pl.BlockSpec((1, 1, block_len, block_len), lambda b: (0, b, 0, 0))
-    flat = pl.BlockSpec((1, block_len, block_len), lambda b: (b, 0, 0))
+    column = pl.BlockSpec((rows, 2 * block_len), lambda b: (0, b))
+    square = pl.BlockSpec((1, 2, block_len, block_len), lambda b: (0, b, 0, 0))
+    flat = pl.BlockSpec((2, block_len, block_len), lambda b: (b, 0, 0))
     wide = jax.ShapeDtypeStruct(weight.shape, jnp.float32)
     small = jax.ShapeDtypeStruct((blocks, block_len, block_len), jnp.float32)
     weight_next, first_next, second_next, stat_next, gram, span = pl.pallas_call(
         rotated_kernel,
-        grid=(blocks,),
-        in_specs=[pl.BlockSpec(memory_space=pltpu.SMEM)] * 2
-        + [column] * 3
-        + [pl.BlockSpec((PLANES, rows // PLANES, block_len), lambda b: (0, 0, b))]
-        + [square] * 2,
+        grid=(blocks // 2,),
+        in_specs=[pl.BlockSpec(memory_space=pltpu.SMEM)] + [column] * 4 + [flat] + [square] * 2,
         out_specs=[column] * 3 + [square] + [flat] * 2,
         out_shape=[wide] * 3 + [jax.ShapeDtypeStruct(stat.shape, jnp.float32)] + [small] * 2,
         compiler_params=pltpu.CompilerParams(vmem_limit_bytes=40 << 20),
-    )(lax.axis_index(PLANE).reshape(1), factor.reshape(1, 1), weight, first_mom, second, gradient, stat, basis)
+    )(factor.reshape(1, 1), weight, first_mom, second, turned, outer, stat, basis)
     solved = frame(gram, span)
     return (weight_next, first_next, second_next, jnp.swapaxes(solved, 1, 2)[None], stat_next)
 
@@ -783,6 +829,7 @@
     table_grad = added(spread["mine"], swap(spread["theirs"].astype(jnp.bfloat16), "zb"))
     quarters = jnp.concatenate([piece_zero[None], pieces_between, piece_three], 0)
     layer_grad = jnp.stack(sent_z([pick(quarters, plane) for plane in planes_from_here()]))
+    turned, outer = turned_gradient(layer_grad, rot_basis)
     squares = total_at_once(
         jnp.sum(jnp.square(layer_grad.astype(jnp.float32))) + jnp.sum(table_grad * table_grad)
     )
@@ -791,7 +838,7 @@
     factor = 1.0 / jnp.maximum(gradient_norm, 1.0)
     out_bias_grad = factor * small_grad[2 * model_dim : 3 * model_dim]
     layer_next, layer_first_next, layer_second_next, basis_next, stat_next = rotated_update(
-        layer_weight, layer_first, layer_second, layer_grad, factor, stat_matrix, rot_basis
+        layer_weight, layer_first, layer_second, turned, outer, factor, stat_matrix, rot_basis
     )
     small_next, small_first_next, small_second_next = adam_update(
         small_params, small_first, small_second, factor * small_grad, RATE_SMALL

time: 1100 us -> 1090 us (level)
    unnamed x231 -> x237, local copies, waits for them, and re-layouts: 45.5 us -> 43.7 us
where the time goes in v4:
time: 1090 us; the launch traced here: 1080 us
  waiting for transfers between devices  505 us (46%)
  matrix products  179 us (16%)
  local copies, waits for them, and re-layouts  113 us (10%)
  other arithmetic  92.5 us (8%)
  Pallas kernels  88.4 us (8%)
  starting transfers between devices  68.6 us (6%)
  between operations  33.3 us (3%)
    ppermute x33, waiting for transfers between devices, swap(): return lax.ppermute(tensor, axis, [(0, 1), (1, 0)])  301 us
    dot_general x14, matrix products, plain_dot(): return jnp.dot(left, right, preferred_element_type=jnp.float32)  88.7 us
    all_gather x1, waiting for transfers between devices, body(): gathered = lax.all_gather(weight_low, ALL, axis=0, tiled=True)  49.7 us
    dot_general x9, matrix products, outer_dot(): lax.dot_general(left, right, (((0,), (0,)), ((), ())), preferred_element_...  44.7 us
    unnamed x237, local copies, waits for them, and re-layouts  43.7 us
    dot_general x4, matrix products, low_dot(): lax.dot_general(left, right, LANES_BOTH, preferred_element_type=jnp.float32)  43.6 us
    all_to_all x1, waiting for transfers between devices, body(): lax.all_to_all(joined, SEQ, split_axis=0, concat_axis=0, tiled=True)  34.4 us
    all_to_all x1, waiting for transfers between devices, body(): lax.all_to_all(grad_joined, SEQ, split_axis=0, concat_axis=0, tiled=True)  33.5 us
  transfers between devices with their start and end apart: 50, of which 28 were waited for; matrix products, arithmetic and copies ran while one was open for 24% of the time, Pallas kernels for 3%

profile of v4, /device:TPU:0, one launch (start us, length us, event | category | flops | bytes accessed | tf_op | source)
XLA Modules:
  0.0 1080.4 jit_solution(10224761749388919785)
XLA Ops:
  13.5 47.8 %collective-permute-done = bf16[1576,320]{0,1:T(8,128)(2,1)} collective-permute-done((bf16[1576,320]{0,1:T(8,128)(2,1)S(1)}, bf16[1576,320]{0,1:T(8,128)(2,1)}, u32[]{:S(2)}, u32[]{:S(2)}) %collective-permute-start) | collective-permute-done | bytes 1008672 | tf_op jit(solution)/shard_map/ppermute | solution.py:69
  85.3 37.0 %collective-permute-done.2 = bf16[2,1,384,640]{3,2,1,0:T(8,128)(2,1)S(1)} collective-permute-done((bf16[2,1,384,640]{3,2,1,0:T(8,128)(2,1)S(1)}, bf16[2,1,384,640]{3,2,1,0:T(8,128)(2,1)S(1)}, u32[]{:S(2)}, u32[]{:S(2)}) %collective-permute-start.2) | collective-permute-done | bytes 983072 | tf_op jit(solution)/shard_map/ppermute | solution.py:69
  123.1 12.8 %collective-permute-done.5 = bf16[1576,320]{0,1:T(8,128)(2,1)S(1)} collective-permute-done((bf16[1576,320]{0,1:T(8,128)(2,1)}, bf16[1576,320]{0,1:T(8,128)(2,1)S(1)}, u32[]{:S(2)}, u32[]{:S(2)}) %collective-permute-start.5) | collective-permute-done | bytes 1008672 | tf_op jit(solution)/shard_map/ppermute | solution.py:69
  156.8 32.0 %collective-permute-done.7 = bf16[2,1,384,640]{3,2,1,0:T(8,128)(2,1)S(1)} collective-permute-done((bf16[2,1,384,640]{3,2,1,0:T(8,128)(2,1)S(1)}, bf16[2,1,384,640]{3,2,1,0:T(8,128)(2,1)S(1)}, u32[]{:S(2)}, u32[]{:S(2)}) %collective-permute-start.7) | collective-permute-done | bytes 983072 | tf_op jit(solution)/shard_map/ppermute | solution.py:69
  192.7 25.8 %collective-permute-done.3 = bf16[384,640]{1,0:T(8,128)(2,1)S(1)} collective-permute-done((bf16[384,640]{1,0:T(8,128)(2,1)S(1)}, bf16[384,640]{1,0:T(8,128)(2,1)S(1)}, u32[]{:S(2)}, u32[]{:S(2)}) %collective-permute-start.3) | collective-permute-done | bytes 491552 | tf_op jit(solution)/shard_map/ppermute | solution.py:69
  218.5 33.3 %collective-permute-done.8 = bf16[384,640]{1,0:T(8,128)(2,1)} collective-permute-done((bf16[384,640]{1,0:T(8,128)(2,1)S(1)}, bf16[384,640]{1,0:T(8,128)(2,1)}, u32[]{:S(2)}, u32[]{:S(2)}) %collective-permute-start.8) | collective-permute-done | bytes 491552 | tf_op jit(solution)/shard_map/ppermute | solution.py:69
  255.4 49.7 %all-gather.2.cloned.1.call-done.weight_ref = bf16[15360,1280]{1,0:T(8,128)(2,1)} async-done(((bf16[480,1280]{1,0:T(8,128)(2,1)}), bf16[15360,1280]{1,0:T(8,128)(2,1)}) %all-gather.2.cloned.1.call-update) | async-done | bytes 39321616 | tf_op jit(solution)/shard_map/all_gather | solution.py:597
  324.8 34.4 %all-to-all-done = bf16[4,3,384,320]{2,3,1,0:T(8,128)(2,1)} async-done(((bf16[4,3,384,320]{2,3,1,0:T(8,128)(2,1)}), bf16[4,3,384,320]{2,3,1,0:T(8,128)(2,1)}, u32[]{:S(2)}, u32[]{:S(2)}) %all-to-all-start) | async-done | bytes 2949152 | tf_op jit(solution)/shard_map/all_to_all | solution.py:650
  363.6 15.6 %shard_map.272 = (bf16[4,384,320]{2,1,0:T(8,128)(2,1)S(1)}, f32[4,384,320]{2,1,0:T(8,128)S(1)}, f32[8,1536]{1,0:T(8,128)S(1)}) custom-call(s32[1,1536]{1,0:T(1,128)S(1)} %broadcast_in_dim.68.start_ref, bf16[4,3,384,320]{3,2,1,0:T(8,128)(2,1)S(1)} %copy.118.q_ref.k_ref.v_ref, bf16[4,3,384,320]{3,2,1,0:T(8,128)(2,1)S(1)} %copy.118.q_ref.k_ref.v_ref, ...), custom_call_target="tpu_custom_call" | custom-call | tf_op jit(solution)/shard_map/pallas_call | solution.py:276
  390.8 11.8 %all-to-all-done.1 = bf16[4,384,320]{1,2,0:T(8,128)(2,1)} async-done(((bf16[4,384,320]{1,2,0:T(8,128)(2,1)}), bf16[4,384,320]{1,2,0:T(8,128)(2,1)}, u32[]{:S(2)}, u32[]{:S(2)}) %all-to-all-start.1) | async-done | bytes 983072 | tf_op jit(solution)/shard_map/all_to_all | solution.py:652
  408.3 11.9 %multiply_convert_fusion = (bf16[384,5120]{1,0:T(8,128)(2,1)S(1)}, f32[384,5120]{1,0:T(8,128)}) fusion(f32[5120]{0:T(1024)S(1)} %copy-done.81, bf16[15360,1280]{1,0:T(8,128)(2,1)} %all-gather.2.cloned.1.call-done.weight_ref, f32[384,1280]{1,0:T(8,128)S(1)} %get-tuple-element.283, f32[1280]{0:T(1024)S(1)} %copy-done.105, f32[1280]{0:T(1024)S(1)} %copy-done.77, ...), kind=kOutput, calls=%fused_computation.43 | convolution fusion | flops 5055283200 | bytes 26903552 | tf_op jit(solution)/shard_map/dot_general | solution.py:46
  420.3 11.0 %fusion.125 = (f32[384]{0:T(512)S(1)}, f32[384,1280]{1,0:T(8,128)S(1)}) fusion(f32[1280]{0:T(1024)S(1)} %copy-done.108, f32[384,1280]{1,0:T(8,128)S(1)} %get-tuple-element.283, bf16[384,5120]{1,0:T(8,128)(2,1)S(1)} %get-tuple-element.284, bf16[15360,1280]{1,0:T(8,128)(2,1)} %all-gather.2.cloned.1.call-done.weight_ref), kind=kOutput, calls=%fused_computation.271 | convolution fusion | flops 5034638848 | bytes 20978176 | tf_op jit(solution)/shard_map/dot_general | solution.py:50
  484.6 12.0 %convolution_convert_fusion.4 = bf16[256,1280]{1,0:T(8,128)(2,1)S(1)} fusion(bf16[256,3152]{0,1:T(8,128)(2,1)S(1)} %multiply_convert_fusion.1, bf16[3152,640]{0,1:T(8,128)(2,1)} %copy-done.51, bf16[3152,640]{0,1:T(8,128)(2,1)S(1)} %copy-done.50, pred[]{:T(512)S(6)} %eq.71), kind=kOutput, calls=%fused_computation.80 | convolution fusion | flops 2102333440 | bytes 10338305 | tf_op jit(solution)/shard_map/dot_general | solution.py:50
  544.7 17.3 %convert_reduce_fusion = (f32[5120]{0:T(1024)}, bf16[384,5120]{1,0:T(8,128)(2,1)S(1)}) fusion(f32[384,5120]{1,0:T(8,128)} %get-tuple-element.285, bf16[384,1280]{1,0:T(8,128)(2,1)} %copy-done.56, bf16[15360,1280]{1,0:T(8,128)(2,1)} %all-gather.2.cloned.1.call-done.weight_ref), kind=kOutput, calls=%fused_computation.42 | convolution fusion | flops 5076413440 | bytes 25907200 | tf_op jit(solution)/shard_map/dot_general | solution.py:46
  567.8 16.2 %collective-permute-done.19 = bf16[3152,320]{0,1:T(8,128)(2,1)S(1)} collective-permute-done((bf16[3152,320]{0,1:T(8,128)(2,1)}, bf16[3152,320]{0,1:T(8,128)(2,1)S(1)}, u32[]{:S(2)}, u32[]{:S(2)}) %collective-permute-start.19) | collective-permute-done | bytes 2017312 | tf_op jit(solution)/shard_map/ppermute | solution.py:69
  644.0 18.1 %all-to-all-done.2 = bf16[4,384,320]{1,2,0:T(8,128)(2,1)} async-done(((bf16[4,384,320]{1,2,0:T(8,128)(2,1)}), bf16[4,384,320]{1,2,0:T(8,128)(2,1)}, u32[]{:S(2)}, u32[]{:S(2)}) %all-to-all-start.2) | async-done | bytes 983072 | tf_op jit(solution)/shard_map/all_to_all | solution.py:755
  668.1 31.4 %shard_map.273 = bf16[4,3,384,320]{3,2,1,0:T(8,128)(2,1)S(1)} custom-call(s32[1,1536]{1,0:T(1,128)S(1)} %broadcast_in_dim.68.start_ref, bf16[4,3,384,320]{3,2,1,0:T(8,128)(2,1)S(1)} %copy.118.q_ref.k_ref.v_ref, bf16[4,3,384,320]{3,2,1,0:T(8,128)(2,1)S(1)} %copy.118.q_ref.k_ref.v_ref, bf16[4,3,384,320]{3,2,1,0:T(8,128)(2,1)S(1)} %copy.118.q_ref.k_ref.v_ref, ...), custom_call_target="tpu_custom_call" | custom-call | tf_op jit(solution)/shard_map/pallas_call | solution.py:347
  712.9 33.5 %all-to-all-done.3 = bf16[4,3,384,320]{2,3,1,0:T(8,128)(2,1)S(1)} async-done(((bf16[4,3,384,320]{2,3,1,0:T(8,128)(2,1)}), bf16[4,3,384,320]{2,3,1,0:T(8,128)(2,1)S(1)}, u32[]{:S(2)}, u32[]{:S(2)}) %all-to-all-start.3) | async-done | bytes 2949152 | tf_op jit(solution)/shard_map/all_to_all | solution.py:779
  774.3 22.3 %all-to-all-done.4 = bf16[384,4,320]{0,2,1:T(8,128)(2,1)S(1)} async-done(((bf16[384,4,320]{0,2,1:T(8,128)(2,1)}), bf16[384,4,320]{0,2,1:T(8,128)(2,1)S(1)}, u32[]{:S(2)}, u32[]{:S(2)}) %all-to-all-start.4) | async-done | bytes 983072 | tf_op jit(solution)/shard_map/all_to_all | solution.py:788
  814.6 21.4 %collective-permute-done.31 = bf16[1,768,320]{1,2,0:T(8,128)(2,1)} collective-permute-done((bf16[1,768,320]{1,2,0:T(8,128)(2,1)}, bf16[1,768,320]{1,2,0:T(8,128)(2,1)}, u32[]{:S(2)}, u32[]{:S(2)}) %collective-permute-start.31) | collective-permute-done | bytes 491552 | tf_op jit(solution)/shard_map/ppermute | solution.py:69
  854.2 32.0 %collective-permute-done.21 = bf16[1,768,320]{1,2,0:T(8,128)(2,1)} collective-permute-done((bf16[1,768,320]{1,2,0:T(8,128)(2,1)S(1)}, bf16[1,768,320]{1,2,0:T(8,128)(2,1)}, u32[]{:S(2)}, u32[]{:S(2)}) %collective-permute-start.21) | collective-permute-done | bytes 491552 | tf_op jit(solution)/shard_map/ppermute | solution.py:69
  952.7 15.4 %collective-permute-done.35 = bf16[120,1280]{1,0:T(8,128)(2,1)S(1)} collective-permute-done((bf16[120,1280]{1,0:T(8,128)(2,1)S(1)}, bf16[120,1280]{1,0:T(8,128)(2,1)S(1)}, u32[]{:S(2)}, u32[]{:S(2)}) %collective-permute-start.35) | collective-permute-done | bytes 307232 | tf_op jit(solution)/shard_map/ppermute | solution.py:76
  977.1 17.3 %collective-permute-done.40 = bf16[1576,320]{0,1:T(8,128)(2,1)} collective-permute-done((bf16[1576,320]{0,1:T(8,128)(2,1)}, bf16[1576,320]{0,1:T(8,128)(2,1)}, u32[]{:S(2)}, u32[]{:S(2)}) %collective-permute-start.40) | collective-permute-done | bytes 1008672 | tf_op jit(solution)/shard_map/ppermute | solution.py:69
  1044.7 18.1 %shard_map.276 = f32[10,128,128]{2,1,0:T(8,128)S(1)} custom-call(f32[10,128,128]{2,1,0:T(8,128)S(1)} %get-tuple-element.98.gram_ref, f32[10,128,128]{2,1,0:T(8,128)S(1)} %get-tuple-element.99.span_ref), custom_call_target="tpu_custom_call" | custom-call | tf_op jit(solution)/shard_map/pallas_call | solution.py:416
  (498 shorter events, 469.0 us)
Async XLA Ops:
  7.2 297.9 %all-gather.2.cloned.1.call-start = ((), (), s32[]{:S(2)}) async-start(), calls=%async_computation.8 | async-start | bytes 40550400 | tf_op jit(solution)/shard_map/all_gather | solution.py:597
  10.4 50.9 %collective-permute-start = (bf16[1576,320]{0,1:T(8,128)(2,1)S(1)}, bf16[1576,320]{0,1:T(8,128)(2,1)}, u32[]{:S(2)}, u32[]{:S(2)}) collective-permute-start(bf16[1576,320]{0,1:T(8,128)(2,1)S(1)} %convert_element_type.331), channel_id=1, source_target_pairs={{0,8},{8,0},{1,9},{9,1},{2,10},{10,2},{3,11},{11,3},{4,12},{12,4},... | collective-permute-start | bytes 3025928 | tf_op jit(solution)/shard_map/ppermute | solution.py:69
  76.6 45.7 %collective-permute-start.2 = (bf16[2,1,384,640]{3,2,1,0:T(8,128)(2,1)S(1)}, bf16[2,1,384,640]{3,2,1,0:T(8,128)(2,1)S(1)}, u32[]{:S(2)}, u32[]{:S(2)}) collective-permute-start(bf16[2,1,384,640]{3,2,1,0:T(8,128)(2,1)S(1)} %bitcast.280), channel_id=1, source_target_pairs={{0,4},{4,0},{1,5},{5,1},{2,6},{6,2},{3,7},{7,3},{8,12},{12,8},{9,1... | collective-permute-start | bytes 2949128 | tf_op jit(solution)/shard_map/ppermute | solution.py:69
  78.8 57.1 %collective-permute-start.4 = (bf16[1576,320]{0,1:T(8,128)(2,1)S(1)}, bf16[1576,320]{0,1:T(8,128)(2,1)S(1)}, u32[]{:S(2)}, u32[]{:S(2)}) collective-permute-start(bf16[1576,320]{0,1:T(8,128)(2,1)S(1)} %convert_element_type.331), channel_id=1, source_target_pairs={{0,2},{2,0},{1,3},{3,1},{4,6},{6,4},{5,7},{7,5},{8,10},{10,8},{9,1... | collective-permute-start | bytes 3025928 | tf_op jit(solution)/shard_map/ppermute | solution.py:69
  80.4 55.6 %collective-permute-start.5 = (bf16[1576,320]{0,1:T(8,128)(2,1)}, bf16[1576,320]{0,1:T(8,128)(2,1)S(1)}, u32[]{:S(2)}, u32[]{:S(2)}) collective-permute-start(bf16[1576,320]{0,1:T(8,128)(2,1)} %collective-permute-done), channel_id=1, source_target_pairs={{0,2},{2,0},{1,3},{3,1},{4,6},{6,4},{5,7},{7,5},{8,10},{10,8},{9,1... | collective-permute-start | bytes 3025928 | tf_op jit(solution)/shard_map/ppermute | solution.py:69
  148.2 40.5 %collective-permute-start.7 = (bf16[2,1,384,640]{3,2,1,0:T(8,128)(2,1)S(1)}, bf16[2,1,384,640]{3,2,1,0:T(8,128)(2,1)S(1)}, u32[]{:S(2)}, u32[]{:S(2)}) collective-permute-start(bf16[2,1,384,640]{3,2,1,0:T(8,128)(2,1)S(1)} %bitcast.281), channel_id=1, source_target_pairs={{0,4},{4,0},{1,5},{5,1},{2,6},{6,2},{3,7},{7,3},{8,12},{12,8},{9,1... | collective-permute-start | bytes 2949128 | tf_op jit(solution)/shard_map/ppermute | solution.py:69
  149.8 68.6 %collective-permute-start.3 = (bf16[384,640]{1,0:T(8,128)(2,1)S(1)}, bf16[384,640]{1,0:T(8,128)(2,1)S(1)}, u32[]{:S(2)}, u32[]{:S(2)}) collective-permute-start(bf16[384,640]{1,0:T(8,128)(2,1)S(1)} %slice_bitcast_fusion.3), channel_id=1, source_target_pairs={{0,16},{16,0},{1,17},{17,1},{2,18},{18,2},{3,19},{19,3},{4,20},{20... | collective-permute-start | bytes 1474568 | tf_op jit(solution)/shard_map/ppermute | solution.py:69
  189.1 62.8 %collective-permute-start.8 = (bf16[384,640]{1,0:T(8,128)(2,1)S(1)}, bf16[384,640]{1,0:T(8,128)(2,1)}, u32[]{:S(2)}, u32[]{:S(2)}) collective-permute-start(bf16[384,640]{1,0:T(8,128)(2,1)S(1)} %slice_bitcast_fusion.1), channel_id=1, source_target_pairs={{0,16},{16,0},{1,17},{17,1},{2,18},{18,2},{3,19},{19,3},{4,20},{20... | collective-permute-start | bytes 1474568 | tf_op jit(solution)/shard_map/ppermute | solution.py:69
  319.4 39.8 %all-to-all-start = ((bf16[4,3,384,320]{2,3,1,0:T(8,128)(2,1)}), bf16[4,3,384,320]{2,3,1,0:T(8,128)(2,1)}, u32[]{:S(2)}, u32[]{:S(2)}) async-start(bf16[4,3,384,320]{2,3,1,0:T(8,128)(2,1)} %copy.109), calls=%async_computation | async-start | bytes 5898240 | tf_op jit(solution)/shard_map/all_to_all | solution.py:650
  388.8 322.8 %reduce-scatter.3.cloned.1.call-start = ((), (), s32[]{:S(2)}) async-start(), calls=%async_computation.9 | async-start | bytes 10137600 | tf_op jit(solution)/shard_map/reduce_scatter | solution.py:139
  475.4 28.7 %collective-permute-start.17 = (s32[2,2,1,384,1]{3,4,1,0,2:T(1,128)}, s32[2,2,1,384,1]{3,4,1,0,2:T(1,128)}, u32[]{:S(2)}, u32[]{:S(2)}) collective-permute-start(s32[2,2,1,384,1]{3,4,1,0,2:T(1,128)} %pad_add_fusion), channel_id=1, source_target_pairs={{0,1},{1,0},{2,3},{3,2},{4,5},{5,4},{6,7},{7,6},{8,9},{9,8},{10,11... | collective-permute-start | bytes 18440 | tf_op jit(solution)/shard_map/ppermute | solution.py:69
  542.7 426.8 %reduce-scatter.5.cloned.1.call-start = ((), (), s32[]{:S(2)}) async-start(), calls=%async_computation.10 | async-start | bytes 20275200 | tf_op jit(solution)/shard_map/reduce_scatter | solution.py:139
  542.8 41.3 %collective-permute-start.19 = (bf16[3152,320]{0,1:T(8,128)(2,1)}, bf16[3152,320]{0,1:T(8,128)(2,1)S(1)}, u32[]{:S(2)}, u32[]{:S(2)}) collective-permute-start(bf16[3152,320]{0,1:T(8,128)(2,1)} %copy-done.55), channel_id=1, source_target_pairs={{0,2},{2,0},{1,3},{3,1},{4,6},{6,4},{5,7},{7,5},{8,10},{10,8},{9,1... | collective-permute-start | bytes 6051848 | tf_op jit(solution)/shard_map/ppermute | solution.py:69
  707.4 39.0 %all-to-all-start.3 = ((bf16[4,3,384,320]{2,3,1,0:T(8,128)(2,1)}), bf16[4,3,384,320]{2,3,1,0:T(8,128)(2,1)S(1)}, u32[]{:S(2)}, u32[]{:S(2)}) async-start(bf16[4,3,384,320]{2,3,1,0:T(8,128)(2,1)} %copy.122), calls=%async_computation.3 | async-start | bytes 5898240 | tf_op jit(solution)/shard_map/all_to_all | solution.py:779
  758.6 40.0 %collective-permute-start.20 = (bf16[1,2,2,480,1280]{4,3,2,1,0:T(8,128)(2,1)}, bf16[1,2,2,480,1280]{4,3,2,1,0:T(8,128)(2,1)}, u32[]{:S(2)}, u32[]{:S(2)}) collective-permute-start(bf16[1,2,2,480,1280]{4,3,2,1,0:T(8,128)(2,1)} %dynamic-slice_bitcast_fusion), channel_id=1, source_target_pairs={{0,1},{1,0},{2,3},{3,2},{4,5},{5,4},{6,7},{7,6},{8,9},{9,8},{10,11... | collective-permute-start | bytes 14745608 | tf_op jit(solution)/shard_map/ppermute | solution.py:69
  808.5 41.3 %collective-permute-start.22 = (bf16[1,2,480,1280]{3,2,1,0:T(8,128)(2,1)}, bf16[1,2,480,1280]{3,2,1,0:T(8,128)(2,1)}, u32[]{:S(2)}, u32[]{:S(2)}) collective-permute-start(bf16[1,2,480,1280]{3,2,1,0:T(8,128)(2,1)} %pad_maximum_fusion.1), channel_id=1, source_target_pairs={{0,2},{1,5},{2,0},{3,7},{4,6},{5,1},{6,4},{7,3},{8,10},{9,13},{10,... | collective-permute-start | bytes 7372808 | tf_op jit(solution)/shard_map/ppermute | solution.py:130
  812.9 85.5 %collective-permute-start.32 = (bf16[1,768,320]{1,2,0:T(8,128)(2,1)}, bf16[1,768,320]{1,2,0:T(8,128)(2,1)}, u32[]{:S(2)}, u32[]{:S(2)}) collective-permute-start(bf16[1,768,320]{1,2,0:T(8,128)(2,1)} %slice.215), channel_id=1, source_target_pairs={{0,4},{4,0},{1,5},{5,1},{2,6},{6,2},{3,7},{7,3},{8,12},{12,8},{9,1... | collective-permute-start | bytes 1474568 | tf_op jit(solution)/shard_map/ppermute | solution.py:69
  835.9 62.5 %collective-permute-start.33 = (bf16[1,768,320]{1,2,0:T(8,128)(2,1)}, bf16[1,768,320]{1,2,0:T(8,128)(2,1)}, u32[]{:S(2)}, u32[]{:S(2)}) collective-permute-start(bf16[1,768,320]{1,2,0:T(8,128)(2,1)} %collective-permute-done.31), channel_id=1, source_target_pairs={{0,4},{4,0},{1,5},{5,1},{2,6},{6,2},{3,7},{7,3},{8,12},{12,8},{9,1... | collective-permute-start | bytes 1474568 | tf_op jit(solution)/shard_map/ppermute | solution.py:69
  837.9 64.2 %collective-permute-start.23 = (bf16[1,768,320]{1,2,0:T(8,128)(2,1)S(1)}, bf16[1,768,320]{1,2,0:T(8,128)(2,1)}, u32[]{:S(2)}, u32[]{:S(2)}) collective-permute-start(bf16[1,768,320]{1,2,0:T(8,128)(2,1)S(1)} %bitcast.251), channel_id=1, source_target_pairs={{0,4},{4,0},{1,5},{5,1},{2,6},{6,2},{3,7},{7,3},{8,12},{12,8},{9,1... | collective-permute-start | bytes 1474568 | tf_op jit(solution)/shard_map/ppermute | solution.py:69
  839.2 47.0 %collective-permute-start.21 = (bf16[1,768,320]{1,2,0:T(8,128)(2,1)S(1)}, bf16[1,768,320]{1,2,0:T(8,128)(2,1)}, u32[]{:S(2)}, u32[]{:S(2)}) collective-permute-start(bf16[1,768,320]{1,2,0:T(8,128)(2,1)S(1)} %bitcast.252), channel_id=1, source_target_pairs={{0,16},{16,0},{1,17},{17,1},{2,18},{18,2},{3,19},{19,3},{4,20},{20... | collective-permute-start | bytes 1474568 | tf_op jit(solution)/shard_map/ppermute | solution.py:69
  949.6 44.7 %collective-permute-start.40 = (bf16[1576,320]{0,1:T(8,128)(2,1)}, bf16[1576,320]{0,1:T(8,128)(2,1)}, u32[]{:S(2)}, u32[]{:S(2)}) collective-permute-start(bf16[1576,320]{0,1:T(8,128)(2,1)} %add_convert_fusion.2), channel_id=1, source_target_pairs={{0,8},{8,0},{1,9},{9,1},{2,10},{10,2},{3,11},{11,3},{4,12},{12,4},... | collective-permute-start | bytes 3025928 | tf_op jit(solution)/shard_map/ppermute | solution.py:69
  971.9 34.1 %collective-permute-start.39 = (bf16[120,1280]{1,0:T(8,128)(2,1)}, bf16[120,1280]{1,0:T(8,128)(2,1)}, u32[]{:S(2)}, u32[]{:S(2)}) collective-permute-start(bf16[120,1280]{1,0:T(8,128)(2,1)} %get-tuple-element.245), channel_id=1, source_target_pairs={{0,24},{8,0},{16,8},{24,16},{1,25},{9,1},{17,9},{25,17},{2,26},{10... | collective-permute-start | bytes 921608 | tf_op jit(solution)/shard_map/ppermute | solution.py:76
  971.9 34.1 %collective-permute-start.38 = (bf16[120,1280]{1,0:T(8,128)(2,1)}, bf16[120,1280]{1,0:T(8,128)(2,1)}, u32[]{:S(2)}, u32[]{:S(2)}) collective-permute-start(bf16[120,1280]{1,0:T(8,128)(2,1)} %get-tuple-element.246), channel_id=1, source_target_pairs={{0,16},{8,24},{16,0},{24,8},{1,17},{9,25},{17,1},{25,9},{2,18},{10... | collective-permute-start | bytes 921608 | tf_op jit(solution)/shard_map/ppermute | solution.py:76
  975.0 30.9 %collective-permute-start.37 = (bf16[120,1280]{1,0:T(8,128)(2,1)S(1)}, bf16[120,1280]{1,0:T(8,128)(2,1)}, u32[]{:S(2)}, u32[]{:S(2)}) collective-permute-start(bf16[120,1280]{1,0:T(8,128)(2,1)S(1)} %get-tuple-element.247), channel_id=1, source_target_pairs={{0,8},{8,16},{16,24},{24,0},{1,9},{9,17},{17,25},{25,1},{2,10},{10... | collective-permute-start | bytes 921608 | tf_op jit(solution)/shard_map/ppermute | solution.py:76
  (142 other events, 1919.8 us)
Sparse Core Ops, SparseCore 0:
  11.5 293.5 all-gather.1
  542.8 142.1 reduce-scatter.2
  692.6 230.8 reduce-scatter.4
